TPU v7x, 32 devices: a whole 2x2x4 slice. The times are simulated.
32 devices in a mesh: sub: 16 (over z, y, core), slab: 2 (over x).
Axes of the slice: x: 2, y: 2, z: 4, core: 2. Of those that a mesh axis runs over, the one named last changes fastest.
Arguments:
- source: float32 [4, 65536], P(None, ('sub', 'slab')), may hold values from -6 to 6
- operator: float32 [7, 4, 4, 65536], P(None, None, None, ('sub', 'slab')), as said below
- prolong: float32 [4, 4, 65536], P(None, None, ('sub', 'slab')), may hold values from -2 to 2
- columns: int32 [7, 65536], P(None, ('sub', 'slab')), may hold values from 0 to 4095, as said below
- slots: int32 [7, 65536], P(None, ('sub', 'slab')), may hold values from 0 to 6
- aggregates: int32 [65536], P(('sub', 'slab')), may hold values from 0 to 255, as said below
- sends: int32 [65536], P(('sub', 'slab')), may hold values from 0 to 2047, as said below
- prolong_one: float32 [4, 4, 16384], P(None, None, ('sub', 'slab')), as said below
- columns_one: int32 [7, 16384], P(None, ('sub', 'slab')), may hold values from 0 to 895, as said below
- slots_one: int32 [7, 16384], P(None, ('sub', 'slab')), may hold values from 0 to 6, as said below
- aggregates_one: int32 [16384], P(('sub', 'slab')), may hold values from 0 to 63, as said below
- sends_one: int32 [12288], P(('sub', 'slab')), may hold values from 0 to 511, as said below
- columns_two: int32 [7, 4096], P(None, ('sub', 'slab')), may hold values from 0 to 287, as said below
- sends_two: int32 [5120], P(('sub', 'slab')), may hold values from 0 to 127, as said below
Outputs:
- smoothed: float32 [4, 65536], P(None, ('sub', 'slab'))
- smoothed_one: float32 [4, 8192], P(None, ('sub', 'slab'))
- smoothed_two: float32 [4, 1024], P(None, ('sub', 'slab'))
Inputs may be any that keep to these rules, and one draw needn't show every extreme that they name: Fine operator blocks; no other structure. `columns`: values below 2048 name the subdomain's own rows, the rest its ghost rows; every neighbour of a fine cell lies one or two cells away along one grid dimension, the third dimension closes into a loop. `aggregates`: eight fine rows a first-level aggregate. `sends`: local row numbers of the fine subdomain. `prolong_one`: equal on the two devices of a merged subdomain. `columns_one`: values below 512 name the merged subdomain's rows, the rest its ghost rows; equal on both devices of a merged subdomain. `slots_one`: equal on both devices of a merged subdomain. `aggregates_one`: eight first-level rows a second-level aggregate; equal on both devices of a merged subdomain. `sends_one`: row numbers of the merged first-level subdomain. `columns_two`: values below 128 name the merged subdomain's rows, the rest its ghost rows; equal on all four devices of a merged subdomain. `sends_two`: row numbers of the merged second-level subdomain.
All inputs are finite; a program needn't handle non-finite values.
Results may differ from a plain program's by a relative error of at most 0.0001.
Values sent between devices are 32-bit elements; how exact they have to be, the bound alone decides.
No kernel may reach another device: no remote copies, remote signals or barrier semaphores. Data moves between devices by JAX's collectives and lax.ppermute only.
A program may use at most 128 MiB of HBM per device.

v0:
```python
import jax
import jax.numpy as jnp
from jax import lax
from jax.sharding import PartitionSpec as P

GX = 8
GY = 8
GZ = 32


def from_behind(value, axis, steps):
    count = lax.axis_size(axis)
    initial, last = (max(0, -steps), min(count, count - steps))
    return lax.ppermute(value, axis, [(source, source + steps) for source in range(initial, last)])


def from_partner(block, axis, bit):
    count = lax.axis_size(axis)
    route = []
    for low in range(count):
        high = low | 1 << bit
        if high != low and high < count:
            route += [(low, high), (high, low)]
    return lax.ppermute(block, axis, route)


def apply_rows(operator, columns, extended):
    nearby = extended[:, columns]
    total = jnp.zeros_like(operator[0, :, 0, :])
    for comp in range(4):
        total = total + jnp.sum(operator[:, :, comp, :] * nearby[comp][:, None, :], axis=0)
    return total


def row_weights(operator):
    return 1.0 + jnp.sum(jnp.abs(operator), axis=(0, 2))


def restrict_rows(prolong, residual, aggregates, coarse):
    lifted = jnp.sum(prolong * residual[:, None, :], axis=0)
    return jnp.zeros((4, coarse), lifted.dtype).at[:, aggregates].add(lifted)


def galerkin_rows(operator, prolong, columns, slots, aggregates, extended, coarse):
    nearby = extended[:, :, columns]
    inner = jnp.zeros((4,) + nearby.shape[1:], nearby.dtype)
    for comp in range(4):
        inner = (
            inner
            + jnp.transpose(operator[:, :, comp, :], (1, 0, 2))[:, None, :, :] * nearby[comp][None]
        )
    blocks = jnp.zeros_like(inner)
    for comp in range(4):
        blocks = blocks + prolong[comp][:, None, None, :] * inner[comp][None]
    target = (slots * coarse + aggregates[None, :]).reshape(-1)
    total = jnp.zeros((16, 7 * coarse), blocks.dtype).at[:, target].add(blocks.reshape(16, -1))
    return total.reshape(4, 4, 7, coarse).transpose(2, 0, 1, 3)


def slab_move(piece, offset):
    return from_behind(piece, "slab", offset)


def sub_move(piece, offset):
    return from_behind(piece, "sub", offset)


def slab_carry(piece, offset):
    return from_behind(piece, "slab", offset)


def sub_carry(piece, offset):
    return from_behind(piece, "sub", offset)


def extend(values, sends, faces, group, blocks):
    first_count, second_count = faces
    picked = values[:, sends]
    low_first = picked[:, :first_count]
    high_first = picked[:, first_count : 2 * first_count]
    low_second = picked[:, 2 * first_count : 2 * first_count + second_count]
    high_second = picked[:, 2 * first_count + second_count :]
    if blocks:
        parts = [
            slab_carry(high_first, 1),
            slab_carry(low_first, -1),
            sub_carry(high_second, group),
            sub_carry(low_second, -group),
        ]
    else:
        parts = [
            slab_move(high_first, 1),
            slab_move(low_first, -1),
            sub_move(high_second, group),
            sub_move(low_second, -group),
        ]
    return jnp.concatenate([values] + parts, axis=1)


def smooth_level(operator, columns, source, sends, faces, group, final):
    weights = row_weights(operator)
    first = source / weights
    residual = source - apply_rows(operator, columns, extend(first, sends, faces, group, False))
    second = first + residual / weights
    if final:
        residual = source - apply_rows(
            operator, columns, extend(second, sends, faces, group, False)
        )
    return (second, residual)


def join_halves(own, other, parity):
    lower = jnp.concatenate([own, other], axis=-1)
    upper = jnp.concatenate([other, own], axis=-1)
    return jnp.where(parity == 0, lower, upper)


def on_device(
    source,
    operator,
    prolong,
    columns,
    slots,
    aggregates,
    sends,
    prolong_one,
    columns_one,
    slots_one,
    aggregates_one,
    sends_one,
    columns_two,
    sends_two,
):
    faces_zero = (2 * GY * GZ, 2 * GX * GZ)
    faces_one = (GY * (GZ // 2), GX // 2 * (GZ // 2))
    faces_two = (GY * (GZ // 4), GX // 4 * (GZ // 4))
    rows_one = source.shape[1] // 8
    coarse_two = rows_one // 4
    smoothed, residual = smooth_level(operator, columns, source, sends, faces_zero, 1, True)
    source_own = restrict_rows(prolong, residual, aggregates, rows_one)
    extended_zero = extend(prolong.reshape(16, -1), sends, faces_zero, 1, True).reshape(4, 4, -1)
    operator_own = galerkin_rows(
        operator, prolong, columns, slots, aggregates, extended_zero, rows_one
    )
    parity = lax.axis_index("sub") % 2
    extended_one = extend(prolong_one.reshape(16, -1), sends_one, faces_one, 2, True).reshape(
        4, 4, -1
    )
    other_source, other_operator = from_partner((source_own, operator_own), "sub", 0)
    source_merged = join_halves(source_own, other_source, parity)
    operator_merged = join_halves(operator_own, other_operator, parity)
    merged_smooth, residual_one = smooth_level(
        operator_merged, columns_one, source_merged, sends_one, faces_one, 2, True
    )
    smoothed_one = lax.dynamic_slice_in_dim(merged_smooth, parity * rows_one, rows_one, 1)
    source_pair = restrict_rows(prolong_one, residual_one, aggregates_one, coarse_two)
    operator_pair = galerkin_rows(
        operator_merged,
        prolong_one,
        columns_one,
        slots_one,
        aggregates_one,
        extended_one,
        coarse_two,
    )
    quad_bit = lax.axis_index("sub") // 2 % 2
    other_source_two, other_operator_two = from_partner((source_pair, operator_pair), "sub", 1)
    source_group = join_halves(source_pair, other_source_two, quad_bit)
    operator_group = join_halves(operator_pair, other_operator_two, quad_bit)
    group_smooth, unused = smooth_level(
        operator_group, columns_two, source_group, sends_two, faces_two, 4, False
    )
    share = source_group.shape[1] // 4
    smoothed_two = lax.dynamic_slice_in_dim(
        group_smooth, lax.axis_index("sub") % 4 * share, share, 1
    )
    return (smoothed, smoothed_one, smoothed_two)


def solution(mesh):
    placed = (
        P(None, ("sub", "slab")),
        P(None, None, None, ("sub", "slab")),
        P(None, None, ("sub", "slab")),
        P(None, ("sub", "slab")),
        P(None, ("sub", "slab")),
        P(("sub", "slab")),
        P(("sub", "slab")),
        P(None, None, ("sub", "slab")),
        P(None, ("sub", "slab")),
        P(None, ("sub", "slab")),
        P(("sub", "slab")),
        P(("sub", "slab")),
        P(None, ("sub", "slab")),
        P(("sub", "slab")),
    )
    return jax.shard_map(
        on_device,
        mesh=mesh,
        in_specs=placed,
        out_specs=(P(None, ("sub", "slab")), P(None, ("sub", "slab")), P(None, ("sub", "slab"))),
        check_vma=False,
    )
```

profile of v0, /device:TPU:0, one launch (start us, length us, event | category | flops | bytes accessed | tf_op | source)
XLA Modules:
  0.0 562.3 jit_solution(15158373169776939139)
XLA Ops:
  0.7 1.5 abs_reduce_fusion
  4.1 5.5 gather_fusion
  10.5 4.8 collective-permute-start
  22.8 5.0 collective-permute-start.23
  27.8 3.4 fusion.32
  32.2 1.5 slice_bitcast_fusion.27
  36.9 5.5 gather_fusion.4
  50.0 7.0 %collective-permute-start.25 = (f32[16,64]{0,1:T(8,128)}, f32[16,64]{0,1:T(8,128)}, u32[]{:S(2)}, u32[]{:S(2)}) collective-permute-start(f32[16,64]{0,1:T(8,128)} %get-tuple-element.58), channel_id=1, source_target_pairs={{0,4},{2,6},{4,8},{6,10},{8,12},{10,14},{12,16},{14,18},{16,20},{1... | collective-permute-start | bytes 12296 | tf_op jit(solution)/shard_map/ppermute | solution.py:14
  59.0 48.2 %gather_fusion.1 = f32[14336,4]{1,0:T(8,128)} fusion(f32[4,4096]{0,1:T(8,128)S(1)} %copy.304, s32[14336]{0:T(1024)S(1)} %broadcast_clamp_fusion), kind=kCustom, calls=%fused_computation.1 | custom fusion | bytes 516096 | tf_op jit(solution)/shard_map/gather | solution.py:28
  107.2 5.2 copy.305
  113.8 5.5 gather_fusion.2
  119.6 5.1 collective-permute-start.4
  126.5 1.8 copy.322
  128.3 1.8 copy.323
  130.1 1.8 copy.324
  131.8 2.0 collective-permute-start.9
  136.8 2.0 collective-permute-start.11
  143.2 11.3 %gather_fusion.11 = f32[3584,4,4]{2,1,0:T(4,128)} fusion(f32[4,4,896]{1,0,2:T(4,128)S(1)} %copy.349, s32[4096]{0:T(1024)S(1)} %pad_clamp_fusion), kind=kCustom, calls=%fused_computation.11 | custom fusion | bytes 473088 | tf_op jit(solution)/shard_map/gather | solution.py:45
  154.5 5.7 %copy.365 = f32[7,512,4,4]{1,0,3,2:T(8,128)} copy(f32[7,512,4,4]{3,2,1,0:T(4,128)} %bitcast.242) | data formatting | bytes 458752 | tf_op jit(solution)/shard_map/gather | solution.py:45
  162.2 4.4 collective-permute-done.5
  166.6 4.3 collective-permute-start.6
  173.8 3.1 collective-permute-done.7
  177.4 1.5 copy.308
  178.9 48.2 %gather_fusion.3 = f32[14336,4]{1,0:T(8,128)} fusion(f32[4,4096]{0,1:T(8,128)S(1)} %copy.308, s32[14336]{0:T(1024)S(1)} %broadcast_clamp_fusion), kind=kCustom, calls=%fused_computation.3 | custom fusion | bytes 516096 | tf_op jit(solution)/shard_map/gather | solution.py:28
  227.1 5.2 copy.309
  237.8 6.0 %copy.320 = f32[4,4,4096]{1,0,2:T(4,128)} copy(f32[4,4,4096]{2,1,0:T(4,128)S(1)} %constant_dynamic-update-slice_fusion.10) | data formatting | bytes 524288 | tf_op jit(solution)/shard_map/concatenate | solution.py:97
  243.8 107.7 %gather_fusion.5 = f32[14336,4,4]{2,1,0:T(4,128)} fusion(f32[4,4,4096]{1,0,2:T(4,128)} %copy.320, s32[14336]{0:T(1024)S(1)} %broadcast_clamp_fusion), kind=kCustom, calls=%fused_computation.5 | custom fusion | bytes 1892352 | tf_op jit(solution)/shard_map/gather | solution.py:45
  351.5 18.7 %copy.364 = f32[7,2048,4,4]{1,0,3,2:T(8,128)S(1)} copy(f32[7,2048,4,4]{3,2,1,0:T(4,128)} %bitcast.240) | data formatting | bytes 1835008 | tf_op jit(solution)/shard_map/gather | solution.py:45
  371.9 4.5 copy.325
  376.4 77.0 %scatter_custom_fusion.1 = f32[16,1792]{0,1:T(8,128)S(1)} fusion(s32[14336]{0:T(1024)} %bitcast.273, f32[14336,16]{1,0:T(8,128)} %copy.325, f32[]{:T(128)} %constant.28.clone.1), kind=kCustom, calls=%fused_computation.21 | custom fusion | flops 229376 | bytes 115200 | tf_op jit(solution)/shard_map/scatter-add | solution.py:56
  453.7 3.0 collective-permute-start.13
  457.1 11.6 %scatter_custom_fusion = f32[4,256]{0,1:T(8,128)S(1)} fusion(s32[2048]{0:T(1024)} %compare_select_fusion.4, f32[2048,4]{1,0:T(8,128)S(1)} %copy.310, f32[]{:T(128)} %constant.28.clone.1), kind=kCustom, calls=%fused_computation.80 | custom fusion | flops 8192 | bytes 4608 | tf_op jit(solution)/shard_map/scatter-add | solution.py:41
  471.5 1.7 collective-permute-start.14
  474.4 6.4 %collective-permute-start.16 = (f32[4,64]{1,0:T(4,128)S(1)}, f32[4,64]{1,0:T(4,128)S(1)}, u32[]{:S(2)}, u32[]{:S(2)}) collective-permute-start(f32[4,64]{1,0:T(4,128)S(1)} %get-tuple-element.102), channel_id=1, source_target_pairs={{0,4},{2,6},{4,8},{6,10},{8,12},{10,14},{12,16},{14,18},{16,20},{1... | collective-permute-start | bytes 3080 | tf_op jit(solution)/shard_map/ppermute | solution.py:14
  480.9 1.5 collective-permute-start.17
  483.6 19.8 %scatter_custom_fusion.3 = f32[16,448]{0,1:T(8,128)S(1)} fusion(s32[3584]{0:T(1024)} %fusion.24, f32[3584,16]{1,0:T(8,128)S(1)} %copy.354, f32[]{:T(128)} %constant.28.clone.1), kind=kCustom, calls=%fused_computation.58 | custom fusion | flops 57344 | bytes 29184 | tf_op jit(solution)/shard_map/scatter-add | solution.py:56
  503.6 2.7 collective-permute-start.27
  506.6 5.7 %gather_fusion.7 = f32[3584,4]{1,0:T(8,128)S(1)} fusion(f32[4,896]{0,1:T(8,128)S(1)} %copy.330, s32[4096]{0:T(1024)S(1)} %pad_clamp_fusion), kind=kCustom, calls=%fused_computation.7 | custom fusion | bytes 129024 | tf_op jit(solution)/shard_map/gather | solution.py:28
  514.7 4.6 collective-permute-start.18
  520.5 1.9 collective-permute-start.20
  524.4 4.6 collective-permute-done.21
  529.3 5.7 %gather_fusion.9 = f32[3584,4]{1,0:T(8,128)S(1)} fusion(f32[4,896]{0,1:T(8,128)S(1)} %copy.337, s32[4096]{0:T(1024)S(1)} %pad_clamp_fusion), kind=kCustom, calls=%fused_computation.9 | custom fusion | bytes 129024 | tf_op jit(solution)/shard_map/gather | solution.py:28
  536.1 2.4 scatter_custom_fusion.2
  538.6 2.9 collective-permute-start.22
  544.3 4.5 collective-permute-start.28
  550.1 3.5 collective-permute-start.30
  554.9 4.2 collective-permute-done.31
  559.3 1.9 gather_fusion.13
  (251 shorter events, 67.0 us)
Async XLA Ops:
  0.6 43.3 %copy-start.13 = (s32[7,2048]{1,0:T(8,128)S(1)}, s32[7,2048]{1,0:T(8,128)}, u32[]{:S(2)}) copy-start(s32[7,2048]{1,0:T(8,128)} %param.18) | copy-start | bytes 172036
  0.7 44.1 %copy-start.21 = (s32[7,512]{1,0:T(8,128)S(1)}, s32[7,512]{1,0:T(8,128)}, u32[]{:S(2)}) copy-start(s32[7,512]{1,0:T(8,128)} %param.22) | copy-start | bytes 43012
  0.7 44.1 %copy-start.23 = (s32[512]{0:T(512)S(1)}, s32[512]{0:T(512)}, u32[]{:S(2)}) copy-start(s32[512]{0:T(512)} %param.24) | copy-start | bytes 6148
  0.7 44.7 %copy-start.22 = (s32[7,512]{1,0:T(8,128)S(1)}, s32[7,512]{1,0:T(8,128)}, u32[]{:S(2)}) copy-start(s32[7,512]{1,0:T(8,128)} %param.23) | copy-start | bytes 43012
  0.7 45.4 %copy-start.25 = (s32[160]{0:T(256)S(1)}, s32[160]{0:T(256)}, u32[]{:S(2)}) copy-start(s32[160]{0:T(256)} %param.27) | copy-start | bytes 1924
  0.7 45.4 %copy-start.24 = (s32[7,128]{1,0:T(8,128)S(1)}, s32[7,128]{1,0:T(8,128)}, u32[]{:S(2)}) copy-start(s32[7,128]{1,0:T(8,128)} %param.26) | copy-start | bytes 10756
  10.5 38.2 %collective-permute-start = (f32[4,512]{1,0:T(4,128)}, f32[4,512]{1,0:T(4,128)S(1)}, u32[]{:S(2)}, u32[]{:S(2)}) collective-permute-start(f32[4,512]{1,0:T(4,128)} %get-tuple-element.92), channel_id=1, source_target_pairs={{0,1},{2,3},{4,5},{6,7},{8,9},{10,11},{12,13},{14,15},{16,17},{18,... | collective-permute-start | bytes 24584 | tf_op jit(solution)/shard_map/ppermute | solution.py:14
  15.3 34.6 %collective-permute-start.1 = (f32[4,512]{1,0:T(4,128)}, f32[4,512]{1,0:T(4,128)S(1)}, u32[]{:S(2)}, u32[]{:S(2)}) collective-permute-start(f32[4,512]{1,0:T(4,128)} %get-tuple-element.91), channel_id=1, source_target_pairs={{1,0},{3,2},{5,4},{7,6},{9,8},{11,10},{13,12},{15,14},{17,16},{19,... | collective-permute-start | bytes 24584 | tf_op jit(solution)/shard_map/ppermute | solution.py:14
  16.6 40.4 %collective-permute-start.2 = (f32[4,512]{1,0:T(4,128)}, f32[4,512]{1,0:T(4,128)S(1)}, u32[]{:S(2)}, u32[]{:S(2)}) collective-permute-start(f32[4,512]{1,0:T(4,128)} %get-tuple-element.90), channel_id=1, source_target_pairs={{0,2},{2,4},{4,6},{6,8},{8,10},{10,12},{12,14},{14,16},{16,18},{18... | collective-permute-start | bytes 24584 | tf_op jit(solution)/shard_map/ppermute | solution.py:14
  18.1 40.2 %collective-permute-start.3 = (f32[4,512]{1,0:T(4,128)S(1)}, f32[4,512]{1,0:T(4,128)S(1)}, u32[]{:S(2)}, u32[]{:S(2)}) collective-permute-start(f32[4,512]{1,0:T(4,128)S(1)} %get-tuple-element.89), channel_id=1, source_target_pairs={{2,0},{4,2},{6,4},{8,6},{10,8},{12,10},{14,12},{16,14},{18,16},{20... | collective-permute-start | bytes 24584 | tf_op jit(solution)/shard_map/ppermute | solution.py:14
  20.1 87.1 %copy-start.18 = (s32[1024]{0:T(1024)}, s32[1024]{0:T(1024)S(1)}, u32[]{:S(2)}) copy-start(s32[1024]{0:T(1024)S(1)} %pad_clamp_fusion.3) | copy-start | bytes 12292
  22.8 114.0 %collective-permute-start.23 = (f32[16,128]{0,1:T(8,128)}, f32[16,128]{0,1:T(8,128)}, u32[]{:S(2)}, u32[]{:S(2)}) collective-permute-start(f32[16,128]{0,1:T(8,128)} %get-tuple-element.60), channel_id=1, source_target_pairs={{0,1},{2,3},{4,5},{6,7},{8,9},{10,11},{12,13},{14,15},{16,17},{18,... | collective-permute-start | bytes 24584 | tf_op jit(solution)/shard_map/ppermute | solution.py:14
  47.1 65.7 %copy-start.6 = (f32[4,2048]{1,0:T(4,128)S(1)}, f32[4,2048]{1,0:T(4,128)}, u32[]{:S(2)}) copy-start(f32[4,2048]{1,0:T(4,128)} %param.14) | copy-start | bytes 98308
  48.7 91.0 %collective-permute-start.24 = (f32[16,128]{0,1:T(8,128)}, f32[16,128]{0,1:T(8,128)}, u32[]{:S(2)}, u32[]{:S(2)}) collective-permute-start(f32[16,128]{0,1:T(8,128)} %get-tuple-element.59), channel_id=1, source_target_pairs={{1,0},{3,2},{5,4},{7,6},{9,8},{11,10},{13,12},{15,14},{17,16},{19,... | collective-permute-start | bytes 24584 | tf_op jit(solution)/shard_map/ppermute | solution.py:14
  50.0 81.8 %collective-permute-start.25 = (f32[16,64]{0,1:T(8,128)}, f32[16,64]{0,1:T(8,128)}, u32[]{:S(2)}, u32[]{:S(2)}) collective-permute-start(f32[16,64]{0,1:T(8,128)} %get-tuple-element.58), channel_id=1, source_target_pairs={{0,4},{2,6},{4,8},{6,10},{8,12},{10,14},{12,16},{14,18},{16,20},{1... | collective-permute-start | bytes 12296 | tf_op jit(solution)/shard_map/ppermute | solution.py:14
  57.0 77.7 %collective-permute-start.26 = (f32[16,64]{0,1:T(8,128)}, f32[16,64]{0,1:T(8,128)}, u32[]{:S(2)}, u32[]{:S(2)}) collective-permute-start(f32[16,64]{0,1:T(8,128)} %get-tuple-element.57), channel_id=1, source_target_pairs={{4,0},{6,2},{8,4},{10,6},{12,8},{14,10},{16,12},{18,14},{20,16},{2... | collective-permute-start | bytes 12296 | tf_op jit(solution)/shard_map/ppermute | solution.py:14
  119.6 40.5 %collective-permute-start.4 = (f32[4,512]{1,0:T(4,128)S(1)}, f32[4,512]{1,0:T(4,128)S(1)}, u32[]{:S(2)}, u32[]{:S(2)}) collective-permute-start(f32[4,512]{1,0:T(4,128)S(1)} %get-tuple-element.88), channel_id=1, source_target_pairs={{0,1},{2,3},{4,5},{6,7},{8,9},{10,11},{12,13},{14,15},{16,17},{18,... | collective-permute-start | bytes 24584 | tf_op jit(solution)/shard_map/ppermute | solution.py:14
  131.8 101.6 %collective-permute-start.9 = (f32[16,512]{0,1:T(8,128)}, f32[16,512]{0,1:T(8,128)}, u32[]{:S(2)}, u32[]{:S(2)}) collective-permute-start(f32[16,512]{0,1:T(8,128)} %get-tuple-element.32), channel_id=1, source_target_pairs={{0,1},{2,3},{4,5},{6,7},{8,9},{10,11},{12,13},{14,15},{16,17},{18,... | collective-permute-start | bytes 98312 | tf_op jit(solution)/shard_map/ppermute | solution.py:14
  134.7 99.8 %collective-permute-start.10 = (f32[16,512]{0,1:T(8,128)}, f32[16,512]{0,1:T(8,128)}, u32[]{:S(2)}, u32[]{:S(2)}) collective-permute-start(f32[16,512]{0,1:T(8,128)} %get-tuple-element.31), channel_id=1, source_target_pairs={{1,0},{3,2},{5,4},{7,6},{9,8},{11,10},{13,12},{15,14},{17,16},{19,... | collective-permute-start | bytes 98312 | tf_op jit(solution)/shard_map/ppermute | solution.py:14
  136.8 98.8 %collective-permute-start.11 = (f32[16,512]{0,1:T(8,128)}, f32[16,512]{0,1:T(8,128)}, u32[]{:S(2)}, u32[]{:S(2)}) collective-permute-start(f32[16,512]{0,1:T(8,128)} %get-tuple-element.30), channel_id=1, source_target_pairs={{0,2},{2,4},{4,6},{6,8},{8,10},{10,12},{12,14},{14,16},{16,18},{18... | collective-permute-start | bytes 98312 | tf_op jit(solution)/shard_map/ppermute | solution.py:14
  139.7 97.0 %collective-permute-start.12 = (f32[16,512]{0,1:T(8,128)}, f32[16,512]{0,1:T(8,128)}, u32[]{:S(2)}, u32[]{:S(2)}) collective-permute-start(f32[16,512]{0,1:T(8,128)} %get-tuple-element.29), channel_id=1, source_target_pairs={{2,0},{4,2},{6,4},{8,6},{10,8},{12,10},{14,12},{16,14},{18,16},{20... | collective-permute-start | bytes 98312 | tf_op jit(solution)/shard_map/ppermute | solution.py:14
  160.2 72.6 %copy-start = (f32[4,4,2048]{2,1,0:T(4,128)S(1)}, f32[4,4,2048]{2,1,0:T(4,128)}, u32[]{:S(2)}) copy-start(f32[4,4,2048]{2,1,0:T(4,128)} %param.16) | copy-start | bytes 393220
  160.2 6.4 %collective-permute-start.5 = (f32[4,512]{1,0:T(4,128)S(1)}, f32[4,512]{1,0:T(4,128)S(1)}, u32[]{:S(2)}, u32[]{:S(2)}) collective-permute-start(f32[4,512]{1,0:T(4,128)S(1)} %get-tuple-element.87), channel_id=1, source_target_pairs={{1,0},{3,2},{5,4},{7,6},{9,8},{11,10},{13,12},{15,14},{17,16},{19,... | collective-permute-start | bytes 24584 | tf_op jit(solution)/shard_map/ppermute | solution.py:14
  166.6 5.1 collective-permute-start.6
  171.7 5.1 collective-permute-start.7
  370.8 85.9 %copy-start.4 = (f32[7,512,4,4]{1,0,3,2:T(8,128)S(1)}, f32[7,512,4,4]{1,0,3,2:T(8,128)}, u32[]{:S(2)}) copy-start(f32[7,512,4,4]{1,0,3,2:T(8,128)} %copy.365) | copy-start | bytes 688132
  371.1 85.6 %copy-start.11 = (f32[4,2048]{1,0:T(4,128)S(1)}, f32[4,2048]{1,0:T(4,128)}, u32[]{:S(2)}) copy-start(f32[4,2048]{1,0:T(4,128)} %get-tuple-element.61) | copy-start | bytes 98308
  371.3 98.8 %copy-start.19 = (s32[1024]{0:T(1024)S(1)}, s32[1024]{0:T(1024)}, u32[]{:S(2)}) copy-start(s32[1024]{0:T(1024)} %copy-done.18) | copy-start | bytes 12292
  371.9 111.0 %copy-start.14 = (f32[4,512]{1,0:T(4,128)S(1)}, f32[4,512]{1,0:T(4,128)}, u32[]{:S(2)}) copy-start(f32[4,512]{1,0:T(4,128)} %get-tuple-element.82) | copy-start | bytes 24580
  371.9 111.0 %copy-start.15 = (f32[4,512]{1,0:T(4,128)S(1)}, f32[4,512]{1,0:T(4,128)}, u32[]{:S(2)}) copy-start(f32[4,512]{1,0:T(4,128)} %get-tuple-element.83) | copy-start | bytes 24580
  371.9 111.0 %copy-start.16 = (f32[4,512]{1,0:T(4,128)S(1)}, f32[4,512]{1,0:T(4,128)}, u32[]{:S(2)}) copy-start(f32[4,512]{1,0:T(4,128)} %get-tuple-element.84) | copy-start | bytes 24580
  453.7 15.1 %collective-permute-start.13 = (f32[7,4,4,256]{3,0,2,1:T(8,128)S(1)}, f32[7,4,4,256]{3,0,2,1:T(8,128)S(1)}, u32[]{:S(2)}, u32[]{:S(2)}) collective-permute-start(f32[7,4,4,256]{3,0,2,1:T(8,128)S(1)} %bitcast.255), channel_id=1, source_target_pairs={{0,2},{2,0},{4,6},{6,4},{8,10},{10,8},{12,14},{14,12},{16,18},{18,... | collective-permute-start | bytes 344072 | tf_op jit(solution)/shard_map/ppermute | solution.py:24
  468.8 1.2 collective-permute-start.8
  471.5 34.8 %collective-permute-start.14 = (f32[4,128]{1,0:T(4,128)S(1)}, f32[4,128]{1,0:T(4,128)S(1)}, u32[]{:S(2)}, u32[]{:S(2)}) collective-permute-start(f32[4,128]{1,0:T(4,128)S(1)} %get-tuple-element.104), channel_id=1, source_target_pairs={{0,1},{2,3},{4,5},{6,7},{8,9},{10,11},{12,13},{14,15},{16,17},{18,... | collective-permute-start | bytes 6152 | tf_op jit(solution)/shard_map/ppermute | solution.py:14
  473.1 33.2 %collective-permute-start.15 = (f32[4,128]{1,0:T(4,128)S(1)}, f32[4,128]{1,0:T(4,128)S(1)}, u32[]{:S(2)}, u32[]{:S(2)}) collective-permute-start(f32[4,128]{1,0:T(4,128)S(1)} %get-tuple-element.103), channel_id=1, source_target_pairs={{1,0},{3,2},{5,4},{7,6},{9,8},{11,10},{13,12},{15,14},{17,16},{19,... | collective-permute-start | bytes 6152 | tf_op jit(solution)/shard_map/ppermute | solution.py:14
  474.4 31.9 %collective-permute-start.16 = (f32[4,64]{1,0:T(4,128)S(1)}, f32[4,64]{1,0:T(4,128)S(1)}, u32[]{:S(2)}, u32[]{:S(2)}) collective-permute-start(f32[4,64]{1,0:T(4,128)S(1)} %get-tuple-element.102), channel_id=1, source_target_pairs={{0,4},{2,6},{4,8},{6,10},{8,12},{10,14},{12,16},{14,18},{16,20},{1... | collective-permute-start | bytes 3080 | tf_op jit(solution)/shard_map/ppermute | solution.py:14
  480.9 25.4 %collective-permute-start.17 = (f32[4,64]{1,0:T(4,128)S(1)}, f32[4,64]{1,0:T(4,128)S(1)}, u32[]{:S(2)}, u32[]{:S(2)}) collective-permute-start(f32[4,64]{1,0:T(4,128)S(1)} %get-tuple-element.101), channel_id=1, source_target_pairs={{4,0},{6,2},{8,4},{10,6},{12,8},{14,10},{16,12},{18,14},{20,16},{2... | collective-permute-start | bytes 3080 | tf_op jit(solution)/shard_map/ppermute | solution.py:14
  482.5 76.9 %copy-start.20 = (s32[1024]{0:T(1024)S(1)}, s32[1024]{0:T(1024)}, u32[]{:S(2)}) copy-start(s32[1024]{0:T(1024)} %pad_clamp_fusion.1) | copy-start | bytes 12292
  503.6 37.8 %collective-permute-start.27 = (f32[7,4,4,64]{3,0,2,1:T(8,128)S(1)}, f32[7,4,4,64]{3,0,2,1:T(8,128)S(1)}, u32[]{:S(2)}, u32[]{:S(2)}) collective-permute-start(f32[7,4,4,64]{3,0,2,1:T(8,128)S(1)} %bitcast.258), channel_id=1, source_target_pairs={{0,4},{4,0},{2,6},{6,2},{8,12},{12,8},{10,14},{14,10},{16,20},{20,... | collective-permute-start | bytes 86024 | tf_op jit(solution)/shard_map/ppermute | solution.py:24
  514.7 14.3 %collective-permute-start.18 = (f32[4,128]{1,0:T(4,128)S(1)}, f32[4,128]{1,0:T(4,128)S(1)}, u32[]{:S(2)}, u32[]{:S(2)}) collective-permute-start(f32[4,128]{1,0:T(4,128)S(1)} %get-tuple-element.100), channel_id=1, source_target_pairs={{0,1},{2,3},{4,5},{6,7},{8,9},{10,11},{12,13},{14,15},{16,17},{18,... | collective-permute-start | bytes 6152 | tf_op jit(solution)/shard_map/ppermute | solution.py:14
  519.2 9.8 %collective-permute-start.19 = (f32[4,128]{1,0:T(4,128)S(1)}, f32[4,128]{1,0:T(4,128)S(1)}, u32[]{:S(2)}, u32[]{:S(2)}) collective-permute-start(f32[4,128]{1,0:T(4,128)S(1)} %get-tuple-element.99), channel_id=1, source_target_pairs={{1,0},{3,2},{5,4},{7,6},{9,8},{11,10},{13,12},{15,14},{17,16},{19,... | collective-permute-start | bytes 6152 | tf_op jit(solution)/shard_map/ppermute | solution.py:14
  520.5 3.8 collective-permute-start.20
  522.5 6.5 %collective-permute-start.21 = (f32[4,64]{1,0:T(4,128)S(1)}, f32[4,64]{1,0:T(4,128)S(1)}, u32[]{:S(2)}, u32[]{:S(2)}) collective-permute-start(f32[4,64]{1,0:T(4,128)S(1)} %get-tuple-element.97), channel_id=1, source_target_pairs={{4,0},{6,2},{8,4},{10,6},{12,8},{14,10},{16,12},{18,14},{20,16},{2... | collective-permute-start | bytes 3080 | tf_op jit(solution)/shard_map/ppermute | solution.py:14
  538.6 4.5 collective-permute-start.22
  544.3 14.8 %collective-permute-start.28 = (f32[4,64]{1,0:T(4,128)S(1)}, f32[4,64]{1,0:T(4,128)S(1)}, u32[]{:S(2)}, u32[]{:S(2)}) collective-permute-start(f32[4,64]{1,0:T(4,128)S(1)} %get-tuple-element.108), channel_id=1, source_target_pairs={{0,1},{2,3},{4,5},{6,7},{8,9},{10,11},{12,13},{14,15},{16,17},{18,... | collective-permute-start | bytes 3080 | tf_op jit(solution)/shard_map/ppermute | solution.py:14
  548.8 10.3 %collective-permute-start.29 = (f32[4,64]{1,0:T(4,128)S(1)}, f32[4,64]{1,0:T(4,128)S(1)}, u32[]{:S(2)}, u32[]{:S(2)}) collective-permute-start(f32[4,64]{1,0:T(4,128)S(1)} %get-tuple-element.107), channel_id=1, source_target_pairs={{1,0},{3,2},{5,4},{7,6},{9,8},{11,10},{13,12},{15,14},{17,16},{19,... | collective-permute-start | bytes 3080 | tf_op jit(solution)/shard_map/ppermute | solution.py:14
  550.1 4.8 collective-permute-start.30
  553.6 5.5 collective-permute-start.31
  (10 other events, 149.2 us)
where the time goes:
time: 565 us; the launch traced here: 562 us
  local copies, waits for them, and re-layouts  337 us (60%)
  other arithmetic  123 us (22%)
  starting transfers between devices  81.6 us (14%)
  waiting for transfers between devices  19 us (3%)
    gather x4, local copies, waits for them, and re-layouts, galerkin_rows(): nearby = extended[:, :, columns]  143 us
    gather x10, local copies, waits for them, and re-layouts, apply_rows(): nearby = extended[:, columns]  121 us
    scatter-add x2, other arithmetic, galerkin_rows(): jnp.zeros((16, 7 * coarse), blocks.dtype).at[:, target]  96.8 us
    ppermute x28, starting transfers between devices, from_behind(): lax.ppermute(value, axis, [(source, source + steps) for source in range(i...  73 us
    gather x12, local copies, waits for them, and re-layouts, extend(): picked = values[:, sends]  21.5 us
    ppermute x28, waiting for transfers between devices, from_behind(): lax.ppermute(value, axis, [(source, source + steps) for source in range(i...  16.5 us
    scatter-add x2, other arithmetic, restrict_rows(): return jnp.zeros((4, coarse), lifted.dtype).at[:, aggregates].add(lifted)  14 us
  transfers between devices with their start and end apart: 32, of which 7 were waited for; matrix products, arithmetic and copies ran while one was open for 40% of the time, Pallas kernels for 0%

commit v1 on v0

v1 whole, which is shorter than its diff:
```python
import functools

import jax
import jax.numpy as jnp
from jax import lax
from jax.experimental import pallas as pl
from jax.experimental.pallas import tpu as pltpu
from jax.sharding import PartitionSpec as P

GX = 8
GY = 8
GZ = 32
LANES = 128
F32 = jnp.float32
BF16 = jnp.bfloat16


def split(value):
    high = value.astype(BF16)
    return high, (value - high.astype(F32)).astype(BF16)


def upper_half(shape):
    return lax.broadcasted_iota(jnp.int32, shape, 0) >= 4


def fold(value):
    return value + pltpu.roll(value, 4, 0)


def pair_rows(first, second):
    return jnp.where(upper_half(first.shape), second, first)


def twice(rows):
    return jnp.concatenate([rows, rows], axis=0)


def table_four(chunks):
    if len(chunks) % 2:
        chunks = chunks + [jnp.zeros_like(chunks[0])]
    rows = [pair_rows(chunks[j], chunks[j + 1]) for j in range(0, len(chunks), 2)]
    return jnp.concatenate(split(jnp.concatenate(rows, axis=0)), axis=1)


def table_sixteen(chunks):
    return jnp.concatenate(split(jnp.concatenate(chunks, axis=0)), axis=1)


def onehot(columns):
    low = jnp.broadcast_to(columns & (LANES - 1), (LANES, columns.shape[1]))
    hot = (lax.broadcasted_iota(jnp.int32, low.shape, 0) == low).astype(F32).astype(BF16)
    return twice(hot)


def choose_four(picked, high):
    shape = (8, picked.shape[1])
    high = jnp.broadcast_to(high, shape) - upper_half(shape).astype(jnp.int32)
    total = jnp.zeros(shape, F32)
    for j in range(picked.shape[0] // 8):
        total = jnp.where(high == 2 * j, picked[8 * j : 8 * j + 8], total)
    return fold(total)


def choose_sixteen(picked, high):
    shape = (8, picked.shape[1])
    high = jnp.broadcast_to(high, shape)
    total = [jnp.zeros(shape, F32), jnp.zeros(shape, F32)]
    for j in range(picked.shape[0] // 16):
        here = high == j
        for half in range(2):
            at = 16 * j + 8 * half
            total[half] = jnp.where(here, picked[at : at + 8], total[half])
    return total


def matmul(left, right):
    return jnp.dot(left, right, preferred_element_type=F32)


def gather_four(table, columns):
    return choose_four(matmul(table, onehot(columns)), columns >> 7)


def gather_sixteen(table, columns):
    return jnp.concatenate(choose_sixteen(matmul(table, onehot(columns)), columns >> 7), axis=0)


def sum_components(value):
    first = value.astype(BF16)
    rest = value - first.astype(F32)
    second = rest.astype(BF16)
    third = (rest - second.astype(F32)).astype(BF16)
    row = lax.broadcasted_iota(jnp.int32, (8, 48), 0) & 3
    column = (lax.broadcasted_iota(jnp.int32, (8, 48), 1) >> 2) & 3
    ones = (row == column).astype(F32).astype(BF16)
    return matmul(ones, jnp.concatenate([first, second, third], axis=0))


def row_weights(operator_at):
    total = jnp.abs(operator_at(0))
    for k in range(1, 7):
        total = total + jnp.abs(operator_at(k))
    return 1.0 + sum_components(total)


def spread_row(value, row, rows=8):
    return jnp.broadcast_to(value[row : row + 1], (rows, value.shape[1]))


def lift(prolong, residual):
    low = pair_rows(spread_row(residual, 0), spread_row(residual, 1))
    high = pair_rows(spread_row(residual, 2), spread_row(residual, 3))
    return fold(prolong[:8] * low + prolong[8:] * high)


def expand(rows):
    return [
        [pair_rows(spread_row(rows, 4 * a + 2 * h), spread_row(rows, 4 * a + 2 * h + 1)) for h in (0, 1)]
        for a in range(4)
    ]


def triple_product(wide_prolong, operator, near):
    wide = expand(operator)
    out = [None, None]
    for a in range(4):
        inner = fold(wide[a][0] * near[0] + wide[a][1] * near[1])
        for half in range(2):
            term = wide_prolong[a][half] * inner
            out[half] = term if out[half] is None else out[half] + term
    return out


def scatter(values, targets, count):
    high, low = split(values)
    shape = (count, values.shape[1])
    hot = lax.broadcasted_iota(jnp.int32, shape, 0) == jnp.broadcast_to(targets, shape)
    hot = hot.astype(F32).astype(BF16)
    both = lax.dot_general(
        jnp.concatenate([high, low], axis=0),
        hot,
        (((1,), (1,)), ((), ())),
        preferred_element_type=F32,
    )
    rows = values.shape[0]
    return both[:rows] + both[rows:]


def chunks_of(value):
    return [value[:, at : at + LANES] for at in range(0, value.shape[1], LANES)]


def place():
    sub, slab = lax.axis_index("sub"), lax.axis_index("slab")
    return sub, slab


def neighbours(index, count, even, odd):
    is_even = index % 2 == 0
    if odd is None:
        odd = jnp.zeros_like(even)
    below = jnp.where(is_even, odd, even)
    above = jnp.where(is_even, even, odd)
    below = jnp.where(index > 0, below, jnp.zeros_like(below))
    above = jnp.where(index < count - 1, above, jnp.zeros_like(above))
    return below, above


def swap_halves(below, above, half):
    lane = lax.broadcasted_iota(jnp.int32, below.shape, 1)
    return pltpu.roll(jnp.where(lane < half, above, below), half, 1)


def call(body, outs, *args, scratch=()):
    return pl.pallas_call(
        body,
        out_shape=[jax.ShapeDtypeStruct(shape, F32) for shape in outs],
        in_specs=[pl.BlockSpec(memory_space=pltpu.VMEM)] * len(args),
        out_specs=[pl.BlockSpec(memory_space=pltpu.VMEM)] * len(outs),
        scratch_shapes=list(scratch),
        compiler_params=pltpu.CompilerParams(vmem_limit_bytes=48 * 1024 * 1024),
    )(*args)


TILE = 256


def tiles(count, body):
    def step(index, carry):
        body(pl.ds(pl.multiple_of(index * TILE, TILE), TILE))
        return carry

    lax.fori_loop(0, count // TILE, step, 0)


def fine_first(
    source, operator, prolong, sends, prolong_one, sends_one, w_ref, first_ref, *rest
):
    picks = rest[-1]
    parity_out, cross_out, slab_outs = rest[0], rest[1], rest[2:-1]
    weights = row_weights(lambda k: operator[16 * k : 16 * k + 16])
    first = twice(source[...]) / weights
    w_ref[...] = weights
    first_ref[...] = first
    table = jnp.concatenate(
        [table_four(chunks_of(first)), table_sixteen(chunks_of(prolong[...]))], axis=0
    )
    split_at = first.shape[1] // LANES * 4

    def pick(at):
        columns = sends[:, at]
        picked = matmul(table, onehot(columns))
        picks[0:8, at] = choose_four(picked[:split_at], columns >> 7)
        low, high = choose_sixteen(picked[split_at:], columns >> 7)
        picks[8:16, at] = low
        picks[16:24, at] = high

    tiles(sends.shape[1], pick)
    coarse = gather_sixteen(table_sixteen(chunks_of(prolong_one[...])), sends_one[...])
    sub, slab = place()
    count = sends.shape[1] // 4
    low_first, high_first = picks[:, 0:count], picks[:, count : 2 * count]
    low_second, high_second = picks[:, 2 * count : 3 * count], picks[:, 3 * count :]
    even = sub % 2 == 0
    parity_out[...] = jnp.where(even, high_second, low_second)
    cross_out[:, 0:count] = jnp.where(even, low_second, high_second)
    cross_out[0:16, count:] = coarse[:, 2 * LANES :]
    cross_out[16:24, count:] = jnp.zeros((8, LANES), F32)
    slab_even = slab % 2 == 0
    for position, out in enumerate(slab_outs):
        up = slab_even if position == 0 else jnp.logical_not(slab_even)
        out[:, 0:count] = jnp.where(up, high_first, low_first)
        out[0:16, count:] = jnp.where(up, coarse[:, LANES : 2 * LANES], coarse[:, 0:LANES])
        out[16:24, count:] = jnp.zeros((8, LANES), F32)


def fine_ghosts(rows, count, sizes, parity_in, cross_in, slab_ins):
    sub, slab = place()
    at = slice(0, count)
    slab_values = [ref[rows, at] for ref in slab_ins] + [None]
    below, above = neighbours(slab, sizes[1], slab_values[0], slab_values[1])
    left, right = neighbours(sub, sizes[0], parity_in[rows, at], cross_in[rows, at])
    return chunks_of(below) + chunks_of(above) + chunks_of(left) + chunks_of(right)


def apply_tile(table, operator, columns, at):
    total = None
    for k in range(7):
        near = twice(gather_four(table, columns[k : k + 1, at]))
        term = operator[16 * k : 16 * k + 16, at] * near
        total = term if total is None else total + term
    return sum_components(total)


def fine_second(
    sizes, source, operator, columns, sends, w_ref, first_ref, parity_in, cross_in, *rest
):
    slab_count = (len(rest) - 5) // 2
    slab_ins, rest = rest[:slab_count], rest[slab_count:]
    smoothed, parity_out, cross_out = rest[0], rest[1], rest[2]
    slab_outs, second_ref, picks = rest[3:-2], rest[-2], rest[-1]
    count = sends.shape[1] // 4
    ghosts = fine_ghosts(slice(0, 8), count, sizes, parity_in, cross_in, slab_ins)
    table = table_four(chunks_of(first_ref[...]) + ghosts)

    def step(at):
        residual = twice(source[:, at]) - apply_tile(table, operator, columns, at)
        second_ref[:, at] = first_ref[:, at] + residual / w_ref[:, at]

    tiles(source.shape[1], step)
    smoothed[...] = second_ref[0:4]
    table = table_four(chunks_of(second_ref[...]))

    def pick(at):
        picks[:, at] = gather_four(table, sends[:, at])

    tiles(sends.shape[1], pick)
    sub, slab = place()
    low_first, high_first = picks[:, 0:count], picks[:, count : 2 * count]
    low_second, high_second = picks[:, 2 * count : 3 * count], picks[:, 3 * count :]
    even = sub % 2 == 0
    parity_out[:, 0:count] = jnp.where(even, high_second, low_second)
    parity_out[:, count : count + LANES] = cross_in[0:8, count:]
    parity_out[:, count + LANES :] = cross_in[8:16, count:]
    cross_out[...] = jnp.where(even, low_second, high_second)
    slab_even = slab % 2 == 0
    for position, out in enumerate(slab_outs):
        up = slab_even if position == 0 else jnp.logical_not(slab_even)
        out[...] = jnp.where(up, high_first, low_first)


def coarsen(table, operator, prolong, columns, slots, aggregates, sums, count):
    def step(at):
        wide_prolong = expand(prolong[:, at])
        totals = [[jnp.zeros((8, TILE), F32) for _ in range(2)] for _ in range(7)]
        for k in range(7):
            column = columns[k : k + 1, at]
            near = choose_sixteen(matmul(table, onehot(column)), column >> 7)
            blocks = triple_product(wide_prolong, operator[16 * k : 16 * k + 16, at], near)
            slot = jnp.broadcast_to(slots[k : k + 1, at], (8, TILE))
            for s in range(7):
                here = slot == s
                for half in range(2):
                    totals[s][half] = totals[s][half] + jnp.where(here, blocks[half], 0.0)
        for s in range(7):
            for half in range(2):
                row = 16 * s + 8 * half
                sums[row : row + 8, at] = totals[s][half]

    tiles(columns.shape[1], step)
    return scatter(sums[...], aggregates[...], count)


def fine_coarsen(
    sizes,
    source,
    operator,
    prolong,
    columns,
    slots,
    aggregates,
    second_ref,
    parity_old,
    cross_old,
    parity_in,
    cross_in,
    *rest,
):
    slab_count = (len(rest) - 3) // 2
    slab_old, slab_ins, rest = rest[:slab_count], rest[slab_count : 2 * slab_count], rest[-3:]
    out, sums, lifted = rest
    count = parity_old.shape[1]
    ghosts = fine_ghosts(slice(0, 8), count, sizes, parity_in, cross_in, slab_ins)
    table = table_four(chunks_of(second_ref[...]) + ghosts)

    def step(at):
        residual = twice(source[:, at]) - apply_tile(table, operator, columns, at)
        lifted[:, at] = lift(prolong[:, at], residual)

    tiles(source.shape[1], step)
    rows = out.shape[1]
    out[112:120] = scatter(lifted[...], aggregates[...], rows)
    ghosts = fine_ghosts(slice(8, 24), count, sizes, parity_old, cross_old, slab_old)
    table = table_sixteen(chunks_of(prolong[...]) + ghosts)
    out[0:112] = coarsen(table, operator, prolong, columns, slots, aggregates, sums, rows)


def slab_faces(picks, slab, slab_outs):
    slab_even = slab % 2 == 0
    for position, out in enumerate(slab_outs):
        up = slab_even if position == 0 else jnp.logical_not(slab_even)
        out[...] = jnp.where(up, picks[:, LANES : 2 * LANES], picks[:, 0:LANES])


def pair_first(own, other, sends, operator, source, weights, first, group_out, *slab_outs):
    sub, slab = place()
    even = sub % 2 == 0
    half = own.shape[1]
    lower = jnp.where(even, own[...], other[...])
    upper = jnp.where(even, other[...], own[...])
    operator[:, 0:half] = lower[0:112]
    operator[:, half:] = upper[0:112]
    source[:, 0:half] = lower[112:120]
    source[:, half:] = upper[112:120]
    weights[...] = row_weights(lambda k: operator[16 * k : 16 * k + 16])
    first[...] = source[...] / weights[...]
    picks = gather_four(table_four(chunks_of(first[...])), sends[...])
    group_out[...] = picks[:, 2 * LANES :]
    slab_faces(picks, slab, slab_outs)


def pair_ghosts(sizes, even_in, odd_in, slab_ins):
    sub, slab = place()
    values = [ref[...] for ref in slab_ins] + [None]
    below, above = neighbours(slab, sizes[1], values[0], values[1])
    left, right = neighbours(sub // 2, sizes[0] // 2, even_in[...], odd_in[...])
    return [below, above, swap_halves(left, right, LANES // 2)]


def pair_second(
    sizes, operator, source, weights, first, columns, sends, even_in, odd_in, *rest
):
    slab_count = (len(rest) - 3) // 2
    slab_ins, rest = rest[:slab_count], rest[slab_count:]
    smoothed, second_ref, group_out = rest[0], rest[1], rest[2]
    slab_outs = rest[3:]
    table = table_four(chunks_of(first[...]) + pair_ghosts(sizes, even_in, odd_in, slab_ins))

    def step(at):
        residual = source[:, at] - apply_tile(table, operator, columns, at)
        second_ref[:, at] = first[:, at] + residual / weights[:, at]

    tiles(source.shape[1], step)
    sub, slab = place()
    half = smoothed.shape[1]
    smoothed[...] = jnp.where(sub % 2 == 0, second_ref[0:4, 0:half], second_ref[0:4, half:])
    picks = gather_four(table_four(chunks_of(second_ref[...])), sends[...])
    group_out[...] = picks[:, 2 * LANES :]
    slab_faces(picks, slab, slab_outs)


def pair_coarsen(
    sizes,
    operator,
    source,
    second_ref,
    prolong,
    columns,
    slots,
    aggregates,
    sends,
    parity_old,
    cross_old,
    forwarded,
    even_in,
    odd_in,
    *rest,
):
    slab_count = (len(rest) - 6) // 2
    slab_old, slab_ins, rest = rest[:slab_count], rest[slab_count : 2 * slab_count], rest[-6:]
    message, operator_two, source_two, first_two, sums, lifted = rest
    sub, slab = place()
    even = sub % 2 == 0
    table = table_four(chunks_of(second_ref[...]) + pair_ghosts(sizes, even_in, odd_in, slab_ins))

    def step(at):
        residual = source[:, at] - apply_tile(table, operator, columns, at)
        lifted[:, at] = lift(prolong[:, at], residual)

    tiles(source.shape[1], step)
    source_two[...] = scatter(lifted[...], aggregates[...], LANES)

    count = parity_old.shape[1]
    values = [ref[0:16, count:] for ref in slab_old] + [None]
    below, above = neighbours(slab, sizes[1], values[0], values[1])
    mine = cross_old[0:16, count:]
    partners = jnp.concatenate(
        [forwarded[:, count : count + LANES], forwarded[:, count + LANES :]], axis=0
    )
    group = sub // 2
    left = jnp.where(even, mine, partners)
    right = jnp.where(even, partners, mine)
    left = jnp.where(group > 0, left, jnp.zeros_like(left))
    right = jnp.where(group < sizes[0] // 2 - 1, right, jnp.zeros_like(right))
    ghosts = [below, above, swap_halves(left, right, LANES // 2)]
    table = table_sixteen(chunks_of(prolong[...]) + ghosts)
    operator_two[...] = coarsen(
        table, operator, prolong, columns, slots, aggregates, sums, LANES
    )
    first = source_two[...] / row_weights(lambda k: operator_two[16 * k : 16 * k + 16])
    first_two[...] = first
    lane = lax.broadcasted_iota(jnp.int32, first.shape, 1)
    first = jnp.where(lane < LANES // 2, first, 0.0)
    placed = jnp.where(group % 2 == 0, first, pltpu.roll(first, LANES // 2, 1))
    picks = gather_four(table_four([placed]), sends[...])
    faces = picks[:, 0:LANES]
    seconds = pltpu.roll(picks[:, LANES:], LANES // 2, 1)
    sent = pair_rows(jnp.where(lane < LANES // 2, first, seconds), faces)
    message[...] = jnp.broadcast_to(sent[None], message.shape)


def group_second(sizes, operator, source, first_two, columns, received, out):
    sub, slab = place()
    subs, slabs = sizes
    group, pair = sub // 4, sub // 2 % 2
    shape = (8, LANES)
    lane = lax.broadcasted_iota(jnp.int32, shape, 1)
    half = LANES // 2

    def from_pair(group_at, pair_at, slab_at):
        valid = (group_at >= 0) & (group_at < subs // 4) & (slab_at >= 0) & (slab_at < slabs)
        index = (group_at * 4 + pair_at * 2 + sub % 2) * slabs + slab_at
        index = jnp.where(valid, index, 0)
        return jnp.where(valid, received[index], jnp.zeros(shape, F32))

    def from_group(group_at, slab_at):
        return from_pair(group_at, 0, slab_at) + from_pair(group_at, 1, slab_at)

    def lower(value):
        return pair_rows(value, pltpu.roll(value, 4, 0))

    def upper(value):
        return pair_rows(pltpu.roll(value, 4, 0), value)

    pairs = [lower(from_pair(group, j, slab)) for j in range(2)]
    first = jnp.where(lane < half, pairs[0], pltpu.roll(pairs[1], half, 1))
    firsts = swap_halves(
        upper(from_group(group, slab - 1)), upper(from_group(group, slab + 1)), half
    )
    width = GX // 4 * (GZ // 4)
    left = lower(from_group(group - 1, slab))
    right = lower(from_group(group + 1, slab))
    seconds = jnp.where(
        lane < width,
        pltpu.roll(left, LANES - half - width, 1),
        pltpu.roll(right, LANES - half + width, 1),
    )
    seconds = jnp.where(lane < 2 * width, seconds, 0.0)
    table = table_four([first, firsts, seconds])
    mine = jnp.where(pair == 0, columns[...], pltpu.roll(columns[...], half, 1))
    total = None
    for k in range(7):
        near = twice(gather_four(table, mine[k : k + 1]))
        term = operator[16 * k : 16 * k + 16] * near
        total = term if total is None else total + term
    residual = source[...] - sum_components(total)
    weights = row_weights(lambda k: operator[16 * k : 16 * k + 16])
    second = first_two[...] + residual / weights
    share = out.shape[1]
    out[...] = jnp.where(sub % 2 == 0, second[0:4, 0:share], second[0:4, share : 2 * share])


def pairing(value, axis, group, odd):
    count = lax.axis_size(axis)
    blocks = count // group
    route = []
    for index in range(count):
        block = index // group
        mate = ((block - 1) ^ 1) + 1 if odd else block ^ 1
        route.append((index, mate % blocks * group + index % group))
    return lax.ppermute(value, axis, route)


def slab_pairings(values):
    return [pairing(value, "slab", 1, position == 1) for position, value in enumerate(values)]


def on_device(
    source,
    operator,
    prolong,
    columns,
    slots,
    aggregates,
    sends,
    prolong_one,
    columns_one,
    slots_one,
    aggregates_one,
    sends_one,
    columns_two,
    sends_two,
):
    sizes = (lax.axis_size("sub"), lax.axis_size("slab"))
    slab_moves = 1 if sizes[1] == 2 else 2
    rows = source.shape[1]
    rows_one = rows // 8
    pair_rows_one = 2 * rows_one
    count = 2 * GY * GZ
    operator = operator.reshape(112, rows)
    prolong = prolong.reshape(16, rows)
    prolong_one = prolong_one.reshape(16, pair_rows_one)
    sends = sends.reshape(1, -1)
    sends_one = sends_one.reshape(1, -1)
    aggregates = aggregates.reshape(1, -1)
    aggregates_one = aggregates_one.reshape(1, -1)
    sends_two = jnp.pad(sends_two, (0, -sends_two.shape[0] % LANES)).reshape(1, -1)

    weights, first, even, odd, *slabs = call(
        fine_first,
        [(8, rows), (8, rows), (24, count), (24, count + LANES)]
        + [(24, count + LANES)] * slab_moves,
        source,
        operator,
        prolong,
        sends,
        prolong_one,
        sends_one,
        scratch=[pltpu.VMEM((24, sends.shape[1]), F32)],
    )
    even_old = pairing(even, "sub", 1, False)
    odd_old = pairing(odd, "sub", 1, True)
    slabs_old = slab_pairings(slabs)

    smoothed, even, odd, *rest = call(
        functools.partial(fine_second, sizes),
        [(4, rows), (8, count + 2 * LANES), (8, count)]
        + [(8, count)] * slab_moves
        + [(8, rows)],
        source,
        operator,
        columns,
        sends,
        weights,
        first,
        even_old,
        odd_old,
        *slabs_old,
        scratch=[pltpu.VMEM((8, sends.shape[1]), F32)],
    )
    slabs, second = rest[:-1], rest[-1]
    forwarded = pairing(even, "sub", 1, False)
    odd_in = pairing(odd, "sub", 1, True)
    slabs_in = slab_pairings(slabs)

    (own,) = call(
        functools.partial(fine_coarsen, sizes),
        [(120, rows_one)],
        source,
        operator,
        prolong,
        columns,
        slots,
        aggregates,
        second,
        even_old,
        odd_old,
        forwarded,
        odd_in,
        *slabs_old,
        *slabs_in,
        scratch=[pltpu.VMEM((112, rows), F32), pltpu.VMEM((8, rows), F32)],
    )
    other = pairing(own, "sub", 1, False)

    faces = [(8, LANES)] * (1 + slab_moves)
    operator_one, source_one, weights_one, first_one, group_out, *slabs = call(
        pair_first,
        [(112, pair_rows_one)] + [(8, pair_rows_one)] * 3 + faces,
        own,
        other,
        sends_one,
    )
    even_in = pairing(group_out, "sub", 2, False)
    odd_in = pairing(group_out, "sub", 2, True)
    slabs_in = slab_pairings(slabs)

    smoothed_one, second_one, group_out, *slabs = call(
        functools.partial(pair_second, sizes),
        [(4, rows_one), (8, pair_rows_one)] + faces,
        operator_one,
        source_one,
        weights_one,
        first_one,
        columns_one,
        sends_one,
        even_in,
        odd_in,
        *slabs_in,
    )
    even_in = pairing(group_out, "sub", 2, False)
    odd_in = pairing(group_out, "sub", 2, True)
    slabs_in = slab_pairings(slabs)

    message, operator_two, source_two, first_two = call(
        functools.partial(pair_coarsen, sizes),
        [(sizes[0] * sizes[1], 8, LANES), (112, LANES), (8, LANES), (8, LANES)],
        operator_one,
        source_one,
        second_one,
        prolong_one,
        columns_one,
        slots_one,
        aggregates_one,
        sends_two,
        even_old,
        odd_old,
        forwarded,
        even_in,
        odd_in,
        *slabs_old,
        *slabs_in,
        scratch=[pltpu.VMEM((112, pair_rows_one), F32), pltpu.VMEM((8, pair_rows_one), F32)],
    )
    received = lax.all_to_all(message, ("sub", "slab"), 0, 0)

    (smoothed_two,) = call(
        functools.partial(group_second, sizes),
        [(4, rows_one // 8)],
        operator_two,
        source_two,
        first_two,
        columns_two,
        received,
    )
    return (smoothed, smoothed_one, smoothed_two)


def solution(mesh):
    placed = (
        P(None, ("sub", "slab")),
        P(None, None, None, ("sub", "slab")),
        P(None, None, ("sub", "slab")),
        P(None, ("sub", "slab")),
        P(None, ("sub", "slab")),
        P(("sub", "slab")),
        P(("sub", "slab")),
        P(None, None, ("sub", "slab")),
        P(None, ("sub", "slab")),
        P(None, ("sub", "slab")),
        P(("sub", "slab")),
        P(("sub", "slab")),
        P(None, ("sub", "slab")),
        P(("sub", "slab")),
    )
    return jax.shard_map(
        on_device,
        mesh=mesh,
        in_specs=placed,
        out_specs=(P(None, ("sub", "slab")), P(None, ("sub", "slab")), P(None, ("sub", "slab"))),
        check_vma=False,
    )
```

time: 565 us -> 71.5 us (0.13)
  local copies, waits for them, and re-layouts: 337 us -> 4.44 us
  other arithmetic: 123 us -> 0 us
  starting transfers between devices: 81.6 us -> 18.3 us
  Pallas kernels: 0 us -> 24.3 us
  blocking collectives: 0 us -> 11.9 us
  waiting for transfers between devices: 19 us -> 11.6 us
    gather x26 -> x0, local copies, waits for them, and re-layouts: 286 us -> none  [the longest x4 143 us: galerkin_rows(): nearby = extended[:, :, columns]]
    scatter-add x4 -> x0, other arithmetic: 111 us -> none  [the longest x2 96.8 us: galerkin_rows(): jnp.zeros((16, 7 * coarse), blocks.dtype).at[:, target]]
    ppermute x32 -> x13, starting transfers between devices: 81.6 us -> 18.3 us  [pairing(): return lax.ppermute(value, axis, route)]
    pallas_call x0 -> x7, Pallas kernels: none -> 24.3 us  [call(): pl.pallas_call(body, out_shape=[jax.ShapeDtypeStruct(shape, F32) for shap...]
    all_to_all x0 -> x1, blocking collectives: none -> 11.9 us  [on_device(): received = lax.all_to_all(message, ('sub', 'slab'), 0, 0)]
    concatenate x18 -> x0, local copies, waits for them, and re-layouts: 11 us -> none  [extend(): return jnp.concatenate([values] + parts, axis=1)]
    transpose x10 -> x0, local copies, waits for them, and re-layouts: 8.55 us -> none  [galerkin_rows(): jnp.transpose(operator[:, :, comp, :], (1, 0, 2))[:, None, :, :]]
    ppermute x8 -> x0, local copies, waits for them, and re-layouts: 7.59 us -> none  [from_behind(): lax.ppermute(value, axis, [(source, source + steps) for source in range(i...]
  transfers between devices with their start and end apart: 32 -> 13, of which waited for: 7 -> 6; matrix products, arithmetic and copies ran while one was open for 40% -> 0% of each run, Pallas kernels for 0% -> 0%
where the time goes in v1:
time: 71.5 us; the launch traced here: 71.2 us
  Pallas kernels  24.3 us (34%)
  starting transfers between devices  18.3 us (26%)
  blocking collectives  11.9 us (17%)
  waiting for transfers between devices  11.6 us (16%)
  local copies, waits for them, and re-layouts  4.44 us (6%)
  between operations  0.75 us (1%)
    pallas_call x7, Pallas kernels, call(): pl.pallas_call(body, out_shape=[jax.ShapeDtypeStruct(shape, F32) for shap...  24.3 us
    ppermute x13, starting transfers between devices, pairing(): return lax.ppermute(value, axis, route)  18.3 us
    all_to_all x1, blocking collectives, on_device(): received = lax.all_to_all(message, ('sub', 'slab'), 0, 0)  11.9 us
    ppermute x13, waiting for transfers between devices, pairing(): return lax.ppermute(value, axis, route)  11.6 us
    unnamed x26, local copies, waits for them, and re-layouts  2.84 us
    reshape x1, local copies, waits for them, and re-layouts, on_device(): operator = operator.reshape(112, rows)  1.53 us
  transfers between devices with their start and end apart: 13, of which 6 were waited for; matrix products, arithmetic and copies ran while one was open for 0% of the time, Pallas kernels for 0%

profile of v1, /device:TPU:0, one launch (start us, length us, event | category | flops | bytes accessed | tf_op | source)
XLA Modules:
  0.0 71.2 jit_solution(4038256207885498402)
XLA Ops:
  0.6 0.0 copy-start.11
  0.6 0.0 copy-start.9
  0.7 1.5 %reshape.30.operator = f32[112,2048]{1,0:T(8,128)S(1)} reshape(f32[7,4,4,2048]{3,2,1,0:T(4,128)} %param.15) | data formatting | bytes 1835008 | tf_op jit(solution)/shard_map/reshape | solution.py:551
  2.2 0.0 copy-done.11
  2.2 0.0 copy-done.9
  2.2 0.0 copy-start.10
  2.3 0.7 copy-done.10
  3.0 0.7 %copy-done = f32[4,2048]{1,0:T(4,128)S(1)} copy-done((f32[4,2048]{1,0:T(4,128)S(1)}, f32[4,2048]{1,0:T(4,128)}, u32[]{:S(2)}) %copy-start) | copy-done | bytes 32792
  3.7 0.0 copy-done.4
  3.7 2.1 %shard_map.157 = (f32[8,2048]{1,0:T(8,128)S(1)}, f32[8,2048]{1,0:T(8,128)S(1)}, f32[24,512]{1,0:T(8,128)S(1)}, f32[24,640]{1,0:T(8,128)S(1)}, f32[24,640]{1,0:T(8,128)S(1)}) custom-call(f32[4,2048]{1,0:T(4,128)S(1)} %copy-done, f32[112,2048]{1,0:T(8,128)S(1)} %reshape.30.operator, f32[16,2048]{1,0:T(8,128)S(1)} %reshape.32.prolong, s32[1,2048]{1,0:T(1,128)S(1)} %bitcast.4, ...), custom_call_target="tpu_custom_call" | custom-call | tf_op jit(solution)/shard_map/pallas_call | solution.py:176
  5.8 5.5 %collective-permute-start.1 = (f32[24,640]{1,0:T(8,128)S(1)}, f32[24,640]{1,0:T(8,128)S(1)}, u32[]{:S(2)}, u32[]{:S(2)}) collective-permute-start(f32[24,640]{1,0:T(8,128)S(1)} %get-tuple-element.30), channel_id=1, source_target_pairs={{0,30},{2,4},{4,2},{6,8},{8,6},{10,12},{12,10},{14,16},{16,14},{18... | collective-permute-start | bytes 184328 | tf_op jit(solution)/shard_map/ppermute | solution.py:522
  11.3 1.5 %collective-permute-start.2 = (f32[24,640]{1,0:T(8,128)S(1)}, f32[24,640]{1,0:T(8,128)S(1)}, u32[]{:S(2)}, u32[]{:S(2)}) collective-permute-start(f32[24,640]{1,0:T(8,128)S(1)} %get-tuple-element.31), channel_id=1, source_target_pairs={{0,1},{1,0},{2,3},{3,2},{4,5},{5,4},{6,7},{7,6},{8,9},{9,8},{10,11... | collective-permute-start | bytes 184328 | tf_op jit(solution)/shard_map/ppermute | solution.py:522
  12.8 0.0 collective-permute-start
  12.8 1.2 %collective-permute-done.parity_in.parity_old = f32[24,512]{1,0:T(8,128)S(1)} collective-permute-done((f32[24,512]{1,0:T(8,128)S(1)}, f32[24,512]{1,0:T(8,128)S(1)}, u32[]{:S(2)}, u32[]{:S(2)}) %collective-permute-start) | collective-permute-done | bytes 49184 | tf_op jit(solution)/shard_map/ppermute | solution.py:522
  14.0 0.0 collective-permute-done.1.cross_in.cross_old
  14.0 1.5 %collective-permute-done.2.rest_0_ = f32[24,640]{1,0:T(8,128)S(1)} collective-permute-done((f32[24,640]{1,0:T(8,128)S(1)}, f32[24,640]{1,0:T(8,128)S(1)}, u32[]{:S(2)}, u32[]{:S(2)}) %collective-permute-start.2) | collective-permute-done | bytes 61472 | tf_op jit(solution)/shard_map/ppermute | solution.py:522
  15.5 0.0 copy-done.1
  15.5 5.5 %shard_map.158 = (f32[4,2048]{1,0:T(4,128)}, f32[8,768]{1,0:T(8,128)S(1)}, f32[8,512]{1,0:T(8,128)S(1)}, f32[8,512]{1,0:T(8,128)S(1)}, f32[8,2048]{1,0:T(8,128)S(1)}) custom-call(f32[4,2048]{1,0:T(4,128)S(1)} %copy-done, f32[112,2048]{1,0:T(8,128)S(1)} %reshape.30.operator, s32[7,2048]{1,0:T(8,128)S(1)} %copy-done.1, s32[1,2048]{1,0:T(1,128)S(1)} %bitcast.5, ...), custom_call_target="tpu_custom_call" | custom-call | tf_op jit(solution)/shard_map/pallas_call | solution.py:176
  21.1 0.0 collective-permute-start.3
  21.1 2.1 %collective-permute-start.4 = (f32[8,512]{1,0:T(8,128)S(1)}, f32[8,512]{1,0:T(8,128)S(1)}, u32[]{:S(2)}, u32[]{:S(2)}) collective-permute-start(f32[8,512]{1,0:T(8,128)S(1)} %get-tuple-element.35), channel_id=1, source_target_pairs={{0,30},{2,4},{4,2},{6,8},{8,6},{10,12},{12,10},{14,16},{16,14},{18... | collective-permute-start | bytes 49160 | tf_op jit(solution)/shard_map/ppermute | solution.py:522
  23.2 1.5 %collective-permute-start.5 = (f32[8,512]{1,0:T(8,128)S(1)}, f32[8,512]{1,0:T(8,128)S(1)}, u32[]{:S(2)}, u32[]{:S(2)}) collective-permute-start(f32[8,512]{1,0:T(8,128)S(1)} %get-tuple-element.36), channel_id=1, source_target_pairs={{0,1},{1,0},{2,3},{3,2},{4,5},{5,4},{6,7},{7,6},{8,9},{9,8},{10,11... | collective-permute-start | bytes 49160 | tf_op jit(solution)/shard_map/ppermute | solution.py:522
  24.7 2.2 %collective-permute-done.4.cross_in = f32[8,512]{1,0:T(8,128)S(1)} collective-permute-done((f32[8,512]{1,0:T(8,128)S(1)}, f32[8,512]{1,0:T(8,128)S(1)}, u32[]{:S(2)}, u32[]{:S(2)}) %collective-permute-start.4) | collective-permute-done | bytes 16416 | tf_op jit(solution)/shard_map/ppermute | solution.py:522
  27.0 0.0 collective-permute-done.5.rest_1_
  27.0 0.0 collective-permute-done.3.parity_in.forwarded
  27.0 11.0 %shard_map.159.own = f32[120,256]{1,0:T(8,128)S(1)} custom-call(f32[4,2048]{1,0:T(4,128)S(1)} %copy-done, f32[112,2048]{1,0:T(8,128)S(1)} %reshape.30.operator, f32[16,2048]{1,0:T(8,128)S(1)} %reshape.32.prolong, s32[7,2048]{1,0:T(8,128)S(1)} %copy-done.1, s32[7,2048]{1,0:T(8,128)S(1)} %copy-done.2, s32[1,2048]{1,0:T(1,128)S(1)} %bitcast.6, ...), custom_call_target="tpu_custom_call" | custom-call | tf_op jit(solution)/shard_map/pallas_call | solution.py:176
  38.0 0.1 collective-permute-start.6
  38.1 1.3 %collective-permute-done.6.other = f32[120,256]{1,0:T(8,128)S(1)} collective-permute-done((f32[120,256]{1,0:T(8,128)S(1)}, f32[120,256]{1,0:T(8,128)S(1)}, u32[]{:S(2)}, u32[]{:S(2)}) %collective-permute-start.6) | collective-permute-done | bytes 122912 | tf_op jit(solution)/shard_map/ppermute | solution.py:522
  39.4 0.3 shard_map.160
  39.7 0.0 collective-permute-start.7
  39.7 2.2 %collective-permute-start.8 = (f32[8,128]{1,0:T(8,128)S(1)}, f32[8,128]{1,0:T(8,128)S(1)}, u32[]{:S(2)}, u32[]{:S(2)}) collective-permute-start(f32[8,128]{1,0:T(8,128)S(1)} %get-tuple-element.41), channel_id=1, source_target_pairs={{0,28},{2,30},{4,8},{6,10},{8,4},{10,6},{12,16},{14,18},{16,12},{1... | collective-permute-start | bytes 12296 | tf_op jit(solution)/shard_map/ppermute | solution.py:522
  42.0 1.5 %collective-permute-start.9 = (f32[8,128]{1,0:T(8,128)S(1)}, f32[8,128]{1,0:T(8,128)S(1)}, u32[]{:S(2)}, u32[]{:S(2)}) collective-permute-start(f32[8,128]{1,0:T(8,128)S(1)} %get-tuple-element.42), channel_id=1, source_target_pairs={{0,1},{1,0},{2,3},{3,2},{4,5},{5,4},{6,7},{7,6},{8,9},{9,8},{10,11... | collective-permute-start | bytes 12296 | tf_op jit(solution)/shard_map/ppermute | solution.py:522
  43.4 0.0 collective-permute-done.7.even_in
  43.4 2.6 %collective-permute-done.8.odd_in = f32[8,128]{1,0:T(8,128)S(1)} collective-permute-done((f32[8,128]{1,0:T(8,128)S(1)}, f32[8,128]{1,0:T(8,128)S(1)}, u32[]{:S(2)}, u32[]{:S(2)}) %collective-permute-start.8) | collective-permute-done | bytes 4128 | tf_op jit(solution)/shard_map/ppermute | solution.py:522
  46.1 0.0 collective-permute-done.9.rest_0_
  46.1 0.0 copy-done.3
  46.1 1.6 %shard_map.161 = (f32[4,256]{1,0:T(4,128)}, f32[8,512]{1,0:T(8,128)S(1)}, f32[8,128]{1,0:T(8,128)S(1)}, f32[8,128]{1,0:T(8,128)S(1)}) custom-call(f32[112,512]{1,0:T(8,128)S(1)} %get-tuple-element.37.operator, f32[8,512]{1,0:T(8,128)S(1)} %get-tuple-element.38.source, f32[8,512]{1,0:T(8,128)S(1)} %get-tuple-element.39.weights, ...), custom_call_target="tpu_custom_call" | custom-call | tf_op jit(solution)/shard_map/pallas_call | solution.py:176
  47.7 0.2 collective-permute-start.10
  47.9 2.2 %collective-permute-start.11 = (f32[8,128]{1,0:T(8,128)S(1)}, f32[8,128]{1,0:T(8,128)S(1)}, u32[]{:S(2)}, u32[]{:S(2)}) collective-permute-start(f32[8,128]{1,0:T(8,128)S(1)} %get-tuple-element.45), channel_id=1, source_target_pairs={{0,28},{2,30},{4,8},{6,10},{8,4},{10,6},{12,16},{14,18},{16,12},{1... | collective-permute-start | bytes 12296 | tf_op jit(solution)/shard_map/ppermute | solution.py:522
  50.1 1.5 %collective-permute-start.12 = (f32[8,128]{1,0:T(8,128)S(1)}, f32[8,128]{1,0:T(8,128)S(1)}, u32[]{:S(2)}, u32[]{:S(2)}) collective-permute-start(f32[8,128]{1,0:T(8,128)S(1)} %get-tuple-element.46), channel_id=1, source_target_pairs={{0,1},{1,0},{2,3},{3,2},{4,5},{5,4},{6,7},{7,6},{8,9},{9,8},{10,11... | collective-permute-start | bytes 12296 | tf_op jit(solution)/shard_map/ppermute | solution.py:522
  51.6 0.0 collective-permute-done.10.even_in
  51.6 2.6 %collective-permute-done.11.odd_in = f32[8,128]{1,0:T(8,128)S(1)} collective-permute-done((f32[8,128]{1,0:T(8,128)S(1)}, f32[8,128]{1,0:T(8,128)S(1)}, u32[]{:S(2)}, u32[]{:S(2)}) %collective-permute-start.11) | collective-permute-done | bytes 4128 | tf_op jit(solution)/shard_map/ppermute | solution.py:522
  54.2 0.0 collective-permute-done.12.rest_1_
  54.2 0.0 copy-done.5
  54.2 0.7 copy-done.8
  54.9 2.6 %shard_map.162 = (f32[32,8,128]{2,1,0:T(8,128)S(1)}, f32[112,128]{1,0:T(8,128)S(1)}, f32[8,128]{1,0:T(8,128)S(1)}, f32[8,128]{1,0:T(8,128)S(1)}) custom-call(f32[112,512]{1,0:T(8,128)S(1)} %get-tuple-element.37.operator, f32[8,512]{1,0:T(8,128)S(1)} %get-tuple-element.38.source, f32[8,512]{1,0:T(8,128)S(1)} %get-tuple-element.44.second_ref, ...), custom_call_target="tpu_custom_call" | custom-call | tf_op jit(solution)/shard_map/pallas_call | solution.py:176
  57.5 11.9 %all_to_all.5.received = f32[32,8,128]{2,1,0:T(8,128)S(1)} all-to-all(f32[32,8,128]{2,1,0:T(8,128)S(1)} %get-tuple-element.50), channel_id=1, replica_groups=mesh['sub'=16,'slab'=2] {'sub','slab'}, dimensions={0} | all-to-all | bytes 262144 | tf_op jit(solution)/shard_map/all_to_all | solution.py:666
  69.4 0.7 copy-done.7
  70.1 1.1 %shard_map.163 = f32[4,32]{1,0:T(4,128)} custom-call(f32[112,128]{1,0:T(8,128)S(1)} %get-tuple-element.47.operator, f32[8,128]{1,0:T(8,128)S(1)} %get-tuple-element.48.source, f32[8,128]{1,0:T(8,128)S(1)} %get-tuple-element.49.first_two, s32[7,128]{1,0:T(8,128)S(1)} %copy-done.7, f32[32,8,128]{2,1,0:T(8,128)S(1)} %all_to_all.5.received), custom_call_target="tpu_custom_call" | custom-call | tf_op jit(solution)/shard_map/pallas_call | solution.py:176
  (17 shorter events, 0.1 us)
Async XLA Ops:
  0.6 1.6 %copy-start.11 = (s32[384]{0:T(512)S(1)}, s32[384]{0:T(512)}, u32[]{:S(2)}) copy-start(s32[384]{0:T(512)} %param.25) | copy-start | bytes 4612
  0.6 1.6 %copy-start.9 = (f32[4,4,2048]{2,1,0:T(4,128)S(1)}, f32[4,4,2048]{2,1,0:T(4,128)}, u32[]{:S(2)}) copy-start(f32[4,4,2048]{2,1,0:T(4,128)} %param.16) | copy-start | bytes 393220
  2.2 0.8 %copy-start.10 = (f32[4,4,512]{2,1,0:T(4,128)S(1)}, f32[4,4,512]{2,1,0:T(4,128)}, u32[]{:S(2)}) copy-start(f32[4,4,512]{2,1,0:T(4,128)} %param.21) | copy-start | bytes 98308
  3.0 0.8 %copy-start = (f32[4,2048]{1,0:T(4,128)S(1)}, f32[4,2048]{1,0:T(4,128)}, u32[]{:S(2)}) copy-start(f32[4,2048]{1,0:T(4,128)} %source.5) | copy-start | bytes 98308
  3.0 0.8 %copy-start.4 = (s32[2048]{0:T(1024)S(1)}, s32[2048]{0:T(1024)}, u32[]{:S(2)}) copy-start(s32[2048]{0:T(1024)} %param.20) | copy-start | bytes 24580
  3.7 11.8 %copy-start.1 = (s32[7,2048]{1,0:T(8,128)S(1)}, s32[7,2048]{1,0:T(8,128)}, u32[]{:S(2)}) copy-start(s32[7,2048]{1,0:T(8,128)} %columns.6) | copy-start | bytes 172036
  5.8 8.2 %collective-permute-start.1 = (f32[24,640]{1,0:T(8,128)S(1)}, f32[24,640]{1,0:T(8,128)S(1)}, u32[]{:S(2)}, u32[]{:S(2)}) collective-permute-start(f32[24,640]{1,0:T(8,128)S(1)} %get-tuple-element.30), channel_id=1, source_target_pairs={{0,30},{2,4},{4,2},{6,8},{8,6},{10,12},{12,10},{14,16},{16,14},{18... | collective-permute-start | bytes 184328 | tf_op jit(solution)/shard_map/ppermute | solution.py:522
  11.3 4.2 %collective-permute-start.2 = (f32[24,640]{1,0:T(8,128)S(1)}, f32[24,640]{1,0:T(8,128)S(1)}, u32[]{:S(2)}, u32[]{:S(2)}) collective-permute-start(f32[24,640]{1,0:T(8,128)S(1)} %get-tuple-element.31), channel_id=1, source_target_pairs={{0,1},{1,0},{2,3},{3,2},{4,5},{5,4},{6,7},{7,6},{8,9},{9,8},{10,11... | collective-permute-start | bytes 184328 | tf_op jit(solution)/shard_map/ppermute | solution.py:522
  12.8 1.2 %collective-permute-start = (f32[24,512]{1,0:T(8,128)S(1)}, f32[24,512]{1,0:T(8,128)S(1)}, u32[]{:S(2)}, u32[]{:S(2)}) collective-permute-start(f32[24,512]{1,0:T(8,128)S(1)} %get-tuple-element.29), channel_id=1, source_target_pairs={{0,2},{2,0},{4,6},{6,4},{8,10},{10,8},{12,14},{14,12},{16,18},{18,... | collective-permute-start | bytes 147464 | tf_op jit(solution)/shard_map/ppermute | solution.py:522
  15.5 11.4 %copy-start.2 = (s32[7,2048]{1,0:T(8,128)S(1)}, s32[7,2048]{1,0:T(8,128)}, u32[]{:S(2)}) copy-start(s32[7,2048]{1,0:T(8,128)} %slots.2) | copy-start | bytes 172036
  21.1 5.9 %copy-start.6 = (s32[2048]{0:T(1024)S(1)}, s32[2048]{0:T(1024)}, u32[]{:S(2)}) copy-start(s32[2048]{0:T(1024)} %param.19) | copy-start | bytes 24580
  21.1 5.9 %collective-permute-start.3 = (f32[8,768]{1,0:T(8,128)S(1)}, f32[8,768]{1,0:T(8,128)S(1)}, u32[]{:S(2)}, u32[]{:S(2)}) collective-permute-start(f32[8,768]{1,0:T(8,128)S(1)} %get-tuple-element.34), channel_id=1, source_target_pairs={{0,2},{2,0},{4,6},{6,4},{8,10},{10,8},{12,14},{14,12},{16,18},{18,... | collective-permute-start | bytes 73736 | tf_op jit(solution)/shard_map/ppermute | solution.py:522
  21.1 5.9 %collective-permute-start.4 = (f32[8,512]{1,0:T(8,128)S(1)}, f32[8,512]{1,0:T(8,128)S(1)}, u32[]{:S(2)}, u32[]{:S(2)}) collective-permute-start(f32[8,512]{1,0:T(8,128)S(1)} %get-tuple-element.35), channel_id=1, source_target_pairs={{0,30},{2,4},{4,2},{6,8},{8,6},{10,12},{12,10},{14,16},{16,14},{18... | collective-permute-start | bytes 49160 | tf_op jit(solution)/shard_map/ppermute | solution.py:522
  23.2 3.7 %collective-permute-start.5 = (f32[8,512]{1,0:T(8,128)S(1)}, f32[8,512]{1,0:T(8,128)S(1)}, u32[]{:S(2)}, u32[]{:S(2)}) collective-permute-start(f32[8,512]{1,0:T(8,128)S(1)} %get-tuple-element.36), channel_id=1, source_target_pairs={{0,1},{1,0},{2,3},{3,2},{4,5},{5,4},{6,7},{7,6},{8,9},{9,8},{10,11... | collective-permute-start | bytes 49160 | tf_op jit(solution)/shard_map/ppermute | solution.py:522
  38.0 1.4 %collective-permute-start.6 = (f32[120,256]{1,0:T(8,128)S(1)}, f32[120,256]{1,0:T(8,128)S(1)}, u32[]{:S(2)}, u32[]{:S(2)}) collective-permute-start(f32[120,256]{1,0:T(8,128)S(1)} %shard_map.159.own), channel_id=1, source_target_pairs={{0,2},{2,0},{4,6},{6,4},{8,10},{10,8},{12,14},{14,12},{16,18},{18,... | collective-permute-start | bytes 368648 | tf_op jit(solution)/shard_map/ppermute | solution.py:522
  39.4 6.7 %copy-start.3 = (s32[7,512]{1,0:T(8,128)S(1)}, s32[7,512]{1,0:T(8,128)}, u32[]{:S(2)}) copy-start(s32[7,512]{1,0:T(8,128)} %columns.8) | copy-start | bytes 43012
  39.7 3.7 %collective-permute-start.7 = (f32[8,128]{1,0:T(8,128)S(1)}, f32[8,128]{1,0:T(8,128)S(1)}, u32[]{:S(2)}, u32[]{:S(2)}) collective-permute-start(f32[8,128]{1,0:T(8,128)S(1)} %get-tuple-element.41), channel_id=1, source_target_pairs={{0,4},{2,6},{4,0},{6,2},{8,12},{10,14},{12,8},{14,10},{16,20},{18,... | collective-permute-start | bytes 12296 | tf_op jit(solution)/shard_map/ppermute | solution.py:522
  39.7 6.4 %collective-permute-start.8 = (f32[8,128]{1,0:T(8,128)S(1)}, f32[8,128]{1,0:T(8,128)S(1)}, u32[]{:S(2)}, u32[]{:S(2)}) collective-permute-start(f32[8,128]{1,0:T(8,128)S(1)} %get-tuple-element.41), channel_id=1, source_target_pairs={{0,28},{2,30},{4,8},{6,10},{8,4},{10,6},{12,16},{14,18},{16,12},{1... | collective-permute-start | bytes 12296 | tf_op jit(solution)/shard_map/ppermute | solution.py:522
  42.0 4.1 %collective-permute-start.9 = (f32[8,128]{1,0:T(8,128)S(1)}, f32[8,128]{1,0:T(8,128)S(1)}, u32[]{:S(2)}, u32[]{:S(2)}) collective-permute-start(f32[8,128]{1,0:T(8,128)S(1)} %get-tuple-element.42), channel_id=1, source_target_pairs={{0,1},{1,0},{2,3},{3,2},{4,5},{5,4},{6,7},{7,6},{8,9},{9,8},{10,11... | collective-permute-start | bytes 12296 | tf_op jit(solution)/shard_map/ppermute | solution.py:522
  46.1 8.1 %copy-start.5 = (s32[7,512]{1,0:T(8,128)S(1)}, s32[7,512]{1,0:T(8,128)}, u32[]{:S(2)}) copy-start(s32[7,512]{1,0:T(8,128)} %slots.3) | copy-start | bytes 43012
  47.7 3.9 %copy-start.12 = (s32[160]{0:T(256)S(1)}, s32[160]{0:T(256)}, u32[]{:S(2)}) copy-start(s32[160]{0:T(256)} %param.27) | copy-start | bytes 1924
  47.7 3.9 %collective-permute-start.10 = (f32[8,128]{1,0:T(8,128)S(1)}, f32[8,128]{1,0:T(8,128)S(1)}, u32[]{:S(2)}, u32[]{:S(2)}) collective-permute-start(f32[8,128]{1,0:T(8,128)S(1)} %get-tuple-element.45), channel_id=1, source_target_pairs={{0,4},{2,6},{4,0},{6,2},{8,12},{10,14},{12,8},{14,10},{16,20},{18,... | collective-permute-start | bytes 12296 | tf_op jit(solution)/shard_map/ppermute | solution.py:522
  47.9 6.3 %collective-permute-start.11 = (f32[8,128]{1,0:T(8,128)S(1)}, f32[8,128]{1,0:T(8,128)S(1)}, u32[]{:S(2)}, u32[]{:S(2)}) collective-permute-start(f32[8,128]{1,0:T(8,128)S(1)} %get-tuple-element.45), channel_id=1, source_target_pairs={{0,28},{2,30},{4,8},{6,10},{8,4},{10,6},{12,16},{14,18},{16,12},{1... | collective-permute-start | bytes 12296 | tf_op jit(solution)/shard_map/ppermute | solution.py:522
  50.1 4.1 %collective-permute-start.12 = (f32[8,128]{1,0:T(8,128)S(1)}, f32[8,128]{1,0:T(8,128)S(1)}, u32[]{:S(2)}, u32[]{:S(2)}) collective-permute-start(f32[8,128]{1,0:T(8,128)S(1)} %get-tuple-element.46), channel_id=1, source_target_pairs={{0,1},{1,0},{2,3},{3,2},{4,5},{5,4},{6,7},{7,6},{8,9},{9,8},{10,11... | collective-permute-start | bytes 12296 | tf_op jit(solution)/shard_map/ppermute | solution.py:522
  54.2 0.7 copy-start.8
  69.4 0.7 copy-start.7

commit v2 on v1

--- a/solution.py
+++ b/solution.py
@@ -48,9 +48,10 @@
 
 
 def onehot(columns):
-    low = jnp.broadcast_to(columns & (LANES - 1), (LANES, columns.shape[1]))
-    hot = (lax.broadcasted_iota(jnp.int32, low.shape, 0) == low).astype(F32).astype(BF16)
-    return twice(hot)
+    low = (columns & (LANES - 1)).astype(jnp.int16)
+    low = jnp.broadcast_to(low, (LANES, columns.shape[1]))
+    here = lax.broadcasted_iota(jnp.int16, low.shape, 0) == low
+    return twice(jnp.where(here, jnp.ones((), BF16), jnp.zeros((), BF16)))
 
 
 def choose_four(picked, high):
@@ -172,37 +173,64 @@
     return pltpu.roll(jnp.where(lane < half, above, below), half, 1)
 
 
-def call(body, outs, *args, scratch=()):
+def call(body, outs, *args, scratch=(), flops=0, space=pltpu.VMEM):
+    outs = [(out, F32) if isinstance(out[0], int) else out for out in outs]
+    cost = pl.CostEstimate(flops=flops, bytes_accessed=0, transcendentals=0) if flops else None
     return pl.pallas_call(
         body,
-        out_shape=[jax.ShapeDtypeStruct(shape, F32) for shape in outs],
-        in_specs=[pl.BlockSpec(memory_space=pltpu.VMEM)] * len(args),
+        out_shape=[jax.ShapeDtypeStruct(shape, dtype) for shape, dtype in outs],
+        in_specs=[pl.BlockSpec(memory_space=space)] * len(args),
         out_specs=[pl.BlockSpec(memory_space=pltpu.VMEM)] * len(outs),
         scratch_shapes=list(scratch),
-        compiler_params=pltpu.CompilerParams(vmem_limit_bytes=48 * 1024 * 1024),
+        cost_estimate=cost,
+        compiler_params=pltpu.CompilerParams(vmem_limit_bytes=32 * 1024 * 1024),
     )(*args)
 
 
-TILE = 256
-
-
-def tiles(count, body):
+def tiles(count, tile, body):
     def step(index, carry):
-        body(pl.ds(pl.multiple_of(index * TILE, TILE), TILE))
+        body(pl.ds(pl.multiple_of(index * tile, tile), tile))
         return carry
 
-    lax.fori_loop(0, count // TILE, step, 0)
-
-
-def fine_first(
-    source, operator, prolong, sends, prolong_one, sends_one, w_ref, first_ref, *rest
-):
-    picks = rest[-1]
-    parity_out, cross_out, slab_outs = rest[0], rest[1], rest[2:-1]
-    weights = row_weights(lambda k: operator[16 * k : 16 * k + 16])
+    lax.fori_loop(0, count // tile, step, 0, unroll=True)
+
+
+def fine_first(handed, slab_moves, *refs):
+    count = handed + 3
+    raw, refs = refs[:count], refs[count:]
+    kept, refs = refs[:handed], refs[handed:]
+    operator, prolong, prolong_one, w_ref, first_ref, parity_out, cross_out = refs[:7]
+    slab_outs, refs = refs[7 : 7 + slab_moves], refs[7 + slab_moves :]
+    operator_raw, prolong_raw, prolong_one_raw, picks, semaphores = refs
+    source, sends, sends_one = kept[0], kept[1], kept[2]
+    targets = [operator_raw, source, prolong_raw, sends, prolong_one_raw, sends_one, *kept[3:]]
+    copies = [
+        pltpu.make_async_copy(
+            raw[at], target if raw[at].ndim > 1 else target.at[0], semaphores.at[at]
+        )
+        for at, target in enumerate(targets)
+    ]
+    for copy in copies:
+        copy.start()
+    copies[0].wait()
+    sums = [None] * 4
+    for k in range(7):
+        for a in range(4):
+            value = jnp.abs(operator_raw[k, a])
+            sums[a] = value if sums[a] is None else sums[a] + value
+    weights = 1.0 + sum_components(jnp.concatenate(sums, axis=0))
+    copies[1].wait()
     first = twice(source[...]) / weights
     w_ref[...] = weights
     first_ref[...] = first
+    for at in range(2, 6):
+        copies[at].wait()
+    for half in range(2):
+        at = slice(8 * half, 8 * half + 8)
+        prolong[at] = jnp.concatenate([prolong_raw[2 * half], prolong_raw[2 * half + 1]], axis=0)
+        prolong_one[at] = jnp.concatenate(
+            [prolong_one_raw[2 * half], prolong_one_raw[2 * half + 1]], axis=0
+        )
     table = jnp.concatenate(
         [table_four(chunks_of(first)), table_sixteen(chunks_of(prolong[...]))], axis=0
     )
@@ -216,7 +244,7 @@
         picks[8:16, at] = low
         picks[16:24, at] = high
 
-    tiles(sends.shape[1], pick)
+    tiles(sends.shape[1], 512, pick)
     coarse = gather_sixteen(table_sixteen(chunks_of(prolong_one[...])), sends_one[...])
     sub, slab = place()
     count = sends.shape[1] // 4
@@ -233,6 +261,14 @@
         out[:, 0:count] = jnp.where(up, high_first, low_first)
         out[0:16, count:] = jnp.where(up, coarse[:, LANES : 2 * LANES], coarse[:, 0:LANES])
         out[16:24, count:] = jnp.zeros((8, LANES), F32)
+    for k in range(7):
+        for half in range(2):
+            row = 16 * k + 8 * half
+            operator[row : row + 8] = jnp.concatenate(
+                [operator_raw[k, 2 * half], operator_raw[k, 2 * half + 1]], axis=0
+            )
+    for copy in copies[6:]:
+        copy.wait()
 
 
 def fine_ghosts(rows, count, sizes, parity_in, cross_in, slab_ins):
@@ -268,14 +304,14 @@
         residual = twice(source[:, at]) - apply_tile(table, operator, columns, at)
         second_ref[:, at] = first_ref[:, at] + residual / w_ref[:, at]
 
-    tiles(source.shape[1], step)
+    tiles(source.shape[1], 1024, step)
     smoothed[...] = second_ref[0:4]
     table = table_four(chunks_of(second_ref[...]))
 
     def pick(at):
         picks[:, at] = gather_four(table, sends[:, at])
 
-    tiles(sends.shape[1], pick)
+    tiles(sends.shape[1], 1024, pick)
     sub, slab = place()
     low_first, high_first = picks[:, 0:count], picks[:, count : 2 * count]
     low_second, high_second = picks[:, 2 * count : 3 * count], picks[:, 3 * count :]
@@ -291,14 +327,16 @@
 
 
 def coarsen(table, operator, prolong, columns, slots, aggregates, sums, count):
+    tile = 512
+
     def step(at):
         wide_prolong = expand(prolong[:, at])
-        totals = [[jnp.zeros((8, TILE), F32) for _ in range(2)] for _ in range(7)]
+        totals = [[jnp.zeros((8, tile), F32) for _ in range(2)] for _ in range(7)]
         for k in range(7):
             column = columns[k : k + 1, at]
             near = choose_sixteen(matmul(table, onehot(column)), column >> 7)
             blocks = triple_product(wide_prolong, operator[16 * k : 16 * k + 16, at], near)
-            slot = jnp.broadcast_to(slots[k : k + 1, at], (8, TILE))
+            slot = jnp.broadcast_to(slots[k : k + 1, at], (8, tile))
             for s in range(7):
                 here = slot == s
                 for half in range(2):
@@ -308,42 +346,46 @@
                 row = 16 * s + 8 * half
                 sums[row : row + 8, at] = totals[s][half]
 
-    tiles(columns.shape[1], step)
+    tiles(columns.shape[1], tile, step)
     return scatter(sums[...], aggregates[...], count)
 
 
 def fine_coarsen(
+    sizes, operator, prolong, columns, slots, aggregates, second_ref, parity_old, cross_old, *rest
+):
+    slab_old, (out, sums) = rest[:-2], rest[-2:]
+    count = parity_old.shape[1]
+    ghosts = fine_ghosts(slice(8, 24), count, sizes, parity_old, cross_old, slab_old)
+    table = table_sixteen(chunks_of(prolong[...]) + ghosts)
+    out[...] = coarsen(
+        table, operator, prolong, columns, slots, aggregates, sums, out.shape[1]
+    )
+
+
+def fine_restrict(
     sizes,
     source,
     operator,
     prolong,
     columns,
-    slots,
     aggregates,
     second_ref,
-    parity_old,
-    cross_old,
+    operator_own,
     parity_in,
     cross_in,
     *rest,
 ):
-    slab_count = (len(rest) - 3) // 2
-    slab_old, slab_ins, rest = rest[:slab_count], rest[slab_count : 2 * slab_count], rest[-3:]
-    out, sums, lifted = rest
-    count = parity_old.shape[1]
-    ghosts = fine_ghosts(slice(0, 8), count, sizes, parity_in, cross_in, slab_ins)
+    slab_ins, (out, lifted) = rest[:-2], rest[-2:]
+    ghosts = fine_ghosts(slice(0, 8), cross_in.shape[1], sizes, parity_in, cross_in, slab_ins)
     table = table_four(chunks_of(second_ref[...]) + ghosts)
 
     def step(at):
         residual = twice(source[:, at]) - apply_tile(table, operator, columns, at)
         lifted[:, at] = lift(prolong[:, at], residual)
 
-    tiles(source.shape[1], step)
-    rows = out.shape[1]
-    out[112:120] = scatter(lifted[...], aggregates[...], rows)
-    ghosts = fine_ghosts(slice(8, 24), count, sizes, parity_old, cross_old, slab_old)
-    table = table_sixteen(chunks_of(prolong[...]) + ghosts)
-    out[0:112] = coarsen(table, operator, prolong, columns, slots, aggregates, sums, rows)
+    tiles(source.shape[1], 1024, step)
+    out[0:112] = operator_own[...]
+    out[112:120] = scatter(lifted[...], aggregates[...], out.shape[1])
 
 
 def slab_faces(picks, slab, slab_outs):
@@ -391,7 +433,7 @@
         residual = source[:, at] - apply_tile(table, operator, columns, at)
         second_ref[:, at] = first[:, at] + residual / weights[:, at]
 
-    tiles(source.shape[1], step)
+    tiles(source.shape[1], 512, step)
     sub, slab = place()
     half = smoothed.shape[1]
     smoothed[...] = jnp.where(sub % 2 == 0, second_ref[0:4, 0:half], second_ref[0:4, half:])
@@ -403,34 +445,18 @@
 def pair_coarsen(
     sizes,
     operator,
-    source,
-    second_ref,
     prolong,
     columns,
     slots,
     aggregates,
-    sends,
     parity_old,
     cross_old,
     forwarded,
-    even_in,
-    odd_in,
     *rest,
 ):
-    slab_count = (len(rest) - 6) // 2
-    slab_old, slab_ins, rest = rest[:slab_count], rest[slab_count : 2 * slab_count], rest[-6:]
-    message, operator_two, source_two, first_two, sums, lifted = rest
+    slab_old, (operator_two, weights_two, sums) = rest[:-3], rest[-3:]
     sub, slab = place()
     even = sub % 2 == 0
-    table = table_four(chunks_of(second_ref[...]) + pair_ghosts(sizes, even_in, odd_in, slab_ins))
-
-    def step(at):
-        residual = source[:, at] - apply_tile(table, operator, columns, at)
-        lifted[:, at] = lift(prolong[:, at], residual)
-
-    tiles(source.shape[1], step)
-    source_two[...] = scatter(lifted[...], aggregates[...], LANES)
-
     count = parity_old.shape[1]
     values = [ref[0:16, count:] for ref in slab_old] + [None]
     below, above = neighbours(slab, sizes[1], values[0], values[1])
@@ -448,55 +474,92 @@
     operator_two[...] = coarsen(
         table, operator, prolong, columns, slots, aggregates, sums, LANES
     )
-    first = source_two[...] / row_weights(lambda k: operator_two[16 * k : 16 * k + 16])
+    weights_two[...] = row_weights(lambda k: operator_two[16 * k : 16 * k + 16])
+
+
+def pair_restrict(
+    sizes,
+    operator,
+    source,
+    second_ref,
+    prolong,
+    columns,
+    aggregates,
+    sends,
+    weights_two,
+    even_in,
+    odd_in,
+    *rest,
+):
+    slab_count = (len(rest) - 4) // 2
+    slab_ins, rest = rest[:slab_count], rest[slab_count:]
+    source_two, first_two, whole_out = rest[:3]
+    slab_outs, lifted = rest[3:-1], rest[-1]
+    sub, slab = place()
+    table = table_four(chunks_of(second_ref[...]) + pair_ghosts(sizes, even_in, odd_in, slab_ins))
+
+    def step(at):
+        residual = source[:, at] - apply_tile(table, operator, columns, at)
+        lifted[:, at] = lift(prolong[:, at], residual)
+
+    tiles(source.shape[1], 512, step)
+    total = scatter(lifted[...], aggregates[...], LANES)
+    source_two[...] = total
+    first = total / weights_two[...]
     first_two[...] = first
+    half = LANES // 2
     lane = lax.broadcasted_iota(jnp.int32, first.shape, 1)
-    first = jnp.where(lane < LANES // 2, first, 0.0)
-    placed = jnp.where(group % 2 == 0, first, pltpu.roll(first, LANES // 2, 1))
-    picks = gather_four(table_four([placed]), sends[...])
+    first = jnp.where(lane < half, first, 0.0)
+    placed = jnp.where(sub // 2 % 2 == 0, first, pltpu.roll(first, half, 1))
+    filler = jnp.zeros((1, -sends.shape[1] % LANES), jnp.int32)
+    picks = gather_four(table_four([placed]), jnp.concatenate([sends[...], filler], axis=1))
     faces = picks[:, 0:LANES]
-    seconds = pltpu.roll(picks[:, LANES:], LANES // 2, 1)
-    sent = pair_rows(jnp.where(lane < LANES // 2, first, seconds), faces)
-    message[...] = jnp.broadcast_to(sent[None], message.shape)
-
-
-def group_second(sizes, operator, source, first_two, columns, received, out):
-    sub, slab = place()
-    subs, slabs = sizes
+    seconds = pltpu.roll(picks[:, LANES:], half, 1)
+
+    def sent(value):
+        return jnp.where(lane < half, value, seconds)
+
+    whole_out[...] = sent(first)
+    slab_even = slab % 2 == 0
+    for position, out in enumerate(slab_outs):
+        up = slab_even if position == 0 else jnp.logical_not(slab_even)
+        out[...] = sent(jnp.where(up, pltpu.roll(faces, half, 1), faces))
+
+
+def group_apply(sizes, operator, first_two, columns, *rest):
+    received, out = rest[:-1], rest[-1]
+    sub, slab = place()
     group, pair = sub // 4, sub // 2 % 2
-    shape = (8, LANES)
-    lane = lax.broadcasted_iota(jnp.int32, shape, 1)
+    even = sub % 2 == 0
     half = LANES // 2
-
-    def from_pair(group_at, pair_at, slab_at):
-        valid = (group_at >= 0) & (group_at < subs // 4) & (slab_at >= 0) & (slab_at < slabs)
-        index = (group_at * 4 + pair_at * 2 + sub % 2) * slabs + slab_at
-        index = jnp.where(valid, index, 0)
-        return jnp.where(valid, received[index], jnp.zeros(shape, F32))
-
-    def from_group(group_at, slab_at):
-        return from_pair(group_at, 0, slab_at) + from_pair(group_at, 1, slab_at)
-
-    def lower(value):
-        return pair_rows(value, pltpu.roll(value, 4, 0))
-
-    def upper(value):
-        return pair_rows(pltpu.roll(value, 4, 0), value)
-
-    pairs = [lower(from_pair(group, j, slab)) for j in range(2)]
-    first = jnp.where(lane < half, pairs[0], pltpu.roll(pairs[1], half, 1))
-    firsts = swap_halves(
-        upper(from_group(group, slab - 1)), upper(from_group(group, slab + 1)), half
+    lane = lax.broadcasted_iota(jnp.int32, (8, LANES), 1)
+    none = jnp.zeros((8, LANES), F32)
+
+    def left_part(value):
+        return jnp.where(lane < half, value, 0.0)
+
+    mine, other = left_part(first_two[...]), left_part(received[0][...])
+    first = jnp.where(
+        pair == 0, mine + pltpu.roll(other, half, 1), other + pltpu.roll(mine, half, 1)
+    )
+    first = jnp.where(even, first, none)
+
+    odd = received[3][...] + received[4][...] if len(received) > 4 else None
+    below, above = neighbours(slab, sizes[1], received[1][...] + received[2][...], odd)
+    firsts = jnp.where(even, left_part(below) + pltpu.roll(left_part(above), half, 1), none)
+
+    left, right = neighbours(
+        group,
+        sizes[0] // 4,
+        received[0][...] + received[2][...],
+        received[1][...] + received[3][...],
     )
     width = GX // 4 * (GZ // 4)
-    left = lower(from_group(group - 1, slab))
-    right = lower(from_group(group + 1, slab))
-    seconds = jnp.where(
-        lane < width,
-        pltpu.roll(left, LANES - half - width, 1),
-        pltpu.roll(right, LANES - half + width, 1),
-    )
-    seconds = jnp.where(lane < 2 * width, seconds, 0.0)
+    left = pltpu.roll(left, LANES - half - width, 1)
+    right = pltpu.roll(right, LANES - half + width, 1)
+    seconds = jnp.where(lane < width, left, jnp.where(lane < 2 * width, right, 0.0))
+    seconds = jnp.where(even, none, seconds)
+
     table = table_four([first, firsts, seconds])
     mine = jnp.where(pair == 0, columns[...], pltpu.roll(columns[...], half, 1))
     total = None
@@ -504,26 +567,89 @@
         near = twice(gather_four(table, mine[k : k + 1]))
         term = operator[16 * k : 16 * k + 16] * near
         total = term if total is None else total + term
-    residual = source[...] - sum_components(total)
-    weights = row_weights(lambda k: operator[16 * k : 16 * k + 16])
-    second = first_two[...] + residual / weights
+    out[...] = sum_components(total)
+
+
+def group_second(source, weights, first_two, own, other, out):
+    sub, slab = place()
+    residual = source[...] - (own[...] + other[...])
+    second = first_two[...] + residual / weights[...]
     share = out.shape[1]
     out[...] = jnp.where(sub % 2 == 0, second[0:4, 0:share], second[0:4, share : 2 * share])
 
 
-def pairing(value, axis, group, odd):
-    count = lax.axis_size(axis)
-    blocks = count // group
+def swap_by_core(value, even_mate, odd_mate):
+    subs, slabs = lax.axis_size("sub"), lax.axis_size("slab")
     route = []
-    for index in range(count):
-        block = index // group
+    for sub in range(subs):
+        for slab in range(slabs):
+            target = (even_mate if sub % 2 == 0 else odd_mate)(sub, slab)
+            if not (0 <= target[0] < subs and 0 <= target[1] < slabs):
+                target = (sub ^ 2, slab)
+            route.append((sub * slabs + slab, target[0] * slabs + target[1]))
+    return lax.ppermute(value, ("sub", "slab"), route)
+
+
+def odd_mate_of(index):
+    return ((index - 1) ^ 1) + 1
+
+
+def group_exchange(whole, slab_values):
+    def along_sub(odd, flip):
+        def mate(sub, slab):
+            block = odd_mate_of(sub // 4) if odd else sub // 4 ^ 1
+            return block * 4 + (sub % 4 ^ flip), slab
+
+        return mate
+
+    def along_slab(odd, flip):
+        return lambda sub, slab: (sub ^ flip, odd_mate_of(slab) if odd else slab ^ 1)
+
+    def pair(sub, slab):
+        return sub ^ 2, slab
+
+    first = slab_values[0]
+    received = [
+        swap_by_core(whole, pair, along_sub(False, 0)),
+        swap_by_core(first, along_slab(False, 0), along_sub(True, 0)),
+        swap_by_core(first, along_slab(False, 2), along_sub(False, 2)),
+    ]
+    if len(slab_values) == 1:
+        return received + [swap_by_core(first, pair, along_sub(True, 2))]
+    second = slab_values[1]
+    return received + [
+        swap_by_core(second, along_slab(True, 0), along_sub(True, 2)),
+        swap_by_core(second, along_slab(True, 2), pair),
+    ]
+
+
+def sub_pairing(value, group, odd):
+    subs, slabs = lax.axis_size("sub"), lax.axis_size("slab")
+    route = []
+    for sub in range(subs):
+        block = sub // group
         mate = ((block - 1) ^ 1) + 1 if odd else block ^ 1
-        route.append((index, mate % blocks * group + index % group))
-    return lax.ppermute(value, axis, route)
+        for slab in range(slabs):
+            target = (mate * group + sub % group, slab)
+            if not 0 <= mate < subs // group:
+                target = (sub ^ group // 2, slab) if group > 1 else (sub, slab ^ 1)
+            route.append((sub * slabs + slab, target[0] * slabs + target[1]))
+    return lax.ppermute(value, ("sub", "slab"), route)
+
+
+def slab_pairing(value, odd):
+    subs, slabs = lax.axis_size("sub"), lax.axis_size("slab")
+    route = []
+    for sub in range(subs):
+        for slab in range(slabs):
+            mate = ((slab - 1) ^ 1) + 1 if odd else slab ^ 1
+            target = (sub, mate) if 0 <= mate < slabs else (sub ^ 1, slab)
+            route.append((sub * slabs + slab, target[0] * slabs + target[1]))
+    return lax.ppermute(value, ("sub", "slab"), route)
 
 
 def slab_pairings(values):
-    return [pairing(value, "slab", 1, position == 1) for position, value in enumerate(values)]
+    return [slab_pairing(value, position == 1) for position, value in enumerate(values)]
 
 
 def on_device(
@@ -548,29 +674,42 @@
     rows_one = rows // 8
     pair_rows_one = 2 * rows_one
     count = 2 * GY * GZ
-    operator = operator.reshape(112, rows)
-    prolong = prolong.reshape(16, rows)
-    prolong_one = prolong_one.reshape(16, pair_rows_one)
-    sends = sends.reshape(1, -1)
-    sends_one = sends_one.reshape(1, -1)
-    aggregates = aggregates.reshape(1, -1)
-    aggregates_one = aggregates_one.reshape(1, -1)
-    sends_two = jnp.pad(sends_two, (0, -sends_two.shape[0] % LANES)).reshape(1, -1)
-
-    weights, first, even, odd, *slabs = call(
-        fine_first,
-        [(8, rows), (8, rows), (24, count), (24, count + LANES)]
+    kept = [
+        source,
+        sends,
+        sends_one,
+        columns,
+        slots,
+        aggregates,
+        columns_one,
+        slots_one,
+        aggregates_one,
+        columns_two,
+        sends_two,
+    ]
+    raw = [operator, kept[0], prolong, kept[1], prolong_one, kept[2], *kept[3:]]
+    handed = len(kept)
+    out = call(
+        functools.partial(fine_first, handed, slab_moves),
+        [((1, value.shape[0]) if value.ndim == 1 else value.shape, value.dtype) for value in kept]
+        + [(112, rows), (16, rows), (16, pair_rows_one)]
+        + [(8, rows), (8, rows), (24, count), (24, count + LANES)]
         + [(24, count + LANES)] * slab_moves,
-        source,
-        operator,
-        prolong,
-        sends,
-        prolong_one,
-        sends_one,
-        scratch=[pltpu.VMEM((24, sends.shape[1]), F32)],
-    )
-    even_old = pairing(even, "sub", 1, False)
-    odd_old = pairing(odd, "sub", 1, True)
+        *[pltpu.with_memory_space_constraint(value, pltpu.HBM) for value in raw],
+        scratch=[
+            pltpu.VMEM(operator.shape, F32),
+            pltpu.VMEM(prolong.shape, F32),
+            pltpu.VMEM(prolong_one.shape, F32),
+            pltpu.VMEM((24, rows), F32),
+            pltpu.SemaphoreType.DMA((len(raw),)),
+        ],
+        space=pltpu.HBM,
+    )
+    source, sends, sends_one, columns, slots, aggregates = out[:6]
+    columns_one, slots_one, aggregates_one, columns_two, sends_two = out[6:11]
+    operator, prolong, prolong_one, weights, first, even, odd, *slabs = out[11:]
+    even_old = sub_pairing(even, 1, False)
+    odd_old = sub_pairing(odd, 1, True)
     slabs_old = slab_pairings(slabs)
 
     smoothed, even, odd, *rest = call(
@@ -590,14 +729,13 @@
         scratch=[pltpu.VMEM((8, sends.shape[1]), F32)],
     )
     slabs, second = rest[:-1], rest[-1]
-    forwarded = pairing(even, "sub", 1, False)
-    odd_in = pairing(odd, "sub", 1, True)
+    forwarded = sub_pairing(even, 1, False)
+    odd_in = sub_pairing(odd, 1, True)
     slabs_in = slab_pairings(slabs)
 
-    (own,) = call(
+    (operator_own,) = call(
         functools.partial(fine_coarsen, sizes),
-        [(120, rows_one)],
-        source,
+        [(112, rows_one)],
         operator,
         prolong,
         columns,
@@ -606,13 +744,26 @@
         second,
         even_old,
         odd_old,
+        *slabs_old,
+        scratch=[pltpu.VMEM((112, rows), F32)],
+        flops=4 * 10**9,
+    )
+    (own,) = call(
+        functools.partial(fine_restrict, sizes),
+        [(120, rows_one)],
+        source,
+        operator,
+        prolong,
+        columns,
+        aggregates,
+        second,
+        operator_own,
         forwarded,
         odd_in,
-        *slabs_old,
         *slabs_in,
-        scratch=[pltpu.VMEM((112, rows), F32), pltpu.VMEM((8, rows), F32)],
-    )
-    other = pairing(own, "sub", 1, False)
+        scratch=[pltpu.VMEM((8, rows), F32)],
+    )
+    other = sub_pairing(own, 1, False)
 
     faces = [(8, LANES)] * (1 + slab_moves)
     operator_one, source_one, weights_one, first_one, group_out, *slabs = call(
@@ -622,10 +773,25 @@
         other,
         sends_one,
     )
-    even_in = pairing(group_out, "sub", 2, False)
-    odd_in = pairing(group_out, "sub", 2, True)
+    even_in = sub_pairing(group_out, 2, False)
+    odd_in = sub_pairing(group_out, 2, True)
     slabs_in = slab_pairings(slabs)
 
+    operator_two, weights_two = call(
+        functools.partial(pair_coarsen, sizes),
+        [(112, LANES), (8, LANES)],
+        operator_one,
+        prolong_one,
+        columns_one,
+        slots_one,
+        aggregates_one,
+        even_old,
+        odd_old,
+        forwarded,
+        *slabs_old,
+        scratch=[pltpu.VMEM((112, pair_rows_one), F32)],
+        flops=10**9,
+    )
     smoothed_one, second_one, group_out, *slabs = call(
         functools.partial(pair_second, sizes),
         [(4, rows_one), (8, pair_rows_one)] + faces,
@@ -639,40 +805,44 @@
         odd_in,
         *slabs_in,
     )
-    even_in = pairing(group_out, "sub", 2, False)
-    odd_in = pairing(group_out, "sub", 2, True)
+    even_in = sub_pairing(group_out, 2, False)
+    odd_in = sub_pairing(group_out, 2, True)
     slabs_in = slab_pairings(slabs)
 
-    message, operator_two, source_two, first_two = call(
-        functools.partial(pair_coarsen, sizes),
-        [(sizes[0] * sizes[1], 8, LANES), (112, LANES), (8, LANES), (8, LANES)],
+    source_two, first_two, whole, *slabs = call(
+        functools.partial(pair_restrict, sizes),
+        [(8, LANES), (8, LANES)] + faces,
         operator_one,
         source_one,
         second_one,
         prolong_one,
         columns_one,
-        slots_one,
         aggregates_one,
         sends_two,
-        even_old,
-        odd_old,
-        forwarded,
+        weights_two,
         even_in,
         odd_in,
-        *slabs_old,
         *slabs_in,
-        scratch=[pltpu.VMEM((112, pair_rows_one), F32), pltpu.VMEM((8, pair_rows_one), F32)],
-    )
-    received = lax.all_to_all(message, ("sub", "slab"), 0, 0)
-
-    (smoothed_two,) = call(
-        functools.partial(group_second, sizes),
-        [(4, rows_one // 8)],
+        scratch=[pltpu.VMEM((8, pair_rows_one), F32)],
+    )
+    received = group_exchange(whole, slabs)
+    (applied,) = call(
+        functools.partial(group_apply, sizes),
+        [(8, LANES)],
         operator_two,
-        source_two,
         first_two,
         columns_two,
-        received,
+        *received,
+    )
+    applied_other = sub_pairing(applied, 1, False)
+    (smoothed_two,) = call(
+        group_second,
+        [(4, rows_one // 8)],
+        source_two,
+        weights_two,
+        first_two,
+        applied,
+        applied_other,
     )
     return (smoothed, smoothed_one, smoothed_two)
 

time: 71.5 us -> 46.4 us (0.65)
  blocking collectives: 11.9 us -> 0 us
  Pallas kernels: 24.3 us -> 15.3 us
  local copies, waits for them, and re-layouts: 4.44 us -> 0 us
  starting transfers between devices: 18.3 us -> 19.2 us
    all_to_all x1 -> x0, blocking collectives: 11.9 us -> none  [on_device(): received = lax.all_to_all(message, ('sub', 'slab'), 0, 0)]
    pallas_call x7 -> x10, Pallas kernels: 24.3 us -> 15.3 us  [call(): pl.pallas_call(body, out_shape=[jax.ShapeDtypeStruct(shape, dtype) for sh...]
    unnamed x26 -> x0, local copies, waits for them, and re-layouts: 2.84 us -> none
    reshape x4 -> x0, local copies, waits for them, and re-layouts: 1.6 us -> none  [the longest x1 1.53 us: on_device(): operator = operator.reshape(112, rows)]
    ppermute x13 -> x18, starting transfers between devices: 18.3 us -> 19.2 us  [the longest x10 12.1 us: sub_pairing(): return lax.ppermute(value, ('sub', 'slab'), route)]
    ppermute x13 -> x18, waiting for transfers between devices: 11.6 us -> 11.1 us  [the longest x10 4.43 us: sub_pairing(): return lax.ppermute(value, ('sub', 'slab'), route)]
  transfers between devices with their start and end apart: 13 -> 18, of which waited for: 6 -> 10; matrix products, arithmetic and copies ran while one was open for 0% -> 0% of each run, Pallas kernels for 0% -> 13%
where the time goes in v2:
time: 46.4 us; the launch traced here: 46.3 us
  starting transfers between devices  19.2 us (41%)
  Pallas kernels  15.3 us (33%)
  waiting for transfers between devices  11.1 us (24%)
  between operations  0.7 us (2%)
    pallas_call x10, Pallas kernels, call(): pl.pallas_call(body, out_shape=[jax.ShapeDtypeStruct(shape, dtype) for sh...  15.3 us
    ppermute x10, starting transfers between devices, sub_pairing(): return lax.ppermute(value, ('sub', 'slab'), route)  12.1 us
    ppermute x10, waiting for transfers between devices, sub_pairing(): return lax.ppermute(value, ('sub', 'slab'), route)  4.43 us
    ppermute x4, starting transfers between devices, slab_pairing(): return lax.ppermute(value, ('sub', 'slab'), route)  3.62 us
    ppermute x4, waiting for transfers between devices, slab_pairing(): return lax.ppermute(value, ('sub', 'slab'), route)  3.59 us
    ppermute x4, starting transfers between devices, swap_by_core(): return lax.ppermute(value, ('sub', 'slab'), route)  3.54 us
    ppermute x4, waiting for transfers between devices, swap_by_core(): return lax.ppermute(value, ('sub', 'slab'), route)  3.07 us
  transfers between devices with their start and end apart: 18, of which 10 were waited for; matrix products, arithmetic and copies ran while one was open for 0% of the time, Pallas kernels for 13%

profile of v2, /device:TPU:0, one launch (start us, length us, event | category | flops | bytes accessed | tf_op | source)
XLA Modules:
  0.0 46.3 jit_solution(16221498309440786759)
XLA Ops:
  0.6 2.2 %shard_map.157 = (f32[4,2048]{1,0:T(4,128)S(1)}, s32[1,2048]{1,0:T(1,128)S(1)}, s32[1,384]{1,0:T(1,128)S(1)}, s32[7,2048]{1,0:T(8,128)S(1)}, s32[7,2048]{1,0:T(8...) custom-call(f32[7,4,4,2048]{3,2,1,0:T(4,128)} %refs_0_.1, ...), custom_call_target="tpu_custom_call" | custom-call | tf_op jit(solution)/shard_map/pallas_call | solution.py:179
  2.8 3.0 %collective-permute-start.1 = (f32[24,640]{1,0:T(8,128)S(1)}, f32[24,640]{1,0:T(8,128)S(1)}, u32[]{:S(2)}, u32[]{:S(2)}) collective-permute-start(f32[24,640]{1,0:T(8,128)S(1)} %get-tuple-element.50), channel_id=1, source_target_pairs={{0,1},{1,0},{2,4},{3,5},{4,2},{5,3},{6,8},{7,9},{8,6},{9,7},{10,12... | collective-permute-start | bytes 184328 | tf_op jit(solution)/shard_map/ppermute | solution.py:637
  5.8 0.1 collective-permute-start.2
  5.9 1.3 %collective-permute-start = (f32[24,512]{1,0:T(8,128)S(1)}, f32[24,512]{1,0:T(8,128)S(1)}, u32[]{:S(2)}, u32[]{:S(2)}) collective-permute-start(f32[24,512]{1,0:T(8,128)S(1)} %get-tuple-element.49), channel_id=1, source_target_pairs={{0,2},{1,3},{2,0},{3,1},{4,6},{5,7},{6,4},{7,5},{8,10},{9,11},{10,... | collective-permute-start | bytes 147464 | tf_op jit(solution)/shard_map/ppermute | solution.py:637
  7.2 0.9 %collective-permute-done.parity_in.parity_old = f32[24,512]{1,0:T(8,128)S(1)} collective-permute-done((f32[24,512]{1,0:T(8,128)S(1)}, f32[24,512]{1,0:T(8,128)S(1)}, u32[]{:S(2)}, u32[]{:S(2)}) %collective-permute-start) | collective-permute-done | bytes 49184 | tf_op jit(solution)/shard_map/ppermute | solution.py:637
  8.1 0.0 collective-permute-done.1.cross_in.cross_old
  8.1 2.0 %collective-permute-done.2.rest_0_ = f32[24,640]{1,0:T(8,128)S(1)} collective-permute-done((f32[24,640]{1,0:T(8,128)S(1)}, f32[24,640]{1,0:T(8,128)S(1)}, u32[]{:S(2)}, u32[]{:S(2)}) %collective-permute-start.2) | collective-permute-done | bytes 61472 | tf_op jit(solution)/shard_map/ppermute | solution.py:648
  10.0 2.1 %shard_map.158 = (f32[4,2048]{1,0:T(4,128)}, f32[8,768]{1,0:T(8,128)S(1)}, f32[8,512]{1,0:T(8,128)S(1)}, f32[8,512]{1,0:T(8,128)S(1)}, f32[8,2048]{1,0:T(8,128)S(1)}) custom-call(f32[4,2048]{1,0:T(4,128)S(1)} %get-tuple-element.43.source, f32[112,2048]{1,0:T(8,128)S(1)} %get-tuple-element.44.operator, s32[7,2048]{1,0:T(8,128)S(1)} %get-tuple-element.45.columns, ...), custom_call_target="tpu_custom_call" | custom-call | tf_op jit(solution)/shard_map/pallas_call | solution.py:179
  12.1 1.3 %collective-permute-start.4 = (f32[8,512]{1,0:T(8,128)S(1)}, f32[8,512]{1,0:T(8,128)S(1)}, u32[]{:S(2)}, u32[]{:S(2)}) collective-permute-start(f32[8,512]{1,0:T(8,128)S(1)} %get-tuple-element.58), channel_id=1, source_target_pairs={{0,1},{1,0},{2,4},{3,5},{4,2},{5,3},{6,8},{7,9},{8,6},{9,7},{10,12... | collective-permute-start | bytes 49160 | tf_op jit(solution)/shard_map/ppermute | solution.py:637
  13.4 0.7 %collective-permute-start.5 = (f32[8,512]{1,0:T(8,128)S(1)}, f32[8,512]{1,0:T(8,128)S(1)}, u32[]{:S(2)}, u32[]{:S(2)}) collective-permute-start(f32[8,512]{1,0:T(8,128)S(1)} %get-tuple-element.59), channel_id=1, source_target_pairs={{0,1},{1,0},{2,3},{3,2},{4,5},{5,4},{6,7},{7,6},{8,9},{9,8},{10,11... | collective-permute-start | bytes 49160 | tf_op jit(solution)/shard_map/ppermute | solution.py:648
  14.1 0.0 collective-permute-start.3
  14.2 4.8 %shard_map.159.operator_own = f32[112,256]{1,0:T(8,128)S(1)} custom-call(f32[112,2048]{1,0:T(8,128)S(1)} %get-tuple-element.44.operator, f32[16,2048]{1,0:T(8,128)S(1)} %get-tuple-element.53.prolong, s32[7,2048]{1,0:T(8,128)S(1)} %get-tuple-element.45.columns, s32[7,2048]{1,0:T(8,128)S(1)} %get-tuple-element.56.slots, ...), custom_call_target="tpu_custom_call" | custom-call | flops 4000000000 | tf_op jit(solution)/shard_map/pallas_call | solution.py:179
  19.0 0.0 collective-permute-done.4.cross_in
  19.0 0.0 collective-permute-done.5.rest_0_
  19.0 0.0 collective-permute-done.3.parity_in.forwarded
  19.0 1.7 %shard_map.160.own = f32[120,256]{1,0:T(8,128)S(1)} custom-call(f32[4,2048]{1,0:T(4,128)S(1)} %get-tuple-element.43.source, f32[112,2048]{1,0:T(8,128)S(1)} %get-tuple-element.44.operator, f32[16,2048]{1,0:T(8,128)S(1)} %get-tuple-element.53.prolong, s32[7,2048]{1,0:T(8,128)S(1)} %get-tuple-element.45.columns, s32[1,2048]{1,0:T(1,128)S(1)} %get-tuple-element.54.aggregates, ...), custom_call_target="tpu_custom_call" | custom-call | tf_op jit(solution)/shard_map/pallas_call | solution.py:179
  20.7 0.5 %collective-permute-start.6 = (f32[120,256]{1,0:T(8,128)S(1)}, f32[120,256]{1,0:T(8,128)S(1)}, u32[]{:S(2)}, u32[]{:S(2)}) collective-permute-start(f32[120,256]{1,0:T(8,128)S(1)} %shard_map.160.own), channel_id=1, source_target_pairs={{0,2},{1,3},{2,0},{3,1},{4,6},{5,7},{6,4},{7,5},{8,10},{9,11},{10,... | collective-permute-start | bytes 368648 | tf_op jit(solution)/shard_map/ppermute | solution.py:637
  21.3 1.0 %collective-permute-done.6.other = f32[120,256]{1,0:T(8,128)S(1)} collective-permute-done((f32[120,256]{1,0:T(8,128)S(1)}, f32[120,256]{1,0:T(8,128)S(1)}, u32[]{:S(2)}, u32[]{:S(2)}) %collective-permute-start.6) | collective-permute-done | bytes 122912 | tf_op jit(solution)/shard_map/ppermute | solution.py:637
  22.3 0.3 shard_map.161
  22.5 1.3 %collective-permute-start.9 = (f32[8,128]{1,0:T(8,128)S(1)}, f32[8,128]{1,0:T(8,128)S(1)}, u32[]{:S(2)}, u32[]{:S(2)}) collective-permute-start(f32[8,128]{1,0:T(8,128)S(1)} %get-tuple-element.67), channel_id=1, source_target_pairs={{0,1},{1,0},{2,3},{3,2},{4,5},{5,4},{6,7},{7,6},{8,9},{9,8},{10,11... | collective-permute-start | bytes 12296 | tf_op jit(solution)/shard_map/ppermute | solution.py:648
  23.9 0.1 collective-permute-start.8
  24.0 1.7 %collective-permute-start.7 = (f32[8,128]{1,0:T(8,128)S(1)}, f32[8,128]{1,0:T(8,128)S(1)}, u32[]{:S(2)}, u32[]{:S(2)}) collective-permute-start(f32[8,128]{1,0:T(8,128)S(1)} %get-tuple-element.66), channel_id=1, source_target_pairs={{0,4},{1,5},{2,6},{3,7},{4,0},{5,1},{6,2},{7,3},{8,12},{9,13},{10,... | collective-permute-start | bytes 12296 | tf_op jit(solution)/shard_map/ppermute | solution.py:637
  25.7 0.5 %collective-permute-done.9.rest_0_ = f32[8,128]{1,0:T(8,128)S(1)} collective-permute-done((f32[8,128]{1,0:T(8,128)S(1)}, f32[8,128]{1,0:T(8,128)S(1)}, u32[]{:S(2)}, u32[]{:S(2)}) %collective-permute-start.9) | collective-permute-done | bytes 4128 | tf_op jit(solution)/shard_map/ppermute | solution.py:648
  26.2 0.0 collective-permute-done.8.odd_in
  26.2 1.4 %collective-permute-done.7.even_in = f32[8,128]{1,0:T(8,128)S(1)} collective-permute-done((f32[8,128]{1,0:T(8,128)S(1)}, f32[8,128]{1,0:T(8,128)S(1)}, u32[]{:S(2)}, u32[]{:S(2)}) %collective-permute-start.7) | collective-permute-done | bytes 4128 | tf_op jit(solution)/shard_map/ppermute | solution.py:637
  27.6 1.2 %shard_map.162 = (f32[4,256]{1,0:T(4,128)}, f32[8,512]{1,0:T(8,128)S(1)}, f32[8,128]{1,0:T(8,128)S(1)}, f32[8,128]{1,0:T(8,128)S(1)}) custom-call(f32[112,512]{1,0:T(8,128)S(1)} %get-tuple-element.61.operator, f32[8,512]{1,0:T(8,128)S(1)} %get-tuple-element.62.source, f32[8,512]{1,0:T(8,128)S(1)} %get-tuple-element.63.weights, ...), custom_call_target="tpu_custom_call" | custom-call | tf_op jit(solution)/shard_map/pallas_call | solution.py:179
  28.8 0.0 collective-permute-start.11
  28.8 4.1 %collective-permute-start.10 = (f32[8,128]{1,0:T(8,128)S(1)}, f32[8,128]{1,0:T(8,128)S(1)}, u32[]{:S(2)}, u32[]{:S(2)}) collective-permute-start(f32[8,128]{1,0:T(8,128)S(1)} %get-tuple-element.75), channel_id=1, source_target_pairs={{0,4},{1,5},{2,6},{3,7},{4,0},{5,1},{6,2},{7,3},{8,12},{9,13},{10,... | collective-permute-start | bytes 12296 | tf_op jit(solution)/shard_map/ppermute | solution.py:637
  32.9 1.5 %collective-permute-start.12 = (f32[8,128]{1,0:T(8,128)S(1)}, f32[8,128]{1,0:T(8,128)S(1)}, u32[]{:S(2)}, u32[]{:S(2)}) collective-permute-start(f32[8,128]{1,0:T(8,128)S(1)} %get-tuple-element.76), channel_id=1, source_target_pairs={{0,1},{1,0},{2,3},{3,2},{4,5},{5,4},{6,7},{7,6},{8,9},{9,8},{10,11... | collective-permute-start | bytes 12296 | tf_op jit(solution)/shard_map/ppermute | solution.py:648
  34.3 1.0 %shard_map.163 = (f32[112,128]{1,0:T(8,128)S(1)}, f32[8,128]{1,0:T(8,128)S(1)}) custom-call(f32[112,512]{1,0:T(8,128)S(1)} %get-tuple-element.61.operator, f32[16,512]{1,0:T(8,128)S(1)} %get-tuple-element.70.prolong, s32[7,512]{1,0:T(8,128)S(1)} %get-tuple-element.65.columns, s32[7,512]{1,0:T(8,128)S(1)} %get-tuple-element.73.slots, ...), custom_call_target="tpu_custom_call" | custom-call | flops 1000000000 | tf_op jit(solution)/shard_map/pallas_call | solution.py:179
  35.3 1.1 %collective-permute-done.12.rest_0_ = f32[8,128]{1,0:T(8,128)S(1)} collective-permute-done((f32[8,128]{1,0:T(8,128)S(1)}, f32[8,128]{1,0:T(8,128)S(1)}, u32[]{:S(2)}, u32[]{:S(2)}) %collective-permute-start.12) | collective-permute-done | bytes 4128 | tf_op jit(solution)/shard_map/ppermute | solution.py:648
  36.5 0.0 collective-permute-done.11.odd_in
  36.5 0.0 collective-permute-done.10.even_in
  36.5 1.0 %shard_map.164 = (f32[8,128]{1,0:T(8,128)S(1)}, f32[8,128]{1,0:T(8,128)S(1)}, f32[8,128]{1,0:T(8,128)S(1)}, f32[8,128]{1,0:T(8,128)S(1)}) custom-call(f32[112,512]{1,0:T(8,128)S(1)} %get-tuple-element.61.operator, f32[8,512]{1,0:T(8,128)S(1)} %get-tuple-element.62.source, f32[8,512]{1,0:T(8,128)S(1)} %get-tuple-element.69.second_ref, ...), custom_call_target="tpu_custom_call" | custom-call | tf_op jit(solution)/shard_map/pallas_call | solution.py:179
  37.5 0.0 collective-permute-start.13
  37.5 2.0 %collective-permute-start.16 = (f32[8,128]{1,0:T(8,128)S(1)}, f32[8,128]{1,0:T(8,128)S(1)}, u32[]{:S(2)}, u32[]{:S(2)}) collective-permute-start(f32[8,128]{1,0:T(8,128)S(1)} %get-tuple-element.82), channel_id=1, source_target_pairs={{0,4},{1,5},{2,6},{3,7},{4,0},{5,1},{6,2},{7,3},{8,12},{9,13},{10,... | collective-permute-start | bytes 12296 | tf_op jit(solution)/shard_map/ppermute | solution.py:590
  39.5 1.0 %collective-permute-start.15 = (f32[8,128]{1,0:T(8,128)S(1)}, f32[8,128]{1,0:T(8,128)S(1)}, u32[]{:S(2)}, u32[]{:S(2)}) collective-permute-start(f32[8,128]{1,0:T(8,128)S(1)} %get-tuple-element.82), channel_id=1, source_target_pairs={{0,5},{1,4},{2,14},{3,15},{4,1},{5,0},{6,10},{7,11},{8,13},{9,12},... | collective-permute-start | bytes 12296 | tf_op jit(solution)/shard_map/ppermute | solution.py:590
  40.5 0.5 %collective-permute-start.14 = (f32[8,128]{1,0:T(8,128)S(1)}, f32[8,128]{1,0:T(8,128)S(1)}, u32[]{:S(2)}, u32[]{:S(2)}) collective-permute-start(f32[8,128]{1,0:T(8,128)S(1)} %get-tuple-element.82), channel_id=1, source_target_pairs={{0,1},{1,0},{2,6},{3,7},{4,5},{5,4},{6,2},{7,3},{8,9},{9,8},{10,18... | collective-permute-start | bytes 12296 | tf_op jit(solution)/shard_map/ppermute | solution.py:590
  41.0 0.1 collective-permute-done.13.rest_0_
  41.1 0.0 collective-permute-done.16.rest_3_
  41.1 2.9 %collective-permute-done.15.rest_2_ = f32[8,128]{1,0:T(8,128)S(1)} collective-permute-done((f32[8,128]{1,0:T(8,128)S(1)}, f32[8,128]{1,0:T(8,128)S(1)}, u32[]{:S(2)}, u32[]{:S(2)}) %collective-permute-start.15) | collective-permute-done | bytes 4128 | tf_op jit(solution)/shard_map/ppermute | solution.py:590
  44.0 0.1 collective-permute-done.14.rest_1_
  44.1 0.4 shard_map.165.own
  44.4 0.0 collective-permute-start.17
  44.4 1.2 %collective-permute-done.17.other = f32[8,128]{1,0:T(8,128)S(1)} collective-permute-done((f32[8,128]{1,0:T(8,128)S(1)}, f32[8,128]{1,0:T(8,128)S(1)}, u32[]{:S(2)}, u32[]{:S(2)}) %collective-permute-start.17) | collective-permute-done | bytes 4128 | tf_op jit(solution)/shard_map/ppermute | solution.py:637
  45.6 0.7 %shard_map.166 = f32[4,32]{1,0:T(4,128)} custom-call(f32[8,128]{1,0:T(8,128)S(1)} %get-tuple-element.77.source, f32[8,128]{1,0:T(8,128)S(1)} %get-tuple-element.74.weights_two.weights, f32[8,128]{1,0:T(8,128)S(1)} %get-tuple-element.78.first_two, f32[8,128]{1,0:T(8,128)S(1)} %shard_map.165.own, f32[8,128]{1,0:T(8,128)S(1)} %collective-permute-done.17.other), custom_call_target="tpu_custom_call" | custom-call | tf_op jit(solution)/shard_map/pallas_call | solution.py:179
Async XLA Ops:
  2.8 5.2 %collective-permute-start.1 = (f32[24,640]{1,0:T(8,128)S(1)}, f32[24,640]{1,0:T(8,128)S(1)}, u32[]{:S(2)}, u32[]{:S(2)}) collective-permute-start(f32[24,640]{1,0:T(8,128)S(1)} %get-tuple-element.50), channel_id=1, source_target_pairs={{0,1},{1,0},{2,4},{3,5},{4,2},{5,3},{6,8},{7,9},{8,6},{9,7},{10,12... | collective-permute-start | bytes 184328 | tf_op jit(solution)/shard_map/ppermute | solution.py:637
  5.8 4.2 %collective-permute-start.2 = (f32[24,640]{1,0:T(8,128)S(1)}, f32[24,640]{1,0:T(8,128)S(1)}, u32[]{:S(2)}, u32[]{:S(2)}) collective-permute-start(f32[24,640]{1,0:T(8,128)S(1)} %get-tuple-element.51), channel_id=1, source_target_pairs={{0,1},{1,0},{2,3},{3,2},{4,5},{5,4},{6,7},{7,6},{8,9},{9,8},{10,11... | collective-permute-start | bytes 184328 | tf_op jit(solution)/shard_map/ppermute | solution.py:648
  5.9 2.2 %collective-permute-start = (f32[24,512]{1,0:T(8,128)S(1)}, f32[24,512]{1,0:T(8,128)S(1)}, u32[]{:S(2)}, u32[]{:S(2)}) collective-permute-start(f32[24,512]{1,0:T(8,128)S(1)} %get-tuple-element.49), channel_id=1, source_target_pairs={{0,2},{1,3},{2,0},{3,1},{4,6},{5,7},{6,4},{7,5},{8,10},{9,11},{10,... | collective-permute-start | bytes 147464 | tf_op jit(solution)/shard_map/ppermute | solution.py:637
  12.1 6.9 %collective-permute-start.4 = (f32[8,512]{1,0:T(8,128)S(1)}, f32[8,512]{1,0:T(8,128)S(1)}, u32[]{:S(2)}, u32[]{:S(2)}) collective-permute-start(f32[8,512]{1,0:T(8,128)S(1)} %get-tuple-element.58), channel_id=1, source_target_pairs={{0,1},{1,0},{2,4},{3,5},{4,2},{5,3},{6,8},{7,9},{8,6},{9,7},{10,12... | collective-permute-start | bytes 49160 | tf_op jit(solution)/shard_map/ppermute | solution.py:637
  13.4 5.6 %collective-permute-start.5 = (f32[8,512]{1,0:T(8,128)S(1)}, f32[8,512]{1,0:T(8,128)S(1)}, u32[]{:S(2)}, u32[]{:S(2)}) collective-permute-start(f32[8,512]{1,0:T(8,128)S(1)} %get-tuple-element.59), channel_id=1, source_target_pairs={{0,1},{1,0},{2,3},{3,2},{4,5},{5,4},{6,7},{7,6},{8,9},{9,8},{10,11... | collective-permute-start | bytes 49160 | tf_op jit(solution)/shard_map/ppermute | solution.py:648
  14.1 4.9 %collective-permute-start.3 = (f32[8,768]{1,0:T(8,128)S(1)}, f32[8,768]{1,0:T(8,128)S(1)}, u32[]{:S(2)}, u32[]{:S(2)}) collective-permute-start(f32[8,768]{1,0:T(8,128)S(1)} %get-tuple-element.57), channel_id=1, source_target_pairs={{0,2},{1,3},{2,0},{3,1},{4,6},{5,7},{6,4},{7,5},{8,10},{9,11},{10,... | collective-permute-start | bytes 73736 | tf_op jit(solution)/shard_map/ppermute | solution.py:637
  20.7 1.5 %collective-permute-start.6 = (f32[120,256]{1,0:T(8,128)S(1)}, f32[120,256]{1,0:T(8,128)S(1)}, u32[]{:S(2)}, u32[]{:S(2)}) collective-permute-start(f32[120,256]{1,0:T(8,128)S(1)} %shard_map.160.own), channel_id=1, source_target_pairs={{0,2},{1,3},{2,0},{3,1},{4,6},{5,7},{6,4},{7,5},{8,10},{9,11},{10,... | collective-permute-start | bytes 368648 | tf_op jit(solution)/shard_map/ppermute | solution.py:637
  22.5 3.6 %collective-permute-start.9 = (f32[8,128]{1,0:T(8,128)S(1)}, f32[8,128]{1,0:T(8,128)S(1)}, u32[]{:S(2)}, u32[]{:S(2)}) collective-permute-start(f32[8,128]{1,0:T(8,128)S(1)} %get-tuple-element.67), channel_id=1, source_target_pairs={{0,1},{1,0},{2,3},{3,2},{4,5},{5,4},{6,7},{7,6},{8,9},{9,8},{10,11... | collective-permute-start | bytes 12296 | tf_op jit(solution)/shard_map/ppermute | solution.py:648
  23.9 2.3 %collective-permute-start.8 = (f32[8,128]{1,0:T(8,128)S(1)}, f32[8,128]{1,0:T(8,128)S(1)}, u32[]{:S(2)}, u32[]{:S(2)}) collective-permute-start(f32[8,128]{1,0:T(8,128)S(1)} %get-tuple-element.66), channel_id=1, source_target_pairs={{0,2},{1,3},{2,0},{3,1},{4,8},{5,9},{6,10},{7,11},{8,4},{9,5},{10,... | collective-permute-start | bytes 12296 | tf_op jit(solution)/shard_map/ppermute | solution.py:637
  24.0 3.6 %collective-permute-start.7 = (f32[8,128]{1,0:T(8,128)S(1)}, f32[8,128]{1,0:T(8,128)S(1)}, u32[]{:S(2)}, u32[]{:S(2)}) collective-permute-start(f32[8,128]{1,0:T(8,128)S(1)} %get-tuple-element.66), channel_id=1, source_target_pairs={{0,4},{1,5},{2,6},{3,7},{4,0},{5,1},{6,2},{7,3},{8,12},{9,13},{10,... | collective-permute-start | bytes 12296 | tf_op jit(solution)/shard_map/ppermute | solution.py:637
  28.8 7.7 %collective-permute-start.11 = (f32[8,128]{1,0:T(8,128)S(1)}, f32[8,128]{1,0:T(8,128)S(1)}, u32[]{:S(2)}, u32[]{:S(2)}) collective-permute-start(f32[8,128]{1,0:T(8,128)S(1)} %get-tuple-element.75), channel_id=1, source_target_pairs={{0,2},{1,3},{2,0},{3,1},{4,8},{5,9},{6,10},{7,11},{8,4},{9,5},{10,... | collective-permute-start | bytes 12296 | tf_op jit(solution)/shard_map/ppermute | solution.py:637
  28.8 7.7 %collective-permute-start.10 = (f32[8,128]{1,0:T(8,128)S(1)}, f32[8,128]{1,0:T(8,128)S(1)}, u32[]{:S(2)}, u32[]{:S(2)}) collective-permute-start(f32[8,128]{1,0:T(8,128)S(1)} %get-tuple-element.75), channel_id=1, source_target_pairs={{0,4},{1,5},{2,6},{3,7},{4,0},{5,1},{6,2},{7,3},{8,12},{9,13},{10,... | collective-permute-start | bytes 12296 | tf_op jit(solution)/shard_map/ppermute | solution.py:637
  32.9 3.6 %collective-permute-start.12 = (f32[8,128]{1,0:T(8,128)S(1)}, f32[8,128]{1,0:T(8,128)S(1)}, u32[]{:S(2)}, u32[]{:S(2)}) collective-permute-start(f32[8,128]{1,0:T(8,128)S(1)} %get-tuple-element.76), channel_id=1, source_target_pairs={{0,1},{1,0},{2,3},{3,2},{4,5},{5,4},{6,7},{7,6},{8,9},{9,8},{10,11... | collective-permute-start | bytes 12296 | tf_op jit(solution)/shard_map/ppermute | solution.py:648
  37.5 3.6 %collective-permute-start.13 = (f32[8,128]{1,0:T(8,128)S(1)}, f32[8,128]{1,0:T(8,128)S(1)}, u32[]{:S(2)}, u32[]{:S(2)}) collective-permute-start(f32[8,128]{1,0:T(8,128)S(1)} %get-tuple-element.81), channel_id=1, source_target_pairs={{0,4},{1,5},{2,10},{3,11},{4,0},{5,1},{6,14},{7,15},{8,12},{9,13},... | collective-permute-start | bytes 12296 | tf_op jit(solution)/shard_map/ppermute | solution.py:590
  37.5 3.6 %collective-permute-start.16 = (f32[8,128]{1,0:T(8,128)S(1)}, f32[8,128]{1,0:T(8,128)S(1)}, u32[]{:S(2)}, u32[]{:S(2)}) collective-permute-start(f32[8,128]{1,0:T(8,128)S(1)} %get-tuple-element.82), channel_id=1, source_target_pairs={{0,4},{1,5},{2,6},{3,7},{4,0},{5,1},{6,2},{7,3},{8,12},{9,13},{10,... | collective-permute-start | bytes 12296 | tf_op jit(solution)/shard_map/ppermute | solution.py:590
  39.5 4.5 %collective-permute-start.15 = (f32[8,128]{1,0:T(8,128)S(1)}, f32[8,128]{1,0:T(8,128)S(1)}, u32[]{:S(2)}, u32[]{:S(2)}) collective-permute-start(f32[8,128]{1,0:T(8,128)S(1)} %get-tuple-element.82), channel_id=1, source_target_pairs={{0,5},{1,4},{2,14},{3,15},{4,1},{5,0},{6,10},{7,11},{8,13},{9,12},... | collective-permute-start | bytes 12296 | tf_op jit(solution)/shard_map/ppermute | solution.py:590
  40.5 3.6 %collective-permute-start.14 = (f32[8,128]{1,0:T(8,128)S(1)}, f32[8,128]{1,0:T(8,128)S(1)}, u32[]{:S(2)}, u32[]{:S(2)}) collective-permute-start(f32[8,128]{1,0:T(8,128)S(1)} %get-tuple-element.82), channel_id=1, source_target_pairs={{0,1},{1,0},{2,6},{3,7},{4,5},{5,4},{6,2},{7,3},{8,9},{9,8},{10,18... | collective-permute-start | bytes 12296 | tf_op jit(solution)/shard_map/ppermute | solution.py:590
  44.4 1.2 %collective-permute-start.17 = (f32[8,128]{1,0:T(8,128)S(1)}, f32[8,128]{1,0:T(8,128)S(1)}, u32[]{:S(2)}, u32[]{:S(2)}) collective-permute-start(f32[8,128]{1,0:T(8,128)S(1)} %shard_map.165.own), channel_id=1, source_target_pairs={{0,2},{1,3},{2,0},{3,1},{4,6},{5,7},{6,4},{7,5},{8,10},{9,11},{10,... | collective-permute-start | bytes 12296 | tf_op jit(solution)/shard_map/ppermute | solution.py:637

commit v3 on v2

--- a/solution.py
+++ b/solution.py
@@ -11,6 +11,20 @@
 GY = 8
 GZ = 32
 LANES = 128
+OWN_SLOTS = 7
+FINE_FIRST = (0, 1, 2)
+FINE_SECOND = (0, 1, 2)
+PAIR_FIRST = (0, 1, 2)
+PAIR_SECOND = (0, 1, 2)
+GROUP = (0, 3, 2, 1)
+
+
+def ordered(values, order):
+    return [values[at] for at in order] + list(values[len(order) :])
+
+
+def restored(refs, order):
+    return [refs[order.index(at)] for at in range(len(order))] + list(refs[len(order) :])
 F32 = jnp.float32
 BF16 = jnp.bfloat16
 
@@ -83,8 +97,12 @@
     return choose_four(matmul(table, onehot(columns)), columns >> 7)
 
 
+def gather_halves(table, columns, chunk):
+    return choose_sixteen(matmul(table, onehot(columns)), (columns >> 7) - chunk)
+
+
 def gather_sixteen(table, columns):
-    return jnp.concatenate(choose_sixteen(matmul(table, onehot(columns)), columns >> 7), axis=0)
+    return jnp.concatenate(gather_halves(table, columns, 0), axis=0)
 
 
 def sum_components(value):
@@ -199,31 +217,35 @@
     count = handed + 3
     raw, refs = refs[:count], refs[count:]
     kept, refs = refs[:handed], refs[handed:]
-    operator, prolong, prolong_one, w_ref, first_ref, parity_out, cross_out = refs[:7]
+    operator_raw, prolong, prolong_one, w_ref, first_ref, parity_out, cross_out = refs[:7]
     slab_outs, refs = refs[7 : 7 + slab_moves], refs[7 + slab_moves :]
-    operator_raw, prolong_raw, prolong_one_raw, picks, semaphores = refs
+    prolong_raw, prolong_one_raw, picks, semaphores, slot_semaphores = refs
     source, sends, sends_one = kept[0], kept[1], kept[2]
-    targets = [operator_raw, source, prolong_raw, sends, prolong_one_raw, sends_one, *kept[3:]]
+    targets = [source, prolong_raw, sends, prolong_one_raw, sends_one, *kept[3:]]
+    slot_copies = [
+        pltpu.make_async_copy(raw[0].at[k], operator_raw.at[k], slot_semaphores.at[k])
+        for k in range(7)
+    ]
     copies = [
         pltpu.make_async_copy(
-            raw[at], target if raw[at].ndim > 1 else target.at[0], semaphores.at[at]
+            value, target if value.ndim > 1 else target.at[0], semaphores.at[at]
         )
-        for at, target in enumerate(targets)
+        for at, (value, target) in enumerate(zip(raw[1:], targets))
     ]
-    for copy in copies:
+    for copy in slot_copies + copies:
         copy.start()
-    copies[0].wait()
     sums = [None] * 4
     for k in range(7):
+        slot_copies[k].wait()
         for a in range(4):
             value = jnp.abs(operator_raw[k, a])
             sums[a] = value if sums[a] is None else sums[a] + value
     weights = 1.0 + sum_components(jnp.concatenate(sums, axis=0))
-    copies[1].wait()
+    copies[0].wait()
     first = twice(source[...]) / weights
     w_ref[...] = weights
     first_ref[...] = first
-    for at in range(2, 6):
+    for at in range(1, 5):
         copies[at].wait()
     for half in range(2):
         at = slice(8 * half, 8 * half + 8)
@@ -261,14 +283,26 @@
         out[:, 0:count] = jnp.where(up, high_first, low_first)
         out[0:16, count:] = jnp.where(up, coarse[:, LANES : 2 * LANES], coarse[:, 0:LANES])
         out[16:24, count:] = jnp.zeros((8, LANES), F32)
+    for copy in copies[5:]:
+        copy.wait()
+
+
+def fine_own(operator_raw, prolong, columns, operator, own_near):
+    table = table_sixteen(chunks_of(prolong[...]))
+
+    def step(at):
+        for k in range(own_near.shape[0] // 16):
+            low, high = gather_halves(table, columns[k : k + 1, at], 0)
+            own_near[16 * k : 16 * k + 8, at] = low
+            own_near[16 * k + 8 : 16 * k + 16, at] = high
+
+    tiles(columns.shape[1], 512, step)
     for k in range(7):
         for half in range(2):
             row = 16 * k + 8 * half
             operator[row : row + 8] = jnp.concatenate(
                 [operator_raw[k, 2 * half], operator_raw[k, 2 * half + 1]], axis=0
             )
-    for copy in copies[6:]:
-        copy.wait()
 
 
 def fine_ghosts(rows, count, sizes, parity_in, cross_in, slab_ins):
@@ -290,12 +324,13 @@
 
 
 def fine_second(
-    sizes, source, operator, columns, sends, w_ref, first_ref, parity_in, cross_in, *rest
+    sizes, source, operator, columns, sends, w_ref, first_ref, *rest
 ):
-    slab_count = (len(rest) - 5) // 2
-    slab_ins, rest = rest[:slab_count], rest[slab_count:]
-    smoothed, parity_out, cross_out = rest[0], rest[1], rest[2]
-    slab_outs, second_ref, picks = rest[3:-2], rest[-2], rest[-1]
+    slab_count = (len(rest) - 6) // 2
+    taken, rest = restored(rest[: slab_count + 2], FINE_FIRST), rest[slab_count + 2 :]
+    parity_in, cross_in, *slab_ins = taken
+    parity_out, cross_out = rest[0], rest[1]
+    slab_outs, second_ref, picks = rest[2:-2], rest[-2], rest[-1]
     count = sends.shape[1] // 4
     ghosts = fine_ghosts(slice(0, 8), count, sizes, parity_in, cross_in, slab_ins)
     table = table_four(chunks_of(first_ref[...]) + ghosts)
@@ -305,7 +340,6 @@
         second_ref[:, at] = first_ref[:, at] + residual / w_ref[:, at]
 
     tiles(source.shape[1], 1024, step)
-    smoothed[...] = second_ref[0:4]
     table = table_four(chunks_of(second_ref[...]))
 
     def pick(at):
@@ -326,15 +360,24 @@
         out[...] = jnp.where(up, high_first, low_first)
 
 
-def coarsen(table, operator, prolong, columns, slots, aggregates, sums, count):
+def coarsen(tables, operator, prolong, columns, slots, aggregates, sums, count, own_near=None):
     tile = 512
+    whole = jnp.concatenate(tables, axis=0)
+    known = 0 if own_near is None else own_near.shape[0] // 16
 
     def step(at):
         wide_prolong = expand(prolong[:, at])
         totals = [[jnp.zeros((8, tile), F32) for _ in range(2)] for _ in range(7)]
         for k in range(7):
             column = columns[k : k + 1, at]
-            near = choose_sixteen(matmul(table, onehot(column)), column >> 7)
+            if k < known:
+                near = gather_halves(tables[1], column, tables[0].shape[0] // 16)
+                near = [
+                    near[half] + own_near[16 * k + 8 * half : 16 * k + 8 * half + 8, at]
+                    for half in range(2)
+                ]
+            else:
+                near = gather_halves(whole, column, 0)
             blocks = triple_product(wide_prolong, operator[16 * k : 16 * k + 16, at], near)
             slot = jnp.broadcast_to(slots[k : k + 1, at], (8, tile))
             for s in range(7):
@@ -351,14 +394,24 @@
 
 
 def fine_coarsen(
-    sizes, operator, prolong, columns, slots, aggregates, second_ref, parity_old, cross_old, *rest
+    sizes,
+    operator,
+    prolong,
+    columns,
+    slots,
+    aggregates,
+    own_near,
+    second_ref,
+    parity_old,
+    cross_old,
+    *rest,
 ):
     slab_old, (out, sums) = rest[:-2], rest[-2:]
     count = parity_old.shape[1]
     ghosts = fine_ghosts(slice(8, 24), count, sizes, parity_old, cross_old, slab_old)
-    table = table_sixteen(chunks_of(prolong[...]) + ghosts)
+    tables = [table_sixteen(chunks_of(prolong[...])), table_sixteen(ghosts)]
     out[...] = coarsen(
-        table, operator, prolong, columns, slots, aggregates, sums, out.shape[1]
+        tables, operator, prolong, columns, slots, aggregates, sums, out.shape[1], own_near
     )
 
 
@@ -371,11 +424,10 @@
     aggregates,
     second_ref,
     operator_own,
-    parity_in,
-    cross_in,
     *rest,
 ):
-    slab_ins, (out, lifted) = rest[:-2], rest[-2:]
+    parity_in, cross_in, *slab_ins = restored(rest[:-2], FINE_SECOND)
+    out, lifted = rest[-2:]
     ghosts = fine_ghosts(slice(0, 8), cross_in.shape[1], sizes, parity_in, cross_in, slab_ins)
     table = table_four(chunks_of(second_ref[...]) + ghosts)
 
@@ -421,12 +473,13 @@
 
 
 def pair_second(
-    sizes, operator, source, weights, first, columns, sends, even_in, odd_in, *rest
+    sizes, operator, source, weights, first, columns, sends, *rest
 ):
-    slab_count = (len(rest) - 3) // 2
-    slab_ins, rest = rest[:slab_count], rest[slab_count:]
-    smoothed, second_ref, group_out = rest[0], rest[1], rest[2]
-    slab_outs = rest[3:]
+    slab_count = (len(rest) - 4) // 2
+    taken, rest = restored(rest[: slab_count + 2], PAIR_FIRST), rest[slab_count + 2 :]
+    even_in, odd_in, *slab_ins = taken
+    second_ref, group_out = rest[0], rest[1]
+    slab_outs = rest[2:]
     table = table_four(chunks_of(first[...]) + pair_ghosts(sizes, even_in, odd_in, slab_ins))
 
     def step(at):
@@ -435,8 +488,6 @@
 
     tiles(source.shape[1], 512, step)
     sub, slab = place()
-    half = smoothed.shape[1]
-    smoothed[...] = jnp.where(sub % 2 == 0, second_ref[0:4, 0:half], second_ref[0:4, half:])
     picks = gather_four(table_four(chunks_of(second_ref[...])), sends[...])
     group_out[...] = picks[:, 2 * LANES :]
     slab_faces(picks, slab, slab_outs)
@@ -449,14 +500,20 @@
     columns,
     slots,
     aggregates,
+    second_fine,
+    second_ref,
     parity_old,
     cross_old,
     forwarded,
     *rest,
 ):
-    slab_old, (operator_two, weights_two, sums) = rest[:-3], rest[-3:]
+    slab_old, rest = rest[:-5], rest[-5:]
+    operator_two, weights_two, smoothed, smoothed_one, sums = rest
     sub, slab = place()
     even = sub % 2 == 0
+    half = smoothed_one.shape[1]
+    smoothed[...] = second_fine[0:4]
+    smoothed_one[...] = jnp.where(even, second_ref[0:4, 0:half], second_ref[0:4, half:])
     count = parity_old.shape[1]
     values = [ref[0:16, count:] for ref in slab_old] + [None]
     below, above = neighbours(slab, sizes[1], values[0], values[1])
@@ -470,9 +527,9 @@
     left = jnp.where(group > 0, left, jnp.zeros_like(left))
     right = jnp.where(group < sizes[0] // 2 - 1, right, jnp.zeros_like(right))
     ghosts = [below, above, swap_halves(left, right, LANES // 2)]
-    table = table_sixteen(chunks_of(prolong[...]) + ghosts)
+    tables = [table_sixteen(chunks_of(prolong[...])), table_sixteen(ghosts)]
     operator_two[...] = coarsen(
-        table, operator, prolong, columns, slots, aggregates, sums, LANES
+        tables, operator, prolong, columns, slots, aggregates, sums, LANES
     )
     weights_two[...] = row_weights(lambda k: operator_two[16 * k : 16 * k + 16])
 
@@ -487,12 +544,11 @@
     aggregates,
     sends,
     weights_two,
-    even_in,
-    odd_in,
     *rest,
 ):
-    slab_count = (len(rest) - 4) // 2
-    slab_ins, rest = rest[:slab_count], rest[slab_count:]
+    slab_count = (len(rest) - 6) // 2
+    taken, rest = restored(rest[: slab_count + 2], PAIR_SECOND), rest[slab_count + 2 :]
+    even_in, odd_in, *slab_ins = taken
     source_two, first_two, whole_out = rest[:3]
     slab_outs, lifted = rest[3:-1], rest[-1]
     sub, slab = place()
@@ -519,21 +575,20 @@
     def sent(value):
         return jnp.where(lane < half, value, seconds)
 
-    whole_out[...] = sent(first)
     slab_even = slab % 2 == 0
     for position, out in enumerate(slab_outs):
         up = slab_even if position == 0 else jnp.logical_not(slab_even)
         out[...] = sent(jnp.where(up, pltpu.roll(faces, half, 1), faces))
+    whole_out[...] = jnp.where(sub % 2 == 0, sent(first), slab_outs[0][...])
 
 
 def group_apply(sizes, operator, first_two, columns, *rest):
-    received, out = rest[:-1], rest[-1]
+    received, out = restored(rest[:-1], GROUP), rest[-1]
     sub, slab = place()
     group, pair = sub // 4, sub // 2 % 2
     even = sub % 2 == 0
     half = LANES // 2
     lane = lax.broadcasted_iota(jnp.int32, (8, LANES), 1)
-    none = jnp.zeros((8, LANES), F32)
 
     def left_part(value):
         return jnp.where(lane < half, value, 0.0)
@@ -542,23 +597,20 @@
     first = jnp.where(
         pair == 0, mine + pltpu.roll(other, half, 1), other + pltpu.roll(mine, half, 1)
     )
-    first = jnp.where(even, first, none)
-
-    odd = received[3][...] + received[4][...] if len(received) > 4 else None
-    below, above = neighbours(slab, sizes[1], received[1][...] + received[2][...], odd)
-    firsts = jnp.where(even, left_part(below) + pltpu.roll(left_part(above), half, 1), none)
-
-    left, right = neighbours(
-        group,
-        sizes[0] // 4,
-        received[0][...] + received[2][...],
-        received[1][...] + received[3][...],
-    )
+    first = jnp.where(even, first, jnp.zeros_like(first))
+
+    slab_even = jnp.where(even, received[1][...], received[0][...])
+    slab_odd = received[4][...] if len(received) > 4 else None
+    below, above = neighbours(slab, sizes[1], slab_even, slab_odd)
+    firsts = left_part(below) + pltpu.roll(left_part(above), half, 1)
+
+    group_even = jnp.where(even, received[2][...], received[1][...])
+    group_odd = jnp.where(even, received[3][...], received[2][...])
+    left, right = neighbours(group, sizes[0] // 4, group_even, group_odd)
     width = GX // 4 * (GZ // 4)
     left = pltpu.roll(left, LANES - half - width, 1)
     right = pltpu.roll(right, LANES - half + width, 1)
     seconds = jnp.where(lane < width, left, jnp.where(lane < 2 * width, right, 0.0))
-    seconds = jnp.where(even, none, seconds)
 
     table = table_four([first, firsts, seconds])
     mine = jnp.where(pair == 0, columns[...], pltpu.roll(columns[...], half, 1))
@@ -578,14 +630,14 @@
     out[...] = jnp.where(sub % 2 == 0, second[0:4, 0:share], second[0:4, share : 2 * share])
 
 
-def swap_by_core(value, even_mate, odd_mate):
+def swap_by_core(value, even_mate, odd_mate, spare=2):
     subs, slabs = lax.axis_size("sub"), lax.axis_size("slab")
     route = []
     for sub in range(subs):
         for slab in range(slabs):
             target = (even_mate if sub % 2 == 0 else odd_mate)(sub, slab)
             if not (0 <= target[0] < subs and 0 <= target[1] < slabs):
-                target = (sub ^ 2, slab)
+                target = (sub ^ spare, slab)
             route.append((sub * slabs + slab, target[0] * slabs + target[1]))
     return lax.ppermute(value, ("sub", "slab"), route)
 
@@ -608,19 +660,20 @@
     def pair(sub, slab):
         return sub ^ 2, slab
 
+    def idle(sub, slab):
+        inside = 0 <= odd_mate_of(sub // 4) < lax.axis_size("sub") // 4
+        return sub ^ (2 if inside else 1), slab
+
     first = slab_values[0]
     received = [
-        swap_by_core(whole, pair, along_sub(False, 0)),
-        swap_by_core(first, along_slab(False, 0), along_sub(True, 0)),
-        swap_by_core(first, along_slab(False, 2), along_sub(False, 2)),
+        swap_by_core(whole, pair, along_slab(False, 2)),
+        swap_by_core(first, along_slab(False, 0), along_sub(False, 2)),
+        swap_by_core(first, along_sub(False, 0), along_sub(True, 2)),
+        swap_by_core(first, along_sub(True, 0), idle, spare=1),
     ]
-    if len(slab_values) == 1:
-        return received + [swap_by_core(first, pair, along_sub(True, 2))]
-    second = slab_values[1]
-    return received + [
-        swap_by_core(second, along_slab(True, 0), along_sub(True, 2)),
-        swap_by_core(second, along_slab(True, 2), pair),
-    ]
+    for value in slab_values[1:]:
+        received.append(swap_by_core(value, along_slab(True, 0), along_slab(True, 2)))
+    return received
 
 
 def sub_pairing(value, group, odd):
@@ -692,29 +745,37 @@
     out = call(
         functools.partial(fine_first, handed, slab_moves),
         [((1, value.shape[0]) if value.ndim == 1 else value.shape, value.dtype) for value in kept]
-        + [(112, rows), (16, rows), (16, pair_rows_one)]
+        + [operator.shape, (16, rows), (16, pair_rows_one)]
         + [(8, rows), (8, rows), (24, count), (24, count + LANES)]
         + [(24, count + LANES)] * slab_moves,
         *[pltpu.with_memory_space_constraint(value, pltpu.HBM) for value in raw],
         scratch=[
-            pltpu.VMEM(operator.shape, F32),
             pltpu.VMEM(prolong.shape, F32),
             pltpu.VMEM(prolong_one.shape, F32),
             pltpu.VMEM((24, rows), F32),
-            pltpu.SemaphoreType.DMA((len(raw),)),
+            pltpu.SemaphoreType.DMA((len(raw) - 1,)),
+            pltpu.SemaphoreType.DMA((7,)),
         ],
         space=pltpu.HBM,
     )
     source, sends, sends_one, columns, slots, aggregates = out[:6]
     columns_one, slots_one, aggregates_one, columns_two, sends_two = out[6:11]
-    operator, prolong, prolong_one, weights, first, even, odd, *slabs = out[11:]
+    operator_raw, prolong, prolong_one, weights, first, even, odd, *slabs = out[11:]
     even_old = sub_pairing(even, 1, False)
     odd_old = sub_pairing(odd, 1, True)
     slabs_old = slab_pairings(slabs)
 
-    smoothed, even, odd, *rest = call(
+    operator, own_near = call(
+        fine_own,
+        [(112, rows), (16 * OWN_SLOTS, rows)],
+        operator_raw,
+        prolong,
+        columns,
+        flops=10**9,
+    )
+    even, odd, *rest = call(
         functools.partial(fine_second, sizes),
-        [(4, rows), (8, count + 2 * LANES), (8, count)]
+        [(8, count + 2 * LANES), (8, count)]
         + [(8, count)] * slab_moves
         + [(8, rows)],
         source,
@@ -723,9 +784,7 @@
         sends,
         weights,
         first,
-        even_old,
-        odd_old,
-        *slabs_old,
+        *ordered([even_old, odd_old, *slabs_old], FINE_FIRST),
         scratch=[pltpu.VMEM((8, sends.shape[1]), F32)],
     )
     slabs, second = rest[:-1], rest[-1]
@@ -741,6 +800,7 @@
         columns,
         slots,
         aggregates,
+        own_near,
         second,
         even_old,
         odd_old,
@@ -758,9 +818,7 @@
         aggregates,
         second,
         operator_own,
-        forwarded,
-        odd_in,
-        *slabs_in,
+        *ordered([forwarded, odd_in, *slabs_in], FINE_SECOND),
         scratch=[pltpu.VMEM((8, rows), F32)],
     )
     other = sub_pairing(own, 1, False)
@@ -777,14 +835,31 @@
     odd_in = sub_pairing(group_out, 2, True)
     slabs_in = slab_pairings(slabs)
 
-    operator_two, weights_two = call(
+    second_one, group_out, *slabs = call(
+        functools.partial(pair_second, sizes),
+        [(8, pair_rows_one)] + faces,
+        operator_one,
+        source_one,
+        weights_one,
+        first_one,
+        columns_one,
+        sends_one,
+        *ordered([even_in, odd_in, *slabs_in], PAIR_FIRST),
+    )
+    even_in = sub_pairing(group_out, 2, False)
+    odd_in = sub_pairing(group_out, 2, True)
+    slabs_in = slab_pairings(slabs)
+
+    operator_two, weights_two, smoothed, smoothed_one = call(
         functools.partial(pair_coarsen, sizes),
-        [(112, LANES), (8, LANES)],
+        [(112, LANES), (8, LANES), (4, rows), (4, rows_one)],
         operator_one,
         prolong_one,
         columns_one,
         slots_one,
         aggregates_one,
+        second,
+        second_one,
         even_old,
         odd_old,
         forwarded,
@@ -792,23 +867,6 @@
         scratch=[pltpu.VMEM((112, pair_rows_one), F32)],
         flops=10**9,
     )
-    smoothed_one, second_one, group_out, *slabs = call(
-        functools.partial(pair_second, sizes),
-        [(4, rows_one), (8, pair_rows_one)] + faces,
-        operator_one,
-        source_one,
-        weights_one,
-        first_one,
-        columns_one,
-        sends_one,
-        even_in,
-        odd_in,
-        *slabs_in,
-    )
-    even_in = sub_pairing(group_out, 2, False)
-    odd_in = sub_pairing(group_out, 2, True)
-    slabs_in = slab_pairings(slabs)
-
     source_two, first_two, whole, *slabs = call(
         functools.partial(pair_restrict, sizes),
         [(8, LANES), (8, LANES)] + faces,
@@ -820,9 +878,7 @@
         aggregates_one,
         sends_two,
         weights_two,
-        even_in,
-        odd_in,
-        *slabs_in,
+        *ordered([even_in, odd_in, *slabs_in], PAIR_SECOND),
         scratch=[pltpu.VMEM((8, pair_rows_one), F32)],
     )
     received = group_exchange(whole, slabs)
@@ -832,7 +888,7 @@
         operator_two,
         first_two,
         columns_two,
-        *received,
+        *ordered(received, GROUP),
     )
     applied_other = sub_pairing(applied, 1, False)
     (smoothed_two,) = call(

time: 46.4 us -> 43.3 us (0.933); the launches traced: 46.3 us -> 42.7 us
  waiting for transfers between devices: 11.1 us -> 8.53 us
  starting transfers between devices: 19.2 us -> 17.9 us
    ppermute x4, waiting for transfers between devices: 3.07 us -> 1.89 us  [swap_by_core(): return lax.ppermute(value, ('sub', 'slab'), route)]
    ppermute x4, waiting for transfers between devices: 3.59 us -> 2.66 us  [slab_pairing(): return lax.ppermute(value, ('sub', 'slab'), route)]
    ppermute x10, starting transfers between devices: 12.1 us -> 11.3 us  [sub_pairing(): return lax.ppermute(value, ('sub', 'slab'), route)]
    pallas_call x10 -> x11, Pallas kernels: 15.3 us -> 15.5 us  [call(): pl.pallas_call(body, out_shape=[jax.ShapeDtypeStruct(shape, dtype) for sh...]
  transfers between devices with their start and end apart: 18 -> 18, of which waited for: 10 -> 7; matrix products, arithmetic and copies ran while one was open for 0% -> 0% of each run, Pallas kernels for 13% -> 16%
where the time goes in v3:
time: 43.3 us; the launch traced here: 42.7 us
  starting transfers between devices  17.9 us (41%)
  Pallas kernels  15.5 us (36%)
  waiting for transfers between devices  8.53 us (20%)
  between operations  0.72 us (2%)
    pallas_call x11, Pallas kernels, call(): pl.pallas_call(body, out_shape=[jax.ShapeDtypeStruct(shape, dtype) for sh...  15.5 us
    ppermute x10, starting transfers between devices, sub_pairing(): return lax.ppermute(value, ('sub', 'slab'), route)  11.3 us
    ppermute x10, waiting for transfers between devices, sub_pairing(): return lax.ppermute(value, ('sub', 'slab'), route)  3.98 us
    ppermute x4, starting transfers between devices, slab_pairing(): return lax.ppermute(value, ('sub', 'slab'), route)  3.38 us
    ppermute x4, starting transfers between devices, swap_by_core(): return lax.ppermute(value, ('sub', 'slab'), route)  3.23 us
    ppermute x4, waiting for transfers between devices, slab_pairing(): return lax.ppermute(value, ('sub', 'slab'), route)  2.66 us
    ppermute x4, waiting for transfers between devices, swap_by_core(): return lax.ppermute(value, ('sub', 'slab'), route)  1.89 us
  transfers between devices with their start and end apart: 18, of which 7 were waited for; matrix products, arithmetic and copies ran while one was open for 0% of the time, Pallas kernels for 16%

profile of v3, /device:TPU:0, one launch (start us, length us, event | category | flops | bytes accessed | tf_op | source)
XLA Modules:
  0.0 42.7 jit_solution(10696835452313768579)
XLA Ops:
  0.6 2.3 %shard_map.157 = (f32[4,2048]{1,0:T(4,128)S(1)}, s32[1,2048]{1,0:T(1,128)S(1)}, s32[1,384]{1,0:T(1,128)S(1)}, s32[7,2048]{1,0:T(8,128)S(1)}, s32[7,2048]{1,0:T(8...) custom-call(f32[7,4,4,2048]{3,2,1,0:T(4,128)} %refs_0_.1, ...), custom_call_target="tpu_custom_call" | custom-call | tf_op jit(solution)/shard_map/pallas_call | solution.py:197
  3.0 0.5 %collective-permute-start = (f32[24,512]{1,0:T(8,128)S(1)}, f32[24,512]{1,0:T(8,128)S(1)}, u32[]{:S(2)}, u32[]{:S(2)}) collective-permute-start(f32[24,512]{1,0:T(8,128)S(1)} %get-tuple-element.54), channel_id=1, source_target_pairs={{0,2},{1,3},{2,0},{3,1},{4,6},{5,7},{6,4},{7,5},{8,10},{9,11},{10,... | collective-permute-start | bytes 147464 | tf_op jit(solution)/shard_map/ppermute | solution.py:690
  3.5 2.6 %collective-permute-start.1 = (f32[24,640]{1,0:T(8,128)S(1)}, f32[24,640]{1,0:T(8,128)S(1)}, u32[]{:S(2)}, u32[]{:S(2)}) collective-permute-start(f32[24,640]{1,0:T(8,128)S(1)} %get-tuple-element.55), channel_id=1, source_target_pairs={{0,1},{1,0},{2,4},{3,5},{4,2},{5,3},{6,8},{7,9},{8,6},{9,7},{10,12... | collective-permute-start | bytes 184328 | tf_op jit(solution)/shard_map/ppermute | solution.py:690
  6.1 0.1 collective-permute-start.2
  6.1 2.1 %shard_map.158 = (f32[112,2048]{1,0:T(8,128)S(1)}, f32[112,2048]{1,0:T(8,128)S(1)}) custom-call(f32[7,4,4,2048]{3,2,1,0:T(4,128)S(1)} %get-tuple-element.46.operator_raw, f32[16,2048]{1,0:T(8,128)S(1)} %get-tuple-element.47.prolong, s32[7,2048]{1,0:T(8,128)S(1)} %get-tuple-element.48.columns), custom_call_target="tpu_custom_call" | custom-call | flops 1000000000 | tf_op jit(solution)/shard_map/pallas_call | solution.py:197
  8.3 0.0 collective-permute-done.rest_0_.parity_old
  8.3 0.0 collective-permute-done.1.rest_1_.cross_old
  8.3 2.0 %collective-permute-done.2.rest_2_.rest_0_ = f32[24,640]{1,0:T(8,128)S(1)} collective-permute-done((f32[24,640]{1,0:T(8,128)S(1)}, f32[24,640]{1,0:T(8,128)S(1)}, u32[]{:S(2)}, u32[]{:S(2)}) %collective-permute-start.2) | collective-permute-done | bytes 61472 | tf_op jit(solution)/shard_map/ppermute | solution.py:701
  10.3 1.7 %shard_map.159 = (f32[8,768]{1,0:T(8,128)S(1)}, f32[8,512]{1,0:T(8,128)S(1)}, f32[8,512]{1,0:T(8,128)S(1)}, f32[8,2048]{1,0:T(8,128)S(1)}) custom-call(f32[4,2048]{1,0:T(4,128)S(1)} %get-tuple-element.45.source, f32[112,2048]{1,0:T(8,128)S(1)} %get-tuple-element.49.operator, s32[7,2048]{1,0:T(8,128)S(1)} %get-tuple-element.48.columns, ...), custom_call_target="tpu_custom_call" | custom-call | tf_op jit(solution)/shard_map/pallas_call | solution.py:197
  12.0 1.4 %collective-permute-start.4 = (f32[8,512]{1,0:T(8,128)S(1)}, f32[8,512]{1,0:T(8,128)S(1)}, u32[]{:S(2)}, u32[]{:S(2)}) collective-permute-start(f32[8,512]{1,0:T(8,128)S(1)} %get-tuple-element.61), channel_id=1, source_target_pairs={{0,1},{1,0},{2,4},{3,5},{4,2},{5,3},{6,8},{7,9},{8,6},{9,7},{10,12... | collective-permute-start | bytes 49160 | tf_op jit(solution)/shard_map/ppermute | solution.py:690
  13.4 0.7 %collective-permute-start.5 = (f32[8,512]{1,0:T(8,128)S(1)}, f32[8,512]{1,0:T(8,128)S(1)}, u32[]{:S(2)}, u32[]{:S(2)}) collective-permute-start(f32[8,512]{1,0:T(8,128)S(1)} %get-tuple-element.62), channel_id=1, source_target_pairs={{0,1},{1,0},{2,3},{3,2},{4,5},{5,4},{6,7},{7,6},{8,9},{9,8},{10,11... | collective-permute-start | bytes 49160 | tf_op jit(solution)/shard_map/ppermute | solution.py:701
  14.1 0.4 collective-permute-start.3
  14.5 3.1 %shard_map.160.operator_own = f32[112,256]{1,0:T(8,128)S(1)} custom-call(f32[112,2048]{1,0:T(8,128)S(1)} %get-tuple-element.49.operator, f32[16,2048]{1,0:T(8,128)S(1)} %get-tuple-element.47.prolong, s32[7,2048]{1,0:T(8,128)S(1)} %get-tuple-element.48.columns, s32[7,2048]{1,0:T(8,128)S(1)} %get-tuple-element.58.slots, ...), custom_call_target="tpu_custom_call" | custom-call | flops 4000000000 | tf_op jit(solution)/shard_map/pallas_call | solution.py:197
  17.6 0.0 collective-permute-done.4.rest_1_
  17.6 0.0 collective-permute-done.5.rest_2_
  17.6 0.0 collective-permute-done.3.rest_0_.forwarded
  17.6 1.7 %shard_map.161.own = f32[120,256]{1,0:T(8,128)S(1)} custom-call(f32[4,2048]{1,0:T(4,128)S(1)} %get-tuple-element.45.source, f32[112,2048]{1,0:T(8,128)S(1)} %get-tuple-element.49.operator, f32[16,2048]{1,0:T(8,128)S(1)} %get-tuple-element.47.prolong, s32[7,2048]{1,0:T(8,128)S(1)} %get-tuple-element.48.columns, s32[1,2048]{1,0:T(1,128)S(1)} %get-tuple-element.50.aggregates, ...), custom_call_target="tpu_custom_call" | custom-call | tf_op jit(solution)/shard_map/pallas_call | solution.py:197
  19.4 0.1 collective-permute-start.6
  19.5 1.2 %collective-permute-done.6.other = f32[120,256]{1,0:T(8,128)S(1)} collective-permute-done((f32[120,256]{1,0:T(8,128)S(1)}, f32[120,256]{1,0:T(8,128)S(1)}, u32[]{:S(2)}, u32[]{:S(2)}) %collective-permute-start.6) | collective-permute-done | bytes 122912 | tf_op jit(solution)/shard_map/ppermute | solution.py:690
  20.7 0.3 shard_map.162
  21.0 1.1 %collective-permute-start.9 = (f32[8,128]{1,0:T(8,128)S(1)}, f32[8,128]{1,0:T(8,128)S(1)}, u32[]{:S(2)}, u32[]{:S(2)}) collective-permute-start(f32[8,128]{1,0:T(8,128)S(1)} %get-tuple-element.73), channel_id=1, source_target_pairs={{0,1},{1,0},{2,3},{3,2},{4,5},{5,4},{6,7},{7,6},{8,9},{9,8},{10,11... | collective-permute-start | bytes 12296 | tf_op jit(solution)/shard_map/ppermute | solution.py:701
  22.1 0.1 collective-permute-start.8
  22.2 2.4 %collective-permute-start.7 = (f32[8,128]{1,0:T(8,128)S(1)}, f32[8,128]{1,0:T(8,128)S(1)}, u32[]{:S(2)}, u32[]{:S(2)}) collective-permute-start(f32[8,128]{1,0:T(8,128)S(1)} %get-tuple-element.72), channel_id=1, source_target_pairs={{0,4},{1,5},{2,6},{3,7},{4,0},{5,1},{6,2},{7,3},{8,12},{9,13},{10,... | collective-permute-start | bytes 12296 | tf_op jit(solution)/shard_map/ppermute | solution.py:690
  24.6 0.0 collective-permute-done.9.rest_2_
  24.7 0.0 collective-permute-done.8.rest_1_
  24.7 1.6 %collective-permute-done.7.rest_0_ = f32[8,128]{1,0:T(8,128)S(1)} collective-permute-done((f32[8,128]{1,0:T(8,128)S(1)}, f32[8,128]{1,0:T(8,128)S(1)}, u32[]{:S(2)}, u32[]{:S(2)}) %collective-permute-start.7) | collective-permute-done | bytes 4128 | tf_op jit(solution)/shard_map/ppermute | solution.py:690
  26.2 0.7 %shard_map.163 = (f32[8,512]{1,0:T(8,128)S(1)}, f32[8,128]{1,0:T(8,128)S(1)}, f32[8,128]{1,0:T(8,128)S(1)}) custom-call(f32[112,512]{1,0:T(8,128)S(1)} %get-tuple-element.64.operator, f32[8,512]{1,0:T(8,128)S(1)} %get-tuple-element.69.source, f32[8,512]{1,0:T(8,128)S(1)} %get-tuple-element.70.weights, f32[8,512]{1,0:T(8,128)S(1)} %get-tuple-element.71.first, ...), custom_call_target="tpu_custom_call" | custom-call | tf_op jit(solution)/shard_map/pallas_call | solution.py:197
  26.9 0.0 collective-permute-start.11
  26.9 3.8 %collective-permute-start.10 = (f32[8,128]{1,0:T(8,128)S(1)}, f32[8,128]{1,0:T(8,128)S(1)}, u32[]{:S(2)}, u32[]{:S(2)}) collective-permute-start(f32[8,128]{1,0:T(8,128)S(1)} %get-tuple-element.79), channel_id=1, source_target_pairs={{0,4},{1,5},{2,6},{3,7},{4,0},{5,1},{6,2},{7,3},{8,12},{9,13},{10,... | collective-permute-start | bytes 12296 | tf_op jit(solution)/shard_map/ppermute | solution.py:690
  30.7 1.5 %collective-permute-start.12 = (f32[8,128]{1,0:T(8,128)S(1)}, f32[8,128]{1,0:T(8,128)S(1)}, u32[]{:S(2)}, u32[]{:S(2)}) collective-permute-start(f32[8,128]{1,0:T(8,128)S(1)} %get-tuple-element.80), channel_id=1, source_target_pairs={{0,1},{1,0},{2,3},{3,2},{4,5},{5,4},{6,7},{7,6},{8,9},{9,8},{10,11... | collective-permute-start | bytes 12296 | tf_op jit(solution)/shard_map/ppermute | solution.py:701
  32.2 1.5 %shard_map.164 = (f32[112,128]{1,0:T(8,128)S(1)}, f32[8,128]{1,0:T(8,128)S(1)}, f32[4,2048]{1,0:T(4,128)}, f32[4,256]{1,0:T(4,128)}) custom-call(f32[112,512]{1,0:T(8,128)S(1)} %get-tuple-element.64.operator, f32[16,512]{1,0:T(8,128)S(1)} %get-tuple-element.65.prolong, s32[7,512]{1,0:T(8,128)S(1)} %get-tuple-element.66.columns, ...), custom_call_target="tpu_custom_call" | custom-call | flops 1000000000 | tf_op jit(solution)/shard_map/pallas_call | solution.py:197
  33.7 0.6 %collective-permute-done.12.rest_2_ = f32[8,128]{1,0:T(8,128)S(1)} collective-permute-done((f32[8,128]{1,0:T(8,128)S(1)}, f32[8,128]{1,0:T(8,128)S(1)}, u32[]{:S(2)}, u32[]{:S(2)}) %collective-permute-start.12) | collective-permute-done | bytes 4128 | tf_op jit(solution)/shard_map/ppermute | solution.py:701
  34.3 0.0 collective-permute-done.11.rest_1_
  34.3 0.0 collective-permute-done.10.rest_0_
  34.3 1.0 %shard_map.165 = (f32[8,128]{1,0:T(8,128)S(1)}, f32[8,128]{1,0:T(8,128)S(1)}, f32[8,128]{1,0:T(8,128)S(1)}, f32[8,128]{1,0:T(8,128)S(1)}) custom-call(f32[112,512]{1,0:T(8,128)S(1)} %get-tuple-element.64.operator, f32[8,512]{1,0:T(8,128)S(1)} %get-tuple-element.69.source, f32[8,512]{1,0:T(8,128)S(1)} %get-tuple-element.74.second_ref, ...), custom_call_target="tpu_custom_call" | custom-call | tf_op jit(solution)/shard_map/pallas_call | solution.py:197
  35.3 0.0 collective-permute-start.13
  35.3 1.5 %collective-permute-start.16 = (f32[8,128]{1,0:T(8,128)S(1)}, f32[8,128]{1,0:T(8,128)S(1)}, u32[]{:S(2)}, u32[]{:S(2)}) collective-permute-start(f32[8,128]{1,0:T(8,128)S(1)} %get-tuple-element.86), channel_id=1, source_target_pairs={{0,1},{1,0},{2,14},{3,15},{4,5},{5,4},{6,10},{7,11},{8,9},{9,8},{1... | collective-permute-start | bytes 12296 | tf_op jit(solution)/shard_map/ppermute | solution.py:642
  36.8 1.7 %collective-permute-start.15 = (f32[8,128]{1,0:T(8,128)S(1)}, f32[8,128]{1,0:T(8,128)S(1)}, u32[]{:S(2)}, u32[]{:S(2)}) collective-permute-start(f32[8,128]{1,0:T(8,128)S(1)} %get-tuple-element.86), channel_id=1, source_target_pairs={{0,8},{1,9},{2,6},{3,7},{4,12},{5,13},{6,2},{7,3},{8,0},{9,1},{10,... | collective-permute-start | bytes 12296 | tf_op jit(solution)/shard_map/ppermute | solution.py:642
  38.6 0.0 collective-permute-start.14
  38.6 0.4 collective-permute-done.13.rest_0_
  38.9 0.0 collective-permute-done.16.rest_3_
  39.0 1.5 %collective-permute-done.15.rest_2_ = f32[8,128]{1,0:T(8,128)S(1)} collective-permute-done((f32[8,128]{1,0:T(8,128)S(1)}, f32[8,128]{1,0:T(8,128)S(1)}, u32[]{:S(2)}, u32[]{:S(2)}) %collective-permute-start.15) | collective-permute-done | bytes 4128 | tf_op jit(solution)/shard_map/ppermute | solution.py:642
  40.4 0.0 collective-permute-done.14.rest_1_
  40.4 0.4 shard_map.166.own
  40.8 0.0 collective-permute-start.17
  40.8 1.2 %collective-permute-done.17.other = f32[8,128]{1,0:T(8,128)S(1)} collective-permute-done((f32[8,128]{1,0:T(8,128)S(1)}, f32[8,128]{1,0:T(8,128)S(1)}, u32[]{:S(2)}, u32[]{:S(2)}) %collective-permute-start.17) | collective-permute-done | bytes 4128 | tf_op jit(solution)/shard_map/ppermute | solution.py:690
  42.0 0.7 %shard_map.167 = f32[4,32]{1,0:T(4,128)} custom-call(f32[8,128]{1,0:T(8,128)S(1)} %get-tuple-element.81.source, f32[8,128]{1,0:T(8,128)S(1)} %get-tuple-element.78.weights_two.weights, f32[8,128]{1,0:T(8,128)S(1)} %get-tuple-element.82.first_two, f32[8,128]{1,0:T(8,128)S(1)} %shard_map.166.own, f32[8,128]{1,0:T(8,128)S(1)} %collective-permute-done.17.other), custom_call_target="tpu_custom_call" | custom-call | tf_op jit(solution)/shard_map/pallas_call | solution.py:197
Async XLA Ops:
  3.0 5.3 %collective-permute-start = (f32[24,512]{1,0:T(8,128)S(1)}, f32[24,512]{1,0:T(8,128)S(1)}, u32[]{:S(2)}, u32[]{:S(2)}) collective-permute-start(f32[24,512]{1,0:T(8,128)S(1)} %get-tuple-element.54), channel_id=1, source_target_pairs={{0,2},{1,3},{2,0},{3,1},{4,6},{5,7},{6,4},{7,5},{8,10},{9,11},{10,... | collective-permute-start | bytes 147464 | tf_op jit(solution)/shard_map/ppermute | solution.py:690
  3.5 4.8 %collective-permute-start.1 = (f32[24,640]{1,0:T(8,128)S(1)}, f32[24,640]{1,0:T(8,128)S(1)}, u32[]{:S(2)}, u32[]{:S(2)}) collective-permute-start(f32[24,640]{1,0:T(8,128)S(1)} %get-tuple-element.55), channel_id=1, source_target_pairs={{0,1},{1,0},{2,4},{3,5},{4,2},{5,3},{6,8},{7,9},{8,6},{9,7},{10,12... | collective-permute-start | bytes 184328 | tf_op jit(solution)/shard_map/ppermute | solution.py:690
  6.1 4.2 %collective-permute-start.2 = (f32[24,640]{1,0:T(8,128)S(1)}, f32[24,640]{1,0:T(8,128)S(1)}, u32[]{:S(2)}, u32[]{:S(2)}) collective-permute-start(f32[24,640]{1,0:T(8,128)S(1)} %get-tuple-element.56), channel_id=1, source_target_pairs={{0,1},{1,0},{2,3},{3,2},{4,5},{5,4},{6,7},{7,6},{8,9},{9,8},{10,11... | collective-permute-start | bytes 184328 | tf_op jit(solution)/shard_map/ppermute | solution.py:701
  12.0 5.6 %collective-permute-start.4 = (f32[8,512]{1,0:T(8,128)S(1)}, f32[8,512]{1,0:T(8,128)S(1)}, u32[]{:S(2)}, u32[]{:S(2)}) collective-permute-start(f32[8,512]{1,0:T(8,128)S(1)} %get-tuple-element.61), channel_id=1, source_target_pairs={{0,1},{1,0},{2,4},{3,5},{4,2},{5,3},{6,8},{7,9},{8,6},{9,7},{10,12... | collective-permute-start | bytes 49160 | tf_op jit(solution)/shard_map/ppermute | solution.py:690
  13.4 4.3 %collective-permute-start.5 = (f32[8,512]{1,0:T(8,128)S(1)}, f32[8,512]{1,0:T(8,128)S(1)}, u32[]{:S(2)}, u32[]{:S(2)}) collective-permute-start(f32[8,512]{1,0:T(8,128)S(1)} %get-tuple-element.62), channel_id=1, source_target_pairs={{0,1},{1,0},{2,3},{3,2},{4,5},{5,4},{6,7},{7,6},{8,9},{9,8},{10,11... | collective-permute-start | bytes 49160 | tf_op jit(solution)/shard_map/ppermute | solution.py:701
  14.1 3.6 %collective-permute-start.3 = (f32[8,768]{1,0:T(8,128)S(1)}, f32[8,768]{1,0:T(8,128)S(1)}, u32[]{:S(2)}, u32[]{:S(2)}) collective-permute-start(f32[8,768]{1,0:T(8,128)S(1)} %get-tuple-element.60), channel_id=1, source_target_pairs={{0,2},{1,3},{2,0},{3,1},{4,6},{5,7},{6,4},{7,5},{8,10},{9,11},{10,... | collective-permute-start | bytes 73736 | tf_op jit(solution)/shard_map/ppermute | solution.py:690
  19.4 1.4 %collective-permute-start.6 = (f32[120,256]{1,0:T(8,128)S(1)}, f32[120,256]{1,0:T(8,128)S(1)}, u32[]{:S(2)}, u32[]{:S(2)}) collective-permute-start(f32[120,256]{1,0:T(8,128)S(1)} %shard_map.161.own), channel_id=1, source_target_pairs={{0,2},{1,3},{2,0},{3,1},{4,6},{5,7},{6,4},{7,5},{8,10},{9,11},{10,... | collective-permute-start | bytes 368648 | tf_op jit(solution)/shard_map/ppermute | solution.py:690
  21.0 3.6 %collective-permute-start.9 = (f32[8,128]{1,0:T(8,128)S(1)}, f32[8,128]{1,0:T(8,128)S(1)}, u32[]{:S(2)}, u32[]{:S(2)}) collective-permute-start(f32[8,128]{1,0:T(8,128)S(1)} %get-tuple-element.73), channel_id=1, source_target_pairs={{0,1},{1,0},{2,3},{3,2},{4,5},{5,4},{6,7},{7,6},{8,9},{9,8},{10,11... | collective-permute-start | bytes 12296 | tf_op jit(solution)/shard_map/ppermute | solution.py:701
  22.1 2.5 %collective-permute-start.8 = (f32[8,128]{1,0:T(8,128)S(1)}, f32[8,128]{1,0:T(8,128)S(1)}, u32[]{:S(2)}, u32[]{:S(2)}) collective-permute-start(f32[8,128]{1,0:T(8,128)S(1)} %get-tuple-element.72), channel_id=1, source_target_pairs={{0,2},{1,3},{2,0},{3,1},{4,8},{5,9},{6,10},{7,11},{8,4},{9,5},{10,... | collective-permute-start | bytes 12296 | tf_op jit(solution)/shard_map/ppermute | solution.py:690
  22.2 4.0 %collective-permute-start.7 = (f32[8,128]{1,0:T(8,128)S(1)}, f32[8,128]{1,0:T(8,128)S(1)}, u32[]{:S(2)}, u32[]{:S(2)}) collective-permute-start(f32[8,128]{1,0:T(8,128)S(1)} %get-tuple-element.72), channel_id=1, source_target_pairs={{0,4},{1,5},{2,6},{3,7},{4,0},{5,1},{6,2},{7,3},{8,12},{9,13},{10,... | collective-permute-start | bytes 12296 | tf_op jit(solution)/shard_map/ppermute | solution.py:690
  26.9 7.4 %collective-permute-start.11 = (f32[8,128]{1,0:T(8,128)S(1)}, f32[8,128]{1,0:T(8,128)S(1)}, u32[]{:S(2)}, u32[]{:S(2)}) collective-permute-start(f32[8,128]{1,0:T(8,128)S(1)} %get-tuple-element.79), channel_id=1, source_target_pairs={{0,2},{1,3},{2,0},{3,1},{4,8},{5,9},{6,10},{7,11},{8,4},{9,5},{10,... | collective-permute-start | bytes 12296 | tf_op jit(solution)/shard_map/ppermute | solution.py:690
  26.9 7.4 %collective-permute-start.10 = (f32[8,128]{1,0:T(8,128)S(1)}, f32[8,128]{1,0:T(8,128)S(1)}, u32[]{:S(2)}, u32[]{:S(2)}) collective-permute-start(f32[8,128]{1,0:T(8,128)S(1)} %get-tuple-element.79), channel_id=1, source_target_pairs={{0,4},{1,5},{2,6},{3,7},{4,0},{5,1},{6,2},{7,3},{8,12},{9,13},{10,... | collective-permute-start | bytes 12296 | tf_op jit(solution)/shard_map/ppermute | solution.py:690
  30.7 3.6 %collective-permute-start.12 = (f32[8,128]{1,0:T(8,128)S(1)}, f32[8,128]{1,0:T(8,128)S(1)}, u32[]{:S(2)}, u32[]{:S(2)}) collective-permute-start(f32[8,128]{1,0:T(8,128)S(1)} %get-tuple-element.80), channel_id=1, source_target_pairs={{0,1},{1,0},{2,3},{3,2},{4,5},{5,4},{6,7},{7,6},{8,9},{9,8},{10,11... | collective-permute-start | bytes 12296 | tf_op jit(solution)/shard_map/ppermute | solution.py:701
  35.3 3.6 %collective-permute-start.13 = (f32[8,128]{1,0:T(8,128)S(1)}, f32[8,128]{1,0:T(8,128)S(1)}, u32[]{:S(2)}, u32[]{:S(2)}) collective-permute-start(f32[8,128]{1,0:T(8,128)S(1)} %get-tuple-element.85), channel_id=1, source_target_pairs={{0,4},{1,5},{2,7},{3,6},{4,0},{5,1},{6,3},{7,2},{8,12},{9,13},{10,... | collective-permute-start | bytes 12296 | tf_op jit(solution)/shard_map/ppermute | solution.py:642
  35.3 3.6 %collective-permute-start.16 = (f32[8,128]{1,0:T(8,128)S(1)}, f32[8,128]{1,0:T(8,128)S(1)}, u32[]{:S(2)}, u32[]{:S(2)}) collective-permute-start(f32[8,128]{1,0:T(8,128)S(1)} %get-tuple-element.86), channel_id=1, source_target_pairs={{0,1},{1,0},{2,14},{3,15},{4,5},{5,4},{6,10},{7,11},{8,9},{9,8},{1... | collective-permute-start | bytes 12296 | tf_op jit(solution)/shard_map/ppermute | solution.py:642
  36.8 3.6 %collective-permute-start.15 = (f32[8,128]{1,0:T(8,128)S(1)}, f32[8,128]{1,0:T(8,128)S(1)}, u32[]{:S(2)}, u32[]{:S(2)}) collective-permute-start(f32[8,128]{1,0:T(8,128)S(1)} %get-tuple-element.86), channel_id=1, source_target_pairs={{0,8},{1,9},{2,6},{3,7},{4,12},{5,13},{6,2},{7,3},{8,0},{9,1},{10,... | collective-permute-start | bytes 12296 | tf_op jit(solution)/shard_map/ppermute | solution.py:642
  38.6 1.9 %collective-permute-start.14 = (f32[8,128]{1,0:T(8,128)S(1)}, f32[8,128]{1,0:T(8,128)S(1)}, u32[]{:S(2)}, u32[]{:S(2)}) collective-permute-start(f32[8,128]{1,0:T(8,128)S(1)} %get-tuple-element.86), channel_id=1, source_target_pairs={{0,2},{1,3},{2,0},{3,1},{4,6},{5,7},{6,4},{7,5},{8,16},{9,17},{10,... | collective-permute-start | bytes 12296 | tf_op jit(solution)/shard_map/ppermute | solution.py:642
  40.8 1.2 %collective-permute-start.17 = (f32[8,128]{1,0:T(8,128)S(1)}, f32[8,128]{1,0:T(8,128)S(1)}, u32[]{:S(2)}, u32[]{:S(2)}) collective-permute-start(f32[8,128]{1,0:T(8,128)S(1)} %shard_map.166.own), channel_id=1, source_target_pairs={{0,2},{1,3},{2,0},{3,1},{4,6},{5,7},{6,4},{7,5},{8,10},{9,11},{10,... | collective-permute-start | bytes 12296 | tf_op jit(solution)/shard_map/ppermute | solution.py:690

commit v4 on v3

--- a/solution.py
+++ b/solution.py
@@ -14,8 +14,6 @@
 OWN_SLOTS = 7
 FINE_FIRST = (0, 1, 2)
 FINE_SECOND = (0, 1, 2)
-PAIR_FIRST = (0, 1, 2)
-PAIR_SECOND = (0, 1, 2)
 GROUP = (0, 3, 2, 1)
 
 
@@ -123,19 +121,23 @@
     return 1.0 + sum_components(total)
 
 
-def spread_row(value, row, rows=8):
-    return jnp.broadcast_to(value[row : row + 1], (rows, value.shape[1]))
-
-
 def lift(prolong, residual):
-    low = pair_rows(spread_row(residual, 0), spread_row(residual, 1))
-    high = pair_rows(spread_row(residual, 2), spread_row(residual, 3))
+    second = upper_half(residual.shape).astype(jnp.int32)
+    low = jnp.take_along_axis(residual, second, axis=0)
+    high = jnp.take_along_axis(residual, second + 2, axis=0)
     return fold(prolong[:8] * low + prolong[8:] * high)
 
 
 def expand(rows):
+    shape = (8, rows.shape[1])
+    second = upper_half(shape).astype(jnp.int32)
     return [
-        [pair_rows(spread_row(rows, 4 * a + 2 * h), spread_row(rows, 4 * a + 2 * h + 1)) for h in (0, 1)]
+        [
+            jnp.take_along_axis(
+                rows[8 * (a // 2) : 8 * (a // 2) + 8], second + (4 * (a % 2) + 2 * h), axis=0
+            )
+            for h in (0, 1)
+        ]
         for a in range(4)
     ]
 
@@ -151,11 +153,18 @@
     return out
 
 
+def onehot_rows(targets, count):
+    shape = (count, targets.shape[1])
+    here = lax.broadcasted_iota(jnp.int32, shape, 0) == jnp.broadcast_to(targets, shape)
+    return here.astype(F32).astype(BF16)
+
+
 def scatter(values, targets, count):
+    return add_up(values, onehot_rows(targets, count))
+
+
+def add_up(values, hot):
     high, low = split(values)
-    shape = (count, values.shape[1])
-    hot = lax.broadcasted_iota(jnp.int32, shape, 0) == jnp.broadcast_to(targets, shape)
-    hot = hot.astype(F32).astype(BF16)
     both = lax.dot_general(
         jnp.concatenate([high, low], axis=0),
         hot,
@@ -219,21 +228,55 @@
     kept, refs = refs[:handed], refs[handed:]
     operator_raw, prolong, prolong_one, w_ref, first_ref, parity_out, cross_out = refs[:7]
     slab_outs, refs = refs[7 : 7 + slab_moves], refs[7 + slab_moves :]
-    prolong_raw, prolong_one_raw, picks, semaphores, slot_semaphores = refs
+    prolong_raw, prolong_one_raw, picks, wide_picks, semaphores, slot_semaphores = refs
     source, sends, sends_one = kept[0], kept[1], kept[2]
-    targets = [source, prolong_raw, sends, prolong_one_raw, sends_one, *kept[3:]]
+    targets = [prolong_raw, sends, prolong_one_raw, sends_one, source, *kept[3:]]
+    sources = [raw[2], raw[3], raw[4], raw[5], raw[1], *raw[6:]]
+    copies = [
+        pltpu.make_async_copy(
+            value, target if value.ndim > 1 else target.at[0], semaphores.at[at]
+        )
+        for at, (value, target) in enumerate(zip(sources, targets))
+    ]
     slot_copies = [
         pltpu.make_async_copy(raw[0].at[k], operator_raw.at[k], slot_semaphores.at[k])
         for k in range(7)
     ]
-    copies = [
-        pltpu.make_async_copy(
-            value, target if value.ndim > 1 else target.at[0], semaphores.at[at]
+    for copy in copies[:5] + slot_copies + copies[5:]:
+        copy.start()
+
+    copies[0].wait()
+    copies[1].wait()
+    for half in range(2):
+        at = slice(8 * half, 8 * half + 8)
+        prolong[at] = jnp.concatenate([prolong_raw[2 * half], prolong_raw[2 * half + 1]], axis=0)
+    wide_table = table_sixteen(chunks_of(prolong[...]))
+
+    def pick_wide(at):
+        wide_picks[:, at] = gather_sixteen(wide_table, sends[:, at])
+
+    tiles(sends.shape[1], 512, pick_wide)
+    copies[2].wait()
+    copies[3].wait()
+    for half in range(2):
+        at = slice(8 * half, 8 * half + 8)
+        prolong_one[at] = jnp.concatenate(
+            [prolong_one_raw[2 * half], prolong_one_raw[2 * half + 1]], axis=0
         )
-        for at, (value, target) in enumerate(zip(raw[1:], targets))
-    ]
-    for copy in slot_copies + copies:
-        copy.start()
+    coarse = gather_sixteen(table_sixteen(chunks_of(prolong_one[...])), sends_one[...])
+    sub, slab = place()
+    even = sub % 2 == 0
+    count = sends.shape[1] // 4
+    low_first, high_first = wide_picks[:, 0:count], wide_picks[:, count : 2 * count]
+    low_second, high_second = wide_picks[:, 2 * count : 3 * count], wide_picks[:, 3 * count :]
+    parity_out[:, 0:count] = jnp.where(even, high_second, low_second)
+    cross_out[:, 0:count] = jnp.where(even, low_second, high_second)
+    cross_out[:, count + LANES :] = coarse[:, 2 * LANES :]
+    for position, out in enumerate(slab_outs):
+        up = slab % 2 == position
+        out[:, 0:count] = jnp.where(up, high_first, low_first)
+        out[:, count + LANES :] = jnp.where(up, coarse[:, LANES : 2 * LANES], coarse[:, 0:LANES])
+
     sums = [None] * 4
     for k in range(7):
         slot_copies[k].wait()
@@ -241,50 +284,39 @@
             value = jnp.abs(operator_raw[k, a])
             sums[a] = value if sums[a] is None else sums[a] + value
     weights = 1.0 + sum_components(jnp.concatenate(sums, axis=0))
-    copies[0].wait()
+    copies[4].wait()
     first = twice(source[...]) / weights
     w_ref[...] = weights
     first_ref[...] = first
-    for at in range(1, 5):
-        copies[at].wait()
-    for half in range(2):
-        at = slice(8 * half, 8 * half + 8)
-        prolong[at] = jnp.concatenate([prolong_raw[2 * half], prolong_raw[2 * half + 1]], axis=0)
-        prolong_one[at] = jnp.concatenate(
-            [prolong_one_raw[2 * half], prolong_one_raw[2 * half + 1]], axis=0
-        )
-    table = jnp.concatenate(
-        [table_four(chunks_of(first)), table_sixteen(chunks_of(prolong[...]))], axis=0
-    )
-    split_at = first.shape[1] // LANES * 4
-
-    def pick(at):
-        columns = sends[:, at]
-        picked = matmul(table, onehot(columns))
-        picks[0:8, at] = choose_four(picked[:split_at], columns >> 7)
-        low, high = choose_sixteen(picked[split_at:], columns >> 7)
-        picks[8:16, at] = low
-        picks[16:24, at] = high
-
-    tiles(sends.shape[1], 512, pick)
-    coarse = gather_sixteen(table_sixteen(chunks_of(prolong_one[...])), sends_one[...])
-    sub, slab = place()
-    count = sends.shape[1] // 4
-    low_first, high_first = picks[:, 0:count], picks[:, count : 2 * count]
-    low_second, high_second = picks[:, 2 * count : 3 * count], picks[:, 3 * count :]
-    even = sub % 2 == 0
-    parity_out[...] = jnp.where(even, high_second, low_second)
-    cross_out[:, 0:count] = jnp.where(even, low_second, high_second)
-    cross_out[0:16, count:] = coarse[:, 2 * LANES :]
-    cross_out[16:24, count:] = jnp.zeros((8, LANES), F32)
-    slab_even = slab % 2 == 0
-    for position, out in enumerate(slab_outs):
-        up = slab_even if position == 0 else jnp.logical_not(slab_even)
-        out[:, 0:count] = jnp.where(up, high_first, low_first)
-        out[0:16, count:] = jnp.where(up, coarse[:, LANES : 2 * LANES], coarse[:, 0:LANES])
-        out[16:24, count:] = jnp.zeros((8, LANES), F32)
+    table = table_four(chunks_of(first))
+    at = slice(count, count + LANES)
+    faces = fine_faces(table, sends, picks)
+    parity, cross, slabs = chosen_faces(faces, sub, slab, len(slab_outs))
+    parity_out[:, at] = parity
+    cross_out[:, at] = cross
+    for out, value in zip(slab_outs, slabs):
+        out[:, at] = value
     for copy in copies[5:]:
         copy.wait()
+
+
+def fine_faces(table, sends, picks):
+    def pick(at):
+        picks[:, at] = gather_four(table, sends[:, at])
+
+    tiles(sends.shape[1], 1024, pick)
+    rows = [picks[0:4, at : at + LANES] for at in range(0, sends.shape[1], LANES)]
+    each = len(rows) // 4
+    return [jnp.concatenate(rows[each * at : each * at + each], axis=0) for at in range(4)]
+
+
+def chosen_faces(faces, sub, slab, slab_count):
+    low_first, high_first, low_second, high_second = faces
+    even = sub % 2 == 0
+    parity = jnp.where(even, high_second, low_second)
+    cross = jnp.where(even, low_second, high_second)
+    slabs = [jnp.where(slab % 2 == at, high_first, low_first) for at in range(slab_count)]
+    return parity, cross, slabs
 
 
 def fine_own(operator_raw, prolong, columns, operator, own_near):
@@ -305,13 +337,20 @@
             )
 
 
-def fine_ghosts(rows, count, sizes, parity_in, cross_in, slab_ins):
+def fine_ghosts(at, sizes, parity_in, cross_in, slab_ins):
     sub, slab = place()
-    at = slice(0, count)
-    slab_values = [ref[rows, at] for ref in slab_ins] + [None]
+    slab_values = [ref[:, at] for ref in slab_ins] + [None]
     below, above = neighbours(slab, sizes[1], slab_values[0], slab_values[1])
-    left, right = neighbours(sub, sizes[0], parity_in[rows, at], cross_in[rows, at])
-    return chunks_of(below) + chunks_of(above) + chunks_of(left) + chunks_of(right)
+    left, right = neighbours(sub, sizes[0], parity_in[:, at], cross_in[:, at])
+    return [below, above, left, right]
+
+
+def four_chunks(faces):
+    return [twice(face[at : at + 4]) for face in faces for at in range(0, face.shape[0], 4)]
+
+
+def sixteen_chunks(faces):
+    return [chunk for face in faces for chunk in chunks_of(face)]
 
 
 def apply_tile(table, operator, columns, at):
@@ -332,36 +371,28 @@
     parity_out, cross_out = rest[0], rest[1]
     slab_outs, second_ref, picks = rest[2:-2], rest[-2], rest[-1]
     count = sends.shape[1] // 4
-    ghosts = fine_ghosts(slice(0, 8), count, sizes, parity_in, cross_in, slab_ins)
-    table = table_four(chunks_of(first_ref[...]) + ghosts)
+    ghosts = fine_ghosts(
+        slice(count, count + LANES), sizes, parity_in, cross_in, slab_ins
+    )
+    table = table_four(chunks_of(first_ref[...]) + four_chunks(ghosts))
 
     def step(at):
         residual = twice(source[:, at]) - apply_tile(table, operator, columns, at)
         second_ref[:, at] = first_ref[:, at] + residual / w_ref[:, at]
 
-    tiles(source.shape[1], 1024, step)
-    table = table_four(chunks_of(second_ref[...]))
-
-    def pick(at):
-        picks[:, at] = gather_four(table, sends[:, at])
-
-    tiles(sends.shape[1], 1024, pick)
+    tiles(source.shape[1], source.shape[1], step)
+    faces = fine_faces(table_four(chunks_of(second_ref[...])), sends, picks)
     sub, slab = place()
-    low_first, high_first = picks[:, 0:count], picks[:, count : 2 * count]
-    low_second, high_second = picks[:, 2 * count : 3 * count], picks[:, 3 * count :]
-    even = sub % 2 == 0
-    parity_out[:, 0:count] = jnp.where(even, high_second, low_second)
-    parity_out[:, count : count + LANES] = cross_in[0:8, count:]
-    parity_out[:, count + LANES :] = cross_in[8:16, count:]
-    cross_out[...] = jnp.where(even, low_second, high_second)
-    slab_even = slab % 2 == 0
-    for position, out in enumerate(slab_outs):
-        up = slab_even if position == 0 else jnp.logical_not(slab_even)
-        out[...] = jnp.where(up, high_first, low_first)
+    parity, cross, slabs = chosen_faces(faces, sub, slab, len(slab_outs))
+    parity_out[:, 0:LANES] = parity
+    parity_out[:, LANES:] = cross_in[:, count + LANES :]
+    cross_out[...] = cross
+    for out, value in zip(slab_outs, slabs):
+        out[...] = value
 
 
 def coarsen(tables, operator, prolong, columns, slots, aggregates, sums, count, own_near=None):
-    tile = 512
+    tile = 256
     whole = jnp.concatenate(tables, axis=0)
     known = 0 if own_near is None else own_near.shape[0] // 16
 
@@ -407,9 +438,9 @@
     *rest,
 ):
     slab_old, (out, sums) = rest[:-2], rest[-2:]
-    count = parity_old.shape[1]
-    ghosts = fine_ghosts(slice(8, 24), count, sizes, parity_old, cross_old, slab_old)
-    tables = [table_sixteen(chunks_of(prolong[...])), table_sixteen(ghosts)]
+    count = parity_old.shape[1] - LANES
+    ghosts = fine_ghosts(slice(0, count), sizes, parity_old, cross_old, slab_old)
+    tables = [table_sixteen(chunks_of(prolong[...])), table_sixteen(sixteen_chunks(ghosts))]
     out[...] = coarsen(
         tables, operator, prolong, columns, slots, aggregates, sums, out.shape[1], own_near
     )
@@ -428,26 +459,27 @@
 ):
     parity_in, cross_in, *slab_ins = restored(rest[:-2], FINE_SECOND)
     out, lifted = rest[-2:]
-    ghosts = fine_ghosts(slice(0, 8), cross_in.shape[1], sizes, parity_in, cross_in, slab_ins)
-    table = table_four(chunks_of(second_ref[...]) + ghosts)
+    ghosts = fine_ghosts(slice(0, LANES), sizes, parity_in, cross_in, slab_ins)
+    table = table_four(chunks_of(second_ref[...]) + four_chunks(ghosts))
 
     def step(at):
         residual = twice(source[:, at]) - apply_tile(table, operator, columns, at)
         lifted[:, at] = lift(prolong[:, at], residual)
 
-    tiles(source.shape[1], 1024, step)
+    tiles(source.shape[1], source.shape[1], step)
     out[0:112] = operator_own[...]
     out[112:120] = scatter(lifted[...], aggregates[...], out.shape[1])
 
 
-def slab_faces(picks, slab, slab_outs):
-    slab_even = slab % 2 == 0
-    for position, out in enumerate(slab_outs):
-        up = slab_even if position == 0 else jnp.logical_not(slab_even)
-        out[...] = jnp.where(up, picks[:, LANES : 2 * LANES], picks[:, 0:LANES])
-
-
-def pair_first(own, other, sends, operator, source, weights, first, group_out, *slab_outs):
+def pair_faces(picks, sub, slab, outs):
+    for position, out in enumerate(outs):
+        face = jnp.where(
+            slab % 2 == position, picks[:, LANES : 2 * LANES], picks[:, 0:LANES]
+        )
+        out[...] = jnp.where(sub % 2 == 0, face, picks[:, 2 * LANES :])
+
+
+def pair_first(own, other, sends, operator, source, weights, first, *outs):
     sub, slab = place()
     even = sub % 2 == 0
     half = own.shape[1]
@@ -460,27 +492,26 @@
     weights[...] = row_weights(lambda k: operator[16 * k : 16 * k + 16])
     first[...] = source[...] / weights[...]
     picks = gather_four(table_four(chunks_of(first[...])), sends[...])
-    group_out[...] = picks[:, 2 * LANES :]
-    slab_faces(picks, slab, slab_outs)
-
-
-def pair_ghosts(sizes, even_in, odd_in, slab_ins):
+    pair_faces(picks, sub, slab, outs)
+
+
+def pair_ghosts(sizes, mine, other):
     sub, slab = place()
-    values = [ref[...] for ref in slab_ins] + [None]
-    below, above = neighbours(slab, sizes[1], values[0], values[1])
-    left, right = neighbours(sub // 2, sizes[0] // 2, even_in[...], odd_in[...])
+    even = sub % 2 == 0
+    mine, other = [mine[0:8], mine[8:16]], [other[0:8], other[8:16]]
+    along_slab = [jnp.where(even, mine[at], other[at]) for at in range(2)]
+    along_sub = [jnp.where(even, other[at], mine[at]) for at in range(2)]
+    below, above = neighbours(
+        slab, sizes[1], along_slab[0], along_slab[1] if sizes[1] > 2 else None
+    )
+    left, right = neighbours(sub // 2, sizes[0] // 2, along_sub[0], along_sub[1])
     return [below, above, swap_halves(left, right, LANES // 2)]
 
 
 def pair_second(
-    sizes, operator, source, weights, first, columns, sends, *rest
+    sizes, operator, source, weights, first, columns, sends, mine, other, second_ref, *outs
 ):
-    slab_count = (len(rest) - 4) // 2
-    taken, rest = restored(rest[: slab_count + 2], PAIR_FIRST), rest[slab_count + 2 :]
-    even_in, odd_in, *slab_ins = taken
-    second_ref, group_out = rest[0], rest[1]
-    slab_outs = rest[2:]
-    table = table_four(chunks_of(first[...]) + pair_ghosts(sizes, even_in, odd_in, slab_ins))
+    table = table_four(chunks_of(first[...]) + pair_ghosts(sizes, mine, other))
 
     def step(at):
         residual = source[:, at] - apply_tile(table, operator, columns, at)
@@ -489,8 +520,7 @@
     tiles(source.shape[1], 512, step)
     sub, slab = place()
     picks = gather_four(table_four(chunks_of(second_ref[...])), sends[...])
-    group_out[...] = picks[:, 2 * LANES :]
-    slab_faces(picks, slab, slab_outs)
+    pair_faces(picks, sub, slab, outs)
 
 
 def pair_coarsen(
@@ -500,6 +530,7 @@
     columns,
     slots,
     aggregates,
+    sends,
     second_fine,
     second_ref,
     parity_old,
@@ -507,20 +538,18 @@
     forwarded,
     *rest,
 ):
-    slab_old, rest = rest[:-5], rest[-5:]
-    operator_two, weights_two, smoothed, smoothed_one, sums = rest
+    slab_old, rest = rest[:-7], rest[-7:]
+    operator_two, weights_two, face_weights, hot_out, smoothed, smoothed_one, sums = rest
     sub, slab = place()
     even = sub % 2 == 0
     half = smoothed_one.shape[1]
     smoothed[...] = second_fine[0:4]
     smoothed_one[...] = jnp.where(even, second_ref[0:4, 0:half], second_ref[0:4, half:])
-    count = parity_old.shape[1]
-    values = [ref[0:16, count:] for ref in slab_old] + [None]
+    after = parity_old.shape[1]
+    values = [ref[:, after:] for ref in slab_old] + [None]
     below, above = neighbours(slab, sizes[1], values[0], values[1])
-    mine = cross_old[0:16, count:]
-    partners = jnp.concatenate(
-        [forwarded[:, count : count + LANES], forwarded[:, count + LANES :]], axis=0
-    )
+    mine = cross_old[:, after:]
+    partners = forwarded[:, LANES:]
     group = sub // 2
     left = jnp.where(even, mine, partners)
     right = jnp.where(even, partners, mine)
@@ -531,7 +560,16 @@
     operator_two[...] = coarsen(
         tables, operator, prolong, columns, slots, aggregates, sums, LANES
     )
-    weights_two[...] = row_weights(lambda k: operator_two[16 * k : 16 * k + 16])
+    weights = row_weights(lambda k: operator_two[16 * k : 16 * k + 16])
+    weights_two[...] = weights
+    filler = jnp.zeros((1, -sends.shape[1] % LANES), jnp.int32)
+    rows = jnp.concatenate([sends[...], filler], axis=1) - group % 2 * (LANES // 2)
+    face_weights[...] = gather_four(table_four([weights]), rows & (LANES - 1))
+    hot = onehot_rows(aggregates[...], LANES)
+    hot_out[0:LANES] = hot
+    hot_out[LANES:] = lax.dot_general(
+        onehot(rows)[0:LANES], hot, (((0,), (0,)), ((), ())), preferred_element_type=F32
+    ).astype(BF16)
 
 
 def pair_restrict(
@@ -541,34 +579,30 @@
     second_ref,
     prolong,
     columns,
-    aggregates,
-    sends,
     weights_two,
+    face_weights,
+    hot,
     *rest,
 ):
-    slab_count = (len(rest) - 6) // 2
-    taken, rest = restored(rest[: slab_count + 2], PAIR_SECOND), rest[slab_count + 2 :]
-    even_in, odd_in, *slab_ins = taken
+    mine, other, *rest = rest
     source_two, first_two, whole_out = rest[:3]
     slab_outs, lifted = rest[3:-1], rest[-1]
     sub, slab = place()
-    table = table_four(chunks_of(second_ref[...]) + pair_ghosts(sizes, even_in, odd_in, slab_ins))
+    table = table_four(chunks_of(second_ref[...]) + pair_ghosts(sizes, mine, other))
 
     def step(at):
         residual = source[:, at] - apply_tile(table, operator, columns, at)
         lifted[:, at] = lift(prolong[:, at], residual)
 
     tiles(source.shape[1], 512, step)
-    total = scatter(lifted[...], aggregates[...], LANES)
+    totals = add_up(lifted[...], hot[...])
+    total = totals[:, 0:LANES]
     source_two[...] = total
     first = total / weights_two[...]
     first_two[...] = first
     half = LANES // 2
     lane = lax.broadcasted_iota(jnp.int32, first.shape, 1)
-    first = jnp.where(lane < half, first, 0.0)
-    placed = jnp.where(sub // 2 % 2 == 0, first, pltpu.roll(first, half, 1))
-    filler = jnp.zeros((1, -sends.shape[1] % LANES), jnp.int32)
-    picks = gather_four(table_four([placed]), jnp.concatenate([sends[...], filler], axis=1))
+    picks = totals[:, LANES:] / face_weights[...]
     faces = picks[:, 0:LANES]
     seconds = pltpu.roll(picks[:, LANES:], half, 1)
 
@@ -630,14 +664,20 @@
     out[...] = jnp.where(sub % 2 == 0, second[0:4, 0:share], second[0:4, share : 2 * share])
 
 
-def swap_by_core(value, even_mate, odd_mate, spare=2):
+def other_core(sub, slab):
+    return sub ^ 1, slab
+
+
+def swap_by_core(value, even_mate, odd_mate, even_spare=None, odd_spare=None):
     subs, slabs = lax.axis_size("sub"), lax.axis_size("slab")
     route = []
     for sub in range(subs):
         for slab in range(slabs):
-            target = (even_mate if sub % 2 == 0 else odd_mate)(sub, slab)
+            even = sub % 2 == 0
+            target = (even_mate if even else odd_mate)(sub, slab)
             if not (0 <= target[0] < subs and 0 <= target[1] < slabs):
-                target = (sub ^ spare, slab)
+                spare = even_spare if even else odd_spare
+                target = (sub ^ 2, slab) if spare is None else spare(sub, slab)
             route.append((sub * slabs + slab, target[0] * slabs + target[1]))
     return lax.ppermute(value, ("sub", "slab"), route)
 
@@ -646,17 +686,38 @@
     return ((index - 1) ^ 1) + 1
 
 
+def along_sub(group, odd, flip):
+    def mate(sub, slab):
+        block = odd_mate_of(sub // group) if odd else sub // group ^ 1
+        return block * group + (sub % group ^ flip), slab
+
+    return mate
+
+
+def along_slab(odd, flip):
+    return lambda sub, slab: (sub ^ flip, odd_mate_of(slab) if odd else slab ^ 1)
+
+
+def pair_exchange(first, second, beside=lambda: ()):
+    def idle(sub, slab):
+        inside = 0 <= odd_mate_of(sub // 2) < lax.axis_size("sub") // 2
+        return (sub, slab ^ 1) if inside else (sub ^ 1, slab)
+
+    def beside_slab(sub, slab):
+        return sub, slab ^ 1
+
+    last = along_sub(2, True, 0)
+    received = [swap_by_core(first, along_slab(False, 0), along_sub(2, False, 0))]
+    if lax.axis_size("slab") > 2:
+        received.append(swap_by_core(second, along_slab(True, 0), last, None, beside_slab))
+    else:
+        received.append(swap_by_core(second, idle, last, None, other_core))
+    mine = jnp.concatenate(received, axis=0)
+    mine, results = lax.optimization_barrier((mine, beside()))
+    return mine, sub_pairing(mine, 1, False), results
+
+
 def group_exchange(whole, slab_values):
-    def along_sub(odd, flip):
-        def mate(sub, slab):
-            block = odd_mate_of(sub // 4) if odd else sub // 4 ^ 1
-            return block * 4 + (sub % 4 ^ flip), slab
-
-        return mate
-
-    def along_slab(odd, flip):
-        return lambda sub, slab: (sub ^ flip, odd_mate_of(slab) if odd else slab ^ 1)
-
     def pair(sub, slab):
         return sub ^ 2, slab
 
@@ -667,9 +728,9 @@
     first = slab_values[0]
     received = [
         swap_by_core(whole, pair, along_slab(False, 2)),
-        swap_by_core(first, along_slab(False, 0), along_sub(False, 2)),
-        swap_by_core(first, along_sub(False, 0), along_sub(True, 2)),
-        swap_by_core(first, along_sub(True, 0), idle, spare=1),
+        swap_by_core(first, along_slab(False, 0), along_sub(4, False, 2)),
+        swap_by_core(first, along_sub(4, False, 0), along_sub(4, True, 2)),
+        swap_by_core(first, along_sub(4, True, 0), idle, other_core, other_core),
     ]
     for value in slab_values[1:]:
         received.append(swap_by_core(value, along_slab(True, 0), along_slab(True, 2)))
@@ -746,13 +807,14 @@
         functools.partial(fine_first, handed, slab_moves),
         [((1, value.shape[0]) if value.ndim == 1 else value.shape, value.dtype) for value in kept]
         + [operator.shape, (16, rows), (16, pair_rows_one)]
-        + [(8, rows), (8, rows), (24, count), (24, count + LANES)]
-        + [(24, count + LANES)] * slab_moves,
+        + [(8, rows), (8, rows), (16, count + LANES), (16, count + 2 * LANES)]
+        + [(16, count + 2 * LANES)] * slab_moves,
         *[pltpu.with_memory_space_constraint(value, pltpu.HBM) for value in raw],
         scratch=[
             pltpu.VMEM(prolong.shape, F32),
             pltpu.VMEM(prolong_one.shape, F32),
-            pltpu.VMEM((24, rows), F32),
+            pltpu.VMEM((8, rows), F32),
+            pltpu.VMEM((16, rows), F32),
             pltpu.SemaphoreType.DMA((len(raw) - 1,)),
             pltpu.SemaphoreType.DMA((7,)),
         ],
@@ -775,8 +837,8 @@
     )
     even, odd, *rest = call(
         functools.partial(fine_second, sizes),
-        [(8, count + 2 * LANES), (8, count)]
-        + [(8, count)] * slab_moves
+        [(16, 2 * LANES), (16, LANES)]
+        + [(16, LANES)] * slab_moves
         + [(8, rows)],
         source,
         operator,
@@ -824,49 +886,52 @@
     other = sub_pairing(own, 1, False)
 
     faces = [(8, LANES)] * (1 + slab_moves)
-    operator_one, source_one, weights_one, first_one, group_out, *slabs = call(
+    pair_sent = [(8, LANES)] * 2
+    operator_one, source_one, weights_one, first_one, *sent = call(
         pair_first,
-        [(112, pair_rows_one)] + [(8, pair_rows_one)] * 3 + faces,
+        [(112, pair_rows_one)] + [(8, pair_rows_one)] * 3 + pair_sent,
         own,
         other,
         sends_one,
     )
-    even_in = sub_pairing(group_out, 2, False)
-    odd_in = sub_pairing(group_out, 2, True)
-    slabs_in = slab_pairings(slabs)
-
-    second_one, group_out, *slabs = call(
+    mine, other, _ = pair_exchange(*sent)
+
+    second_one, *sent = call(
         functools.partial(pair_second, sizes),
-        [(8, pair_rows_one)] + faces,
+        [(8, pair_rows_one)] + pair_sent,
         operator_one,
         source_one,
         weights_one,
         first_one,
         columns_one,
         sends_one,
-        *ordered([even_in, odd_in, *slabs_in], PAIR_FIRST),
-    )
-    even_in = sub_pairing(group_out, 2, False)
-    odd_in = sub_pairing(group_out, 2, True)
-    slabs_in = slab_pairings(slabs)
-
-    operator_two, weights_two, smoothed, smoothed_one = call(
-        functools.partial(pair_coarsen, sizes),
-        [(112, LANES), (8, LANES), (4, rows), (4, rows_one)],
-        operator_one,
-        prolong_one,
-        columns_one,
-        slots_one,
-        aggregates_one,
-        second,
-        second_one,
-        even_old,
-        odd_old,
-        forwarded,
-        *slabs_old,
-        scratch=[pltpu.VMEM((112, pair_rows_one), F32)],
-        flops=10**9,
-    )
+        mine,
+        other,
+    )
+    def coarse_operator():
+        return call(
+            functools.partial(pair_coarsen, sizes),
+            [(112, LANES), (8, LANES), (8, 2 * LANES), ((3 * LANES, pair_rows_one), BF16)]
+            + [(4, rows), (4, rows_one)],
+            operator_one,
+            prolong_one,
+            columns_one,
+            slots_one,
+            aggregates_one,
+            sends_two,
+            second,
+            second_one,
+            even_old,
+            odd_old,
+            forwarded,
+            *slabs_old,
+            scratch=[pltpu.VMEM((112, pair_rows_one), F32)],
+            flops=10**9,
+        )
+
+    mine, other, outs = pair_exchange(*sent, beside=coarse_operator)
+    operator_two, weights_two, face_weights, hot, smoothed, smoothed_one = outs
+
     source_two, first_two, whole, *slabs = call(
         functools.partial(pair_restrict, sizes),
         [(8, LANES), (8, LANES)] + faces,
@@ -875,10 +940,11 @@
         second_one,
         prolong_one,
         columns_one,
-        aggregates_one,
-        sends_two,
         weights_two,
-        *ordered([even_in, odd_in, *slabs_in], PAIR_SECOND),
+        face_weights,
+        hot,
+        mine,
+        other,
         scratch=[pltpu.VMEM((8, pair_rows_one), F32)],
     )
     received = group_exchange(whole, slabs)

time: 43.3 us -> 41.8 us (0.965); the launches traced: 42.7 us -> 41.6 us
  starting transfers between devices: 17.9 us -> 16.2 us
  waiting for transfers between devices: 8.53 us -> 9.89 us
  Pallas kernels: 15.5 us -> 14.8 us
    ppermute x4 -> x8, starting transfers between devices: 3.23 us -> 10.2 us  [swap_by_core(): return lax.ppermute(value, ('sub', 'slab'), route)]
    ppermute x10 -> x8, starting transfers between devices: 11.3 us -> 4.85 us  [sub_pairing(): return lax.ppermute(value, ('sub', 'slab'), route)]
    ppermute x4 -> x2, starting transfers between devices: 3.38 us -> 1.15 us  [slab_pairing(): return lax.ppermute(value, ('sub', 'slab'), route)]
    ppermute x4 -> x8, waiting for transfers between devices: 1.89 us -> 3.52 us  [swap_by_core(): return lax.ppermute(value, ('sub', 'slab'), route)]
    ppermute x4 -> x2, waiting for transfers between devices: 2.66 us -> 1.88 us  [slab_pairing(): return lax.ppermute(value, ('sub', 'slab'), route)]
    pallas_call x11, Pallas kernels: 15.5 us -> 14.8 us  [call(): pl.pallas_call(body, out_shape=[jax.ShapeDtypeStruct(shape, dtype) for sh...]
    ppermute x10 -> x8, waiting for transfers between devices: 3.98 us -> 4.48 us  [sub_pairing(): return lax.ppermute(value, ('sub', 'slab'), route)]
  transfers between devices with their start and end apart: 18 -> 18, of which waited for: 7 -> 8; matrix products, arithmetic and copies ran while one was open for 0% -> 0% of each run, Pallas kernels for 16% -> 16%
where the time goes in v4:
time: 41.8 us; the launch traced here: 41.6 us
  starting transfers between devices  16.2 us (39%)
  Pallas kernels  14.8 us (35%)
  waiting for transfers between devices  9.89 us (24%)
  between operations  0.74 us (2%)
    pallas_call x11, Pallas kernels, call(): pl.pallas_call(body, out_shape=[jax.ShapeDtypeStruct(shape, dtype) for sh...  14.8 us
    ppermute x8, starting transfers between devices, swap_by_core(): return lax.ppermute(value, ('sub', 'slab'), route)  10.2 us
    ppermute x8, starting transfers between devices, sub_pairing(): return lax.ppermute(value, ('sub', 'slab'), route)  4.85 us
    ppermute x8, waiting for transfers between devices, sub_pairing(): return lax.ppermute(value, ('sub', 'slab'), route)  4.48 us
    ppermute x8, waiting for transfers between devices, swap_by_core(): return lax.ppermute(value, ('sub', 'slab'), route)  3.52 us
    ppermute x2, waiting for transfers between devices, slab_pairing(): return lax.ppermute(value, ('sub', 'slab'), route)  1.88 us
    ppermute x2, starting transfers between devices, slab_pairing(): return lax.ppermute(value, ('sub', 'slab'), route)  1.15 us
  transfers between devices with their start and end apart: 18, of which 8 were waited for; matrix products, arithmetic and copies ran while one was open for 0% of the time, Pallas kernels for 16%

profile of v4, /device:TPU:0, one launch (start us, length us, event | category | flops | bytes accessed | tf_op | source)
XLA Modules:
  0.0 41.6 jit_solution(12739599503607068141)
XLA Ops:
  0.6 2.3 %shard_map.157 = (f32[4,2048]{1,0:T(4,128)S(1)}, s32[1,2048]{1,0:T(1,128)S(1)}, s32[1,384]{1,0:T(1,128)S(1)}, s32[7,2048]{1,0:T(8,128)S(1)}, s32[7,2048]{1,0:T(8...) custom-call(f32[7,4,4,2048]{3,2,1,0:T(4,128)} %refs_0_.1, ...), custom_call_target="tpu_custom_call" | custom-call | tf_op jit(solution)/shard_map/pallas_call | solution.py:206
  2.9 0.5 %collective-permute-start = (f32[16,640]{1,0:T(8,128)S(1)}, f32[16,640]{1,0:T(8,128)S(1)}, u32[]{:S(2)}, u32[]{:S(2)}) collective-permute-start(f32[16,640]{1,0:T(8,128)S(1)} %get-tuple-element.63), channel_id=1, source_target_pairs={{0,2},{1,3},{2,0},{3,1},{4,6},{5,7},{6,4},{7,5},{8,10},{9,11},{10,... | collective-permute-start | bytes 122888 | tf_op jit(solution)/shard_map/ppermute | solution.py:751
  3.5 2.6 %collective-permute-start.1 = (f32[16,768]{1,0:T(8,128)S(1)}, f32[16,768]{1,0:T(8,128)S(1)}, u32[]{:S(2)}, u32[]{:S(2)}) collective-permute-start(f32[16,768]{1,0:T(8,128)S(1)} %get-tuple-element.64), channel_id=1, source_target_pairs={{0,1},{1,0},{2,4},{3,5},{4,2},{5,3},{6,8},{7,9},{8,6},{9,7},{10,12... | collective-permute-start | bytes 147464 | tf_op jit(solution)/shard_map/ppermute | solution.py:751
  6.0 0.1 collective-permute-start.2
  6.1 2.1 %shard_map.158 = (f32[112,2048]{1,0:T(8,128)S(1)}, f32[112,2048]{1,0:T(8,128)S(1)}) custom-call(f32[7,4,4,2048]{3,2,1,0:T(4,128)S(1)} %get-tuple-element.55.operator_raw, f32[16,2048]{1,0:T(8,128)S(1)} %get-tuple-element.56.prolong, s32[7,2048]{1,0:T(8,128)S(1)} %get-tuple-element.57.columns), custom_call_target="tpu_custom_call" | custom-call | flops 1000000000 | tf_op jit(solution)/shard_map/pallas_call | solution.py:206
  8.2 0.0 collective-permute-done.rest_0_.parity_old
  8.2 0.0 collective-permute-done.1.rest_1_.cross_old
  8.2 1.9 %collective-permute-done.2.rest_2_.rest_0_ = f32[16,768]{1,0:T(8,128)S(1)} collective-permute-done((f32[16,768]{1,0:T(8,128)S(1)}, f32[16,768]{1,0:T(8,128)S(1)}, u32[]{:S(2)}, u32[]{:S(2)}) %collective-permute-start.2) | collective-permute-done | bytes 49184 | tf_op jit(solution)/shard_map/ppermute | solution.py:762
  10.1 1.5 %shard_map.159 = (f32[16,256]{1,0:T(8,128)S(1)}, f32[16,128]{1,0:T(8,128)S(1)}, f32[16,128]{1,0:T(8,128)S(1)}, f32[8,2048]{1,0:T(8,128)S(1)}) custom-call(f32[4,2048]{1,0:T(4,128)S(1)} %get-tuple-element.54.source, f32[112,2048]{1,0:T(8,128)S(1)} %get-tuple-element.58.operator, s32[7,2048]{1,0:T(8,128)S(1)} %get-tuple-element.57.columns, ...), custom_call_target="tpu_custom_call" | custom-call | tf_op jit(solution)/shard_map/pallas_call | solution.py:206
  11.6 1.0 %collective-permute-start.4 = (f32[16,128]{1,0:T(8,128)S(1)}, f32[16,128]{1,0:T(8,128)S(1)}, u32[]{:S(2)}, u32[]{:S(2)}) collective-permute-start(f32[16,128]{1,0:T(8,128)S(1)} %get-tuple-element.70), channel_id=1, source_target_pairs={{0,1},{1,0},{2,4},{3,5},{4,2},{5,3},{6,8},{7,9},{8,6},{9,7},{10,12... | collective-permute-start | bytes 24584 | tf_op jit(solution)/shard_map/ppermute | solution.py:751
  12.6 1.1 %collective-permute-start.5 = (f32[16,128]{1,0:T(8,128)S(1)}, f32[16,128]{1,0:T(8,128)S(1)}, u32[]{:S(2)}, u32[]{:S(2)}) collective-permute-start(f32[16,128]{1,0:T(8,128)S(1)} %get-tuple-element.71), channel_id=1, source_target_pairs={{0,1},{1,0},{2,3},{3,2},{4,5},{5,4},{6,7},{7,6},{8,9},{9,8},{10,11... | collective-permute-start | bytes 24584 | tf_op jit(solution)/shard_map/ppermute | solution.py:762
  13.7 0.3 collective-permute-start.3
  14.0 2.9 %shard_map.160.operator_own = f32[112,256]{1,0:T(8,128)S(1)} custom-call(f32[112,2048]{1,0:T(8,128)S(1)} %get-tuple-element.58.operator, f32[16,2048]{1,0:T(8,128)S(1)} %get-tuple-element.56.prolong, s32[7,2048]{1,0:T(8,128)S(1)} %get-tuple-element.57.columns, s32[7,2048]{1,0:T(8,128)S(1)} %get-tuple-element.67.slots, ...), custom_call_target="tpu_custom_call" | custom-call | flops 4000000000 | tf_op jit(solution)/shard_map/pallas_call | solution.py:206
  16.9 0.0 collective-permute-done.4.rest_1_
  16.9 0.0 collective-permute-done.5.rest_2_
  16.9 0.0 collective-permute-done.3.rest_0_.forwarded
  16.9 1.5 %shard_map.161.own = f32[120,256]{1,0:T(8,128)S(1)} custom-call(f32[4,2048]{1,0:T(4,128)S(1)} %get-tuple-element.54.source, f32[112,2048]{1,0:T(8,128)S(1)} %get-tuple-element.58.operator, f32[16,2048]{1,0:T(8,128)S(1)} %get-tuple-element.56.prolong, s32[7,2048]{1,0:T(8,128)S(1)} %get-tuple-element.57.columns, s32[1,2048]{1,0:T(1,128)S(1)} %get-tuple-element.59.aggregates, ...), custom_call_target="tpu_custom_call" | custom-call | tf_op jit(solution)/shard_map/pallas_call | solution.py:206
  18.4 0.3 collective-permute-start.6
  18.7 1.1 %collective-permute-done.6.other = f32[120,256]{1,0:T(8,128)S(1)} collective-permute-done((f32[120,256]{1,0:T(8,128)S(1)}, f32[120,256]{1,0:T(8,128)S(1)}, u32[]{:S(2)}, u32[]{:S(2)}) %collective-permute-start.6) | collective-permute-done | bytes 122912 | tf_op jit(solution)/shard_map/ppermute | solution.py:751
  19.8 0.3 shard_map.162
  20.1 0.8 %collective-permute-start.7 = (f32[8,128]{1,0:T(8,128)S(1)}, f32[8,128]{1,0:T(8,128)S(1)}, u32[]{:S(2)}, u32[]{:S(2)}) collective-permute-start(f32[8,128]{1,0:T(8,128)S(1)} %get-tuple-element.78), channel_id=1, source_target_pairs={{0,1},{1,0},{2,6},{3,7},{4,5},{5,4},{6,2},{7,3},{8,9},{9,8},{10,14... | collective-permute-start | bytes 12296 | tf_op jit(solution)/shard_map/ppermute | solution.py:682
  21.0 1.1 %collective-permute-start.8 = (f32[8,128]{1,0:T(8,128)S(1)}, f32[8,128]{1,0:T(8,128)S(1)}, u32[]{:S(2)}, u32[]{:S(2)}) collective-permute-start(f32[8,128]{1,0:T(8,128)S(1)} %get-tuple-element.79), channel_id=1, source_target_pairs={{0,2},{1,3},{2,0},{3,1},{4,5},{5,4},{6,10},{7,11},{8,9},{9,8},{10,... | collective-permute-start | bytes 12296 | tf_op jit(solution)/shard_map/ppermute | solution.py:682
  22.0 1.7 %collective-permute-done.7 = f32[8,128]{1,0:T(8,128)S(1)} collective-permute-done((f32[8,128]{1,0:T(8,128)S(1)}, f32[8,128]{1,0:T(8,128)S(1)}, u32[]{:S(2)}, u32[]{:S(2)}) %collective-permute-start.7) | collective-permute-done | bytes 4128 | tf_op jit(solution)/shard_map/ppermute | solution.py:682
  23.7 0.0 collective-permute-done.8
  23.7 0.0 collective-permute-start.9
  23.8 1.2 %collective-permute-done.9.other = f32[16,128]{1,0:T(8,128)S(1)} collective-permute-done((f32[16,128]{1,0:T(8,128)S(1)}, f32[16,128]{1,0:T(8,128)S(1)}, u32[]{:S(2)}, u32[]{:S(2)}) %collective-permute-start.9) | collective-permute-done | bytes 8224 | tf_op jit(solution)/shard_map/ppermute | solution.py:751
  24.9 0.7 %shard_map.163 = (f32[8,512]{1,0:T(8,128)S(1)}, f32[8,128]{1,0:T(8,128)S(1)}, f32[8,128]{1,0:T(8,128)S(1)}) custom-call(f32[112,512]{1,0:T(8,128)S(1)} %get-tuple-element.73.operator, f32[8,512]{1,0:T(8,128)S(1)} %get-tuple-element.74.source, f32[8,512]{1,0:T(8,128)S(1)} %get-tuple-element.75.weights, f32[8,512]{1,0:T(8,128)S(1)} %get-tuple-element.76.first, ...), custom_call_target="tpu_custom_call" | custom-call | tf_op jit(solution)/shard_map/pallas_call | solution.py:206
  25.6 0.8 %collective-permute-start.10 = (f32[8,128]{1,0:T(8,128)S(1)}, f32[8,128]{1,0:T(8,128)S(1)}, u32[]{:S(2)}, u32[]{:S(2)}) collective-permute-start(f32[8,128]{1,0:T(8,128)S(1)} %get-tuple-element.80), channel_id=1, source_target_pairs={{0,1},{1,0},{2,6},{3,7},{4,5},{5,4},{6,2},{7,3},{8,9},{9,8},{10,14... | collective-permute-start | bytes 12296 | tf_op jit(solution)/shard_map/ppermute | solution.py:682
  26.5 1.6 %collective-permute-start.11 = (f32[8,128]{1,0:T(8,128)S(1)}, f32[8,128]{1,0:T(8,128)S(1)}, u32[]{:S(2)}, u32[]{:S(2)}) collective-permute-start(f32[8,128]{1,0:T(8,128)S(1)} %get-tuple-element.81), channel_id=1, source_target_pairs={{0,2},{1,3},{2,0},{3,1},{4,5},{5,4},{6,10},{7,11},{8,9},{9,8},{10,... | collective-permute-start | bytes 12296 | tf_op jit(solution)/shard_map/ppermute | solution.py:682
  28.1 1.6 %shard_map.164 = (f32[112,128]{1,0:T(8,128)S(1)}, f32[8,128]{1,0:T(8,128)S(1)}, f32[8,256]{1,0:T(8,128)S(1)}, bf16[384,512]{1,0:T(8,128)(2,1)S(1)}, f32[4,2048]{1,0:T(4,128)}, /*index=5*/f32[4,256]{1,0:T(4,128)}) custom-call(f32[112,512]{1,0:T(8,128)S(1)} %get-tuple-element.73.operator, f32[16,512]{1,0:T(8,128)S(1)} %get-tuple-element.82.prolong, ...), custom_call_target="tpu_custom_call" | custom-call | flops 1000000000 | tf_op jit(solution)/shard_map/pallas_call | solution.py:206
  29.7 0.0 collective-permute-done.10
  29.7 0.0 collective-permute-done.11
  29.7 0.1 collective-permute-start.12
  29.8 1.2 %collective-permute-done.12.rest_1_ = f32[16,128]{1,0:T(8,128)S(1)} collective-permute-done((f32[16,128]{1,0:T(8,128)S(1)}, f32[16,128]{1,0:T(8,128)S(1)}, u32[]{:S(2)}, u32[]{:S(2)}) %collective-permute-start.12) | collective-permute-done | bytes 8224 | tf_op jit(solution)/shard_map/ppermute | solution.py:751
  30.9 0.8 %shard_map.165 = (f32[8,128]{1,0:T(8,128)S(1)}, f32[8,128]{1,0:T(8,128)S(1)}, f32[8,128]{1,0:T(8,128)S(1)}, f32[8,128]{1,0:T(8,128)S(1)}) custom-call(f32[112,512]{1,0:T(8,128)S(1)} %get-tuple-element.73.operator, f32[8,512]{1,0:T(8,128)S(1)} %get-tuple-element.74.source, f32[8,512]{1,0:T(8,128)S(1)} %get-tuple-element.86.second_ref, ...), custom_call_target="tpu_custom_call" | custom-call | tf_op jit(solution)/shard_map/pallas_call | solution.py:206
  31.7 3.6 %collective-permute-start.13 = (f32[8,128]{1,0:T(8,128)S(1)}, f32[8,128]{1,0:T(8,128)S(1)}, u32[]{:S(2)}, u32[]{:S(2)}) collective-permute-start(f32[8,128]{1,0:T(8,128)S(1)} %get-tuple-element.103), channel_id=1, source_target_pairs={{0,4},{1,5},{2,7},{3,6},{4,0},{5,1},{6,3},{7,2},{8,12},{9,13},{10,... | collective-permute-start | bytes 12296 | tf_op jit(solution)/shard_map/ppermute | solution.py:682
  35.3 0.5 %collective-permute-start.16 = (f32[8,128]{1,0:T(8,128)S(1)}, f32[8,128]{1,0:T(8,128)S(1)}, u32[]{:S(2)}, u32[]{:S(2)}) collective-permute-start(f32[8,128]{1,0:T(8,128)S(1)} %get-tuple-element.104), channel_id=1, source_target_pairs={{0,1},{1,0},{2,14},{3,15},{4,5},{5,4},{6,10},{7,11},{8,9},{9,8},{1... | collective-permute-start | bytes 12296 | tf_op jit(solution)/shard_map/ppermute | solution.py:682
  35.8 1.6 %collective-permute-start.15 = (f32[8,128]{1,0:T(8,128)S(1)}, f32[8,128]{1,0:T(8,128)S(1)}, u32[]{:S(2)}, u32[]{:S(2)}) collective-permute-start(f32[8,128]{1,0:T(8,128)S(1)} %get-tuple-element.104), channel_id=1, source_target_pairs={{0,8},{1,9},{2,6},{3,7},{4,12},{5,13},{6,2},{7,3},{8,0},{9,1},{10,... | collective-permute-start | bytes 12296 | tf_op jit(solution)/shard_map/ppermute | solution.py:682
  37.4 0.2 collective-permute-start.14
  37.6 0.0 collective-permute-done.13.rest_0_
  37.6 1.3 %collective-permute-done.16.rest_3_ = f32[8,128]{1,0:T(8,128)S(1)} collective-permute-done((f32[8,128]{1,0:T(8,128)S(1)}, f32[8,128]{1,0:T(8,128)S(1)}, u32[]{:S(2)}, u32[]{:S(2)}) %collective-permute-start.16) | collective-permute-done | bytes 4128 | tf_op jit(solution)/shard_map/ppermute | solution.py:682
  38.9 0.5 %collective-permute-done.15.rest_2_ = f32[8,128]{1,0:T(8,128)S(1)} collective-permute-done((f32[8,128]{1,0:T(8,128)S(1)}, f32[8,128]{1,0:T(8,128)S(1)}, u32[]{:S(2)}, u32[]{:S(2)}) %collective-permute-start.15) | collective-permute-done | bytes 4128 | tf_op jit(solution)/shard_map/ppermute | solution.py:682
  39.4 0.0 collective-permute-done.14.rest_1_
  39.4 0.4 shard_map.166.own
  39.8 0.1 collective-permute-start.17
  39.9 1.1 %collective-permute-done.17.other = f32[8,128]{1,0:T(8,128)S(1)} collective-permute-done((f32[8,128]{1,0:T(8,128)S(1)}, f32[8,128]{1,0:T(8,128)S(1)}, u32[]{:S(2)}, u32[]{:S(2)}) %collective-permute-start.17) | collective-permute-done | bytes 4128 | tf_op jit(solution)/shard_map/ppermute | solution.py:751
  41.0 0.7 %shard_map.167 = f32[4,32]{1,0:T(4,128)} custom-call(f32[8,128]{1,0:T(8,128)S(1)} %get-tuple-element.99.source, f32[8,128]{1,0:T(8,128)S(1)} %get-tuple-element.95.weights_two.weights, f32[8,128]{1,0:T(8,128)S(1)} %get-tuple-element.100.first_two, f32[8,128]{1,0:T(8,128)S(1)} %shard_map.166.own, f32[8,128]{1,0:T(8,128)S(1)} %collective-permute-done.17.other), custom_call_target="tpu_custom_call" | custom-call | tf_op jit(solution)/shard_map/pallas_call | solution.py:206
  (2 shorter events, 0.0 us)
Async XLA Ops:
  2.9 5.3 %collective-permute-start = (f32[16,640]{1,0:T(8,128)S(1)}, f32[16,640]{1,0:T(8,128)S(1)}, u32[]{:S(2)}, u32[]{:S(2)}) collective-permute-start(f32[16,640]{1,0:T(8,128)S(1)} %get-tuple-element.63), channel_id=1, source_target_pairs={{0,2},{1,3},{2,0},{3,1},{4,6},{5,7},{6,4},{7,5},{8,10},{9,11},{10,... | collective-permute-start | bytes 122888 | tf_op jit(solution)/shard_map/ppermute | solution.py:751
  3.5 4.8 %collective-permute-start.1 = (f32[16,768]{1,0:T(8,128)S(1)}, f32[16,768]{1,0:T(8,128)S(1)}, u32[]{:S(2)}, u32[]{:S(2)}) collective-permute-start(f32[16,768]{1,0:T(8,128)S(1)} %get-tuple-element.64), channel_id=1, source_target_pairs={{0,1},{1,0},{2,4},{3,5},{4,2},{5,3},{6,8},{7,9},{8,6},{9,7},{10,12... | collective-permute-start | bytes 147464 | tf_op jit(solution)/shard_map/ppermute | solution.py:751
  6.0 4.1 %collective-permute-start.2 = (f32[16,768]{1,0:T(8,128)S(1)}, f32[16,768]{1,0:T(8,128)S(1)}, u32[]{:S(2)}, u32[]{:S(2)}) collective-permute-start(f32[16,768]{1,0:T(8,128)S(1)} %get-tuple-element.65), channel_id=1, source_target_pairs={{0,1},{1,0},{2,3},{3,2},{4,5},{5,4},{6,7},{7,6},{8,9},{9,8},{10,11... | collective-permute-start | bytes 147464 | tf_op jit(solution)/shard_map/ppermute | solution.py:762
  11.6 5.3 %collective-permute-start.4 = (f32[16,128]{1,0:T(8,128)S(1)}, f32[16,128]{1,0:T(8,128)S(1)}, u32[]{:S(2)}, u32[]{:S(2)}) collective-permute-start(f32[16,128]{1,0:T(8,128)S(1)} %get-tuple-element.70), channel_id=1, source_target_pairs={{0,1},{1,0},{2,4},{3,5},{4,2},{5,3},{6,8},{7,9},{8,6},{9,7},{10,12... | collective-permute-start | bytes 24584 | tf_op jit(solution)/shard_map/ppermute | solution.py:751
  12.6 4.3 %collective-permute-start.5 = (f32[16,128]{1,0:T(8,128)S(1)}, f32[16,128]{1,0:T(8,128)S(1)}, u32[]{:S(2)}, u32[]{:S(2)}) collective-permute-start(f32[16,128]{1,0:T(8,128)S(1)} %get-tuple-element.71), channel_id=1, source_target_pairs={{0,1},{1,0},{2,3},{3,2},{4,5},{5,4},{6,7},{7,6},{8,9},{9,8},{10,11... | collective-permute-start | bytes 24584 | tf_op jit(solution)/shard_map/ppermute | solution.py:762
  13.7 3.2 %collective-permute-start.3 = (f32[16,256]{1,0:T(8,128)S(1)}, f32[16,256]{1,0:T(8,128)S(1)}, u32[]{:S(2)}, u32[]{:S(2)}) collective-permute-start(f32[16,256]{1,0:T(8,128)S(1)} %get-tuple-element.69), channel_id=1, source_target_pairs={{0,2},{1,3},{2,0},{3,1},{4,6},{5,7},{6,4},{7,5},{8,10},{9,11},{10,... | collective-permute-start | bytes 49160 | tf_op jit(solution)/shard_map/ppermute | solution.py:751
  18.4 1.4 %collective-permute-start.6 = (f32[120,256]{1,0:T(8,128)S(1)}, f32[120,256]{1,0:T(8,128)S(1)}, u32[]{:S(2)}, u32[]{:S(2)}) collective-permute-start(f32[120,256]{1,0:T(8,128)S(1)} %shard_map.161.own), channel_id=1, source_target_pairs={{0,2},{1,3},{2,0},{3,1},{4,6},{5,7},{6,4},{7,5},{8,10},{9,11},{10,... | collective-permute-start | bytes 368648 | tf_op jit(solution)/shard_map/ppermute | solution.py:751
  20.1 3.6 %collective-permute-start.7 = (f32[8,128]{1,0:T(8,128)S(1)}, f32[8,128]{1,0:T(8,128)S(1)}, u32[]{:S(2)}, u32[]{:S(2)}) collective-permute-start(f32[8,128]{1,0:T(8,128)S(1)} %get-tuple-element.78), channel_id=1, source_target_pairs={{0,1},{1,0},{2,6},{3,7},{4,5},{5,4},{6,2},{7,3},{8,9},{9,8},{10,14... | collective-permute-start | bytes 12296 | tf_op jit(solution)/shard_map/ppermute | solution.py:682
  21.0 2.8 %collective-permute-start.8 = (f32[8,128]{1,0:T(8,128)S(1)}, f32[8,128]{1,0:T(8,128)S(1)}, u32[]{:S(2)}, u32[]{:S(2)}) collective-permute-start(f32[8,128]{1,0:T(8,128)S(1)} %get-tuple-element.79), channel_id=1, source_target_pairs={{0,2},{1,3},{2,0},{3,1},{4,5},{5,4},{6,10},{7,11},{8,9},{9,8},{10,... | collective-permute-start | bytes 12296 | tf_op jit(solution)/shard_map/ppermute | solution.py:682
  23.7 1.2 %collective-permute-start.9 = (f32[16,128]{1,0:T(8,128)S(1)}, f32[16,128]{1,0:T(8,128)S(1)}, u32[]{:S(2)}, u32[]{:S(2)}) collective-permute-start(f32[16,128]{1,0:T(8,128)S(1)} %pad_maximum_fusion.mine), channel_id=1, source_target_pairs={{0,2},{1,3},{2,0},{3,1},{4,6},{5,7},{6,4},{7,5},{8,10},{9,11},{10,... | collective-permute-start | bytes 24584 | tf_op jit(solution)/shard_map/ppermute | solution.py:751
  25.6 4.0 %collective-permute-start.10 = (f32[8,128]{1,0:T(8,128)S(1)}, f32[8,128]{1,0:T(8,128)S(1)}, u32[]{:S(2)}, u32[]{:S(2)}) collective-permute-start(f32[8,128]{1,0:T(8,128)S(1)} %get-tuple-element.80), channel_id=1, source_target_pairs={{0,1},{1,0},{2,6},{3,7},{4,5},{5,4},{6,2},{7,3},{8,9},{9,8},{10,14... | collective-permute-start | bytes 12296 | tf_op jit(solution)/shard_map/ppermute | solution.py:682
  26.5 3.2 %collective-permute-start.11 = (f32[8,128]{1,0:T(8,128)S(1)}, f32[8,128]{1,0:T(8,128)S(1)}, u32[]{:S(2)}, u32[]{:S(2)}) collective-permute-start(f32[8,128]{1,0:T(8,128)S(1)} %get-tuple-element.81), channel_id=1, source_target_pairs={{0,2},{1,3},{2,0},{3,1},{4,5},{5,4},{6,10},{7,11},{8,9},{9,8},{10,... | collective-permute-start | bytes 12296 | tf_op jit(solution)/shard_map/ppermute | solution.py:682
  29.7 1.2 %collective-permute-start.12 = (f32[16,128]{1,0:T(8,128)S(1)}, f32[16,128]{1,0:T(8,128)S(1)}, u32[]{:S(2)}, u32[]{:S(2)}) collective-permute-start(f32[16,128]{1,0:T(8,128)S(1)} %pad_maximum_fusion.1.rest_0_), channel_id=1, source_target_pairs={{0,2},{1,3},{2,0},{3,1},{4,6},{5,7},{6,4},{7,5},{8,10},{9,11},{10,... | collective-permute-start | bytes 24584 | tf_op jit(solution)/shard_map/ppermute | solution.py:751
  31.7 5.9 %collective-permute-start.13 = (f32[8,128]{1,0:T(8,128)S(1)}, f32[8,128]{1,0:T(8,128)S(1)}, u32[]{:S(2)}, u32[]{:S(2)}) collective-permute-start(f32[8,128]{1,0:T(8,128)S(1)} %get-tuple-element.103), channel_id=1, source_target_pairs={{0,4},{1,5},{2,7},{3,6},{4,0},{5,1},{6,3},{7,2},{8,12},{9,13},{10,... | collective-permute-start | bytes 12296 | tf_op jit(solution)/shard_map/ppermute | solution.py:682
  35.3 3.6 %collective-permute-start.16 = (f32[8,128]{1,0:T(8,128)S(1)}, f32[8,128]{1,0:T(8,128)S(1)}, u32[]{:S(2)}, u32[]{:S(2)}) collective-permute-start(f32[8,128]{1,0:T(8,128)S(1)} %get-tuple-element.104), channel_id=1, source_target_pairs={{0,1},{1,0},{2,14},{3,15},{4,5},{5,4},{6,10},{7,11},{8,9},{9,8},{1... | collective-permute-start | bytes 12296 | tf_op jit(solution)/shard_map/ppermute | solution.py:682
  35.8 3.6 %collective-permute-start.15 = (f32[8,128]{1,0:T(8,128)S(1)}, f32[8,128]{1,0:T(8,128)S(1)}, u32[]{:S(2)}, u32[]{:S(2)}) collective-permute-start(f32[8,128]{1,0:T(8,128)S(1)} %get-tuple-element.104), channel_id=1, source_target_pairs={{0,8},{1,9},{2,6},{3,7},{4,12},{5,13},{6,2},{7,3},{8,0},{9,1},{10,... | collective-permute-start | bytes 12296 | tf_op jit(solution)/shard_map/ppermute | solution.py:682
  37.4 2.0 %collective-permute-start.14 = (f32[8,128]{1,0:T(8,128)S(1)}, f32[8,128]{1,0:T(8,128)S(1)}, u32[]{:S(2)}, u32[]{:S(2)}) collective-permute-start(f32[8,128]{1,0:T(8,128)S(1)} %get-tuple-element.104), channel_id=1, source_target_pairs={{0,2},{1,3},{2,0},{3,1},{4,6},{5,7},{6,4},{7,5},{8,16},{9,17},{10,... | collective-permute-start | bytes 12296 | tf_op jit(solution)/shard_map/ppermute | solution.py:682
  39.8 1.2 %collective-permute-start.17 = (f32[8,128]{1,0:T(8,128)S(1)}, f32[8,128]{1,0:T(8,128)S(1)}, u32[]{:S(2)}, u32[]{:S(2)}) collective-permute-start(f32[8,128]{1,0:T(8,128)S(1)} %shard_map.166.own), channel_id=1, source_target_pairs={{0,2},{1,3},{2,0},{3,1},{4,6},{5,7},{6,4},{7,5},{8,10},{9,11},{10,... | collective-permute-start | bytes 12296 | tf_op jit(solution)/shard_map/ppermute | solution.py:751

commit v5 on v4

--- a/solution.py
+++ b/solution.py
@@ -75,10 +75,10 @@
     return fold(total)
 
 
-def choose_sixteen(picked, high):
+def choose_sixteen(picked, high, total=None):
     shape = (8, picked.shape[1])
     high = jnp.broadcast_to(high, shape)
-    total = [jnp.zeros(shape, F32), jnp.zeros(shape, F32)]
+    total = [jnp.zeros(shape, F32)] * 2 if total is None else list(total)
     for j in range(picked.shape[0] // 16):
         here = high == j
         for half in range(2):
@@ -95,8 +95,8 @@
     return choose_four(matmul(table, onehot(columns)), columns >> 7)
 
 
-def gather_halves(table, columns, chunk):
-    return choose_sixteen(matmul(table, onehot(columns)), (columns >> 7) - chunk)
+def gather_halves(table, columns, chunk, outside=None):
+    return choose_sixteen(matmul(table, onehot(columns)), (columns >> 7) - chunk, outside)
 
 
 def gather_sixteen(table, columns):
@@ -402,11 +402,9 @@
         for k in range(7):
             column = columns[k : k + 1, at]
             if k < known:
-                near = gather_halves(tables[1], column, tables[0].shape[0] // 16)
-                near = [
-                    near[half] + own_near[16 * k + 8 * half : 16 * k + 8 * half + 8, at]
-                    for half in range(2)
-                ]
+                row = 16 * k
+                own = [own_near[row : row + 8, at], own_near[row + 8 : row + 16, at]]
+                near = gather_halves(tables[1], column, tables[0].shape[0] // 16, own)
             else:
                 near = gather_halves(whole, column, 0)
             blocks = triple_product(wide_prolong, operator[16 * k : 16 * k + 16, at], near)
@@ -700,8 +698,7 @@
 
 def pair_exchange(first, second, beside=lambda: ()):
     def idle(sub, slab):
-        inside = 0 <= odd_mate_of(sub // 2) < lax.axis_size("sub") // 2
-        return (sub, slab ^ 1) if inside else (sub ^ 1, slab)
+        return sub ^ 2, slab
 
     def beside_slab(sub, slab):
         return sub, slab ^ 1
@@ -711,7 +708,7 @@
     if lax.axis_size("slab") > 2:
         received.append(swap_by_core(second, along_slab(True, 0), last, None, beside_slab))
     else:
-        received.append(swap_by_core(second, idle, last, None, other_core))
+        received.append(swap_by_core(second, idle, last, None, beside_slab))
     mine = jnp.concatenate(received, axis=0)
     mine, results = lax.optimization_barrier((mine, beside()))
     return mine, sub_pairing(mine, 1, False), results

time: 41.8 us -> 41.8 us (level)
  transfers between devices with their start and end apart: 18 -> 18, of which waited for: 8 -> 9; matrix products, arithmetic and copies ran while one was open for 0% -> 0% of each run, Pallas kernels for 16% -> 16%
where the time goes in v5:
time: 41.8 us; the launch traced here: 41.6 us
  starting transfers between devices  16.2 us (39%)
  Pallas kernels  14.8 us (35%)
  waiting for transfers between devices  9.95 us (24%)
  between operations  0.73 us (2%)
    pallas_call x11, Pallas kernels, call(): pl.pallas_call(body, out_shape=[jax.ShapeDtypeStruct(shape, dtype) for sh...  14.8 us
    ppermute x8, starting transfers between devices, swap_by_core(): return lax.ppermute(value, ('sub', 'slab'), route)  10.1 us
    ppermute x8, starting transfers between devices, sub_pairing(): return lax.ppermute(value, ('sub', 'slab'), route)  4.96 us
    ppermute x8, waiting for transfers between devices, sub_pairing(): return lax.ppermute(value, ('sub', 'slab'), route)  4.37 us
    ppermute x8, waiting for transfers between devices, swap_by_core(): return lax.ppermute(value, ('sub', 'slab'), route)  3.7 us
    ppermute x2, waiting for transfers between devices, slab_pairing(): return lax.ppermute(value, ('sub', 'slab'), route)  1.88 us
    ppermute x2, starting transfers between devices, slab_pairing(): return lax.ppermute(value, ('sub', 'slab'), route)  1.15 us
  transfers between devices with their start and end apart: 18, of which 9 were waited for; matrix products, arithmetic and copies ran while one was open for 0% of the time, Pallas kernels for 16%

profile of v5, /device:TPU:0, one launch (start us, length us, event | category | flops | bytes accessed | tf_op | source)
XLA Modules:
  0.0 41.6 jit_solution(8820633587921495019)
XLA Ops:
  0.6 2.3 %shard_map.157 = (f32[4,2048]{1,0:T(4,128)S(1)}, s32[1,2048]{1,0:T(1,128)S(1)}, s32[1,384]{1,0:T(1,128)S(1)}, s32[7,2048]{1,0:T(8,128)S(1)}, s32[7,2048]{1,0:T(8...) custom-call(f32[7,4,4,2048]{3,2,1,0:T(4,128)} %refs_0_.1, ...), custom_call_target="tpu_custom_call" | custom-call | tf_op jit(solution)/shard_map/pallas_call | solution.py:206
  2.9 0.5 %collective-permute-start = (f32[16,640]{1,0:T(8,128)S(1)}, f32[16,640]{1,0:T(8,128)S(1)}, u32[]{:S(2)}, u32[]{:S(2)}) collective-permute-start(f32[16,640]{1,0:T(8,128)S(1)} %get-tuple-element.63), channel_id=1, source_target_pairs={{0,2},{1,3},{2,0},{3,1},{4,6},{5,7},{6,4},{7,5},{8,10},{9,11},{10,... | collective-permute-start | bytes 122888 | tf_op jit(solution)/shard_map/ppermute | solution.py:748
  3.5 2.6 %collective-permute-start.1 = (f32[16,768]{1,0:T(8,128)S(1)}, f32[16,768]{1,0:T(8,128)S(1)}, u32[]{:S(2)}, u32[]{:S(2)}) collective-permute-start(f32[16,768]{1,0:T(8,128)S(1)} %get-tuple-element.64), channel_id=1, source_target_pairs={{0,1},{1,0},{2,4},{3,5},{4,2},{5,3},{6,8},{7,9},{8,6},{9,7},{10,12... | collective-permute-start | bytes 147464 | tf_op jit(solution)/shard_map/ppermute | solution.py:748
  6.0 0.1 collective-permute-start.2
  6.1 2.1 %shard_map.158 = (f32[112,2048]{1,0:T(8,128)S(1)}, f32[112,2048]{1,0:T(8,128)S(1)}) custom-call(f32[7,4,4,2048]{3,2,1,0:T(4,128)S(1)} %get-tuple-element.55.operator_raw, f32[16,2048]{1,0:T(8,128)S(1)} %get-tuple-element.56.prolong, s32[7,2048]{1,0:T(8,128)S(1)} %get-tuple-element.57.columns), custom_call_target="tpu_custom_call" | custom-call | flops 1000000000 | tf_op jit(solution)/shard_map/pallas_call | solution.py:206
  8.2 0.0 collective-permute-done.rest_0_.parity_old
  8.2 0.0 collective-permute-done.1.rest_1_.cross_old
  8.2 1.9 %collective-permute-done.2.rest_2_.rest_0_ = f32[16,768]{1,0:T(8,128)S(1)} collective-permute-done((f32[16,768]{1,0:T(8,128)S(1)}, f32[16,768]{1,0:T(8,128)S(1)}, u32[]{:S(2)}, u32[]{:S(2)}) %collective-permute-start.2) | collective-permute-done | bytes 49184 | tf_op jit(solution)/shard_map/ppermute | solution.py:759
  10.1 1.5 %shard_map.159 = (f32[16,256]{1,0:T(8,128)S(1)}, f32[16,128]{1,0:T(8,128)S(1)}, f32[16,128]{1,0:T(8,128)S(1)}, f32[8,2048]{1,0:T(8,128)S(1)}) custom-call(f32[4,2048]{1,0:T(4,128)S(1)} %get-tuple-element.54.source, f32[112,2048]{1,0:T(8,128)S(1)} %get-tuple-element.58.operator, s32[7,2048]{1,0:T(8,128)S(1)} %get-tuple-element.57.columns, ...), custom_call_target="tpu_custom_call" | custom-call | tf_op jit(solution)/shard_map/pallas_call | solution.py:206
  11.6 1.0 %collective-permute-start.4 = (f32[16,128]{1,0:T(8,128)S(1)}, f32[16,128]{1,0:T(8,128)S(1)}, u32[]{:S(2)}, u32[]{:S(2)}) collective-permute-start(f32[16,128]{1,0:T(8,128)S(1)} %get-tuple-element.70), channel_id=1, source_target_pairs={{0,1},{1,0},{2,4},{3,5},{4,2},{5,3},{6,8},{7,9},{8,6},{9,7},{10,12... | collective-permute-start | bytes 24584 | tf_op jit(solution)/shard_map/ppermute | solution.py:748
  12.6 1.1 %collective-permute-start.5 = (f32[16,128]{1,0:T(8,128)S(1)}, f32[16,128]{1,0:T(8,128)S(1)}, u32[]{:S(2)}, u32[]{:S(2)}) collective-permute-start(f32[16,128]{1,0:T(8,128)S(1)} %get-tuple-element.71), channel_id=1, source_target_pairs={{0,1},{1,0},{2,3},{3,2},{4,5},{5,4},{6,7},{7,6},{8,9},{9,8},{10,11... | collective-permute-start | bytes 24584 | tf_op jit(solution)/shard_map/ppermute | solution.py:759
  13.7 0.3 collective-permute-start.3
  14.0 2.9 %shard_map.160.operator_own = f32[112,256]{1,0:T(8,128)S(1)} custom-call(f32[112,2048]{1,0:T(8,128)S(1)} %get-tuple-element.58.operator, f32[16,2048]{1,0:T(8,128)S(1)} %get-tuple-element.56.prolong, s32[7,2048]{1,0:T(8,128)S(1)} %get-tuple-element.57.columns, s32[7,2048]{1,0:T(8,128)S(1)} %get-tuple-element.67.slots, ...), custom_call_target="tpu_custom_call" | custom-call | flops 4000000000 | tf_op jit(solution)/shard_map/pallas_call | solution.py:206
  16.9 0.0 collective-permute-done.4.rest_1_
  16.9 0.0 collective-permute-done.5.rest_2_
  16.9 0.0 collective-permute-done.3.rest_0_.forwarded
  16.9 1.5 %shard_map.161.own = f32[120,256]{1,0:T(8,128)S(1)} custom-call(f32[4,2048]{1,0:T(4,128)S(1)} %get-tuple-element.54.source, f32[112,2048]{1,0:T(8,128)S(1)} %get-tuple-element.58.operator, f32[16,2048]{1,0:T(8,128)S(1)} %get-tuple-element.56.prolong, s32[7,2048]{1,0:T(8,128)S(1)} %get-tuple-element.57.columns, s32[1,2048]{1,0:T(1,128)S(1)} %get-tuple-element.59.aggregates, ...), custom_call_target="tpu_custom_call" | custom-call | tf_op jit(solution)/shard_map/pallas_call | solution.py:206
  18.4 0.3 collective-permute-start.6
  18.7 1.1 %collective-permute-done.6.other = f32[120,256]{1,0:T(8,128)S(1)} collective-permute-done((f32[120,256]{1,0:T(8,128)S(1)}, f32[120,256]{1,0:T(8,128)S(1)}, u32[]{:S(2)}, u32[]{:S(2)}) %collective-permute-start.6) | collective-permute-done | bytes 122912 | tf_op jit(solution)/shard_map/ppermute | solution.py:748
  19.8 0.3 shard_map.162
  20.1 0.9 %collective-permute-start.7 = (f32[8,128]{1,0:T(8,128)S(1)}, f32[8,128]{1,0:T(8,128)S(1)}, u32[]{:S(2)}, u32[]{:S(2)}) collective-permute-start(f32[8,128]{1,0:T(8,128)S(1)} %get-tuple-element.78), channel_id=1, source_target_pairs={{0,1},{1,0},{2,6},{3,7},{4,5},{5,4},{6,2},{7,3},{8,9},{9,8},{10,14... | collective-permute-start | bytes 12296 | tf_op jit(solution)/shard_map/ppermute | solution.py:680
  21.0 1.7 %collective-permute-start.8 = (f32[8,128]{1,0:T(8,128)S(1)}, f32[8,128]{1,0:T(8,128)S(1)}, u32[]{:S(2)}, u32[]{:S(2)}) collective-permute-start(f32[8,128]{1,0:T(8,128)S(1)} %get-tuple-element.79), channel_id=1, source_target_pairs={{0,4},{1,5},{2,3},{3,2},{4,0},{5,1},{6,10},{7,11},{8,12},{9,13},{1... | collective-permute-start | bytes 12296 | tf_op jit(solution)/shard_map/ppermute | solution.py:680
  22.7 1.1 %collective-permute-done.7 = f32[8,128]{1,0:T(8,128)S(1)} collective-permute-done((f32[8,128]{1,0:T(8,128)S(1)}, f32[8,128]{1,0:T(8,128)S(1)}, u32[]{:S(2)}, u32[]{:S(2)}) %collective-permute-start.7) | collective-permute-done | bytes 4128 | tf_op jit(solution)/shard_map/ppermute | solution.py:680
  23.7 0.8 %collective-permute-done.8 = f32[8,128]{1,0:T(8,128)S(1)} collective-permute-done((f32[8,128]{1,0:T(8,128)S(1)}, f32[8,128]{1,0:T(8,128)S(1)}, u32[]{:S(2)}, u32[]{:S(2)}) %collective-permute-start.8) | collective-permute-done | bytes 4128 | tf_op jit(solution)/shard_map/ppermute | solution.py:680
  24.6 0.1 collective-permute-start.9
  24.7 1.1 %collective-permute-done.9.other = f32[16,128]{1,0:T(8,128)S(1)} collective-permute-done((f32[16,128]{1,0:T(8,128)S(1)}, f32[16,128]{1,0:T(8,128)S(1)}, u32[]{:S(2)}, u32[]{:S(2)}) %collective-permute-start.9) | collective-permute-done | bytes 8224 | tf_op jit(solution)/shard_map/ppermute | solution.py:748
  25.7 0.7 %shard_map.163 = (f32[8,512]{1,0:T(8,128)S(1)}, f32[8,128]{1,0:T(8,128)S(1)}, f32[8,128]{1,0:T(8,128)S(1)}) custom-call(f32[112,512]{1,0:T(8,128)S(1)} %get-tuple-element.73.operator, f32[8,512]{1,0:T(8,128)S(1)} %get-tuple-element.74.source, f32[8,512]{1,0:T(8,128)S(1)} %get-tuple-element.75.weights, f32[8,512]{1,0:T(8,128)S(1)} %get-tuple-element.76.first, ...), custom_call_target="tpu_custom_call" | custom-call | tf_op jit(solution)/shard_map/pallas_call | solution.py:206
  26.5 1.2 %collective-permute-start.10 = (f32[8,128]{1,0:T(8,128)S(1)}, f32[8,128]{1,0:T(8,128)S(1)}, u32[]{:S(2)}, u32[]{:S(2)}) collective-permute-start(f32[8,128]{1,0:T(8,128)S(1)} %get-tuple-element.80), channel_id=1, source_target_pairs={{0,1},{1,0},{2,6},{3,7},{4,5},{5,4},{6,2},{7,3},{8,9},{9,8},{10,14... | collective-permute-start | bytes 12296 | tf_op jit(solution)/shard_map/ppermute | solution.py:680
  27.6 2.0 %collective-permute-start.11 = (f32[8,128]{1,0:T(8,128)S(1)}, f32[8,128]{1,0:T(8,128)S(1)}, u32[]{:S(2)}, u32[]{:S(2)}) collective-permute-start(f32[8,128]{1,0:T(8,128)S(1)} %get-tuple-element.81), channel_id=1, source_target_pairs={{0,4},{1,5},{2,3},{3,2},{4,0},{5,1},{6,10},{7,11},{8,12},{9,13},{1... | collective-permute-start | bytes 12296 | tf_op jit(solution)/shard_map/ppermute | solution.py:680
  29.7 1.6 %shard_map.164 = (f32[112,128]{1,0:T(8,128)S(1)}, f32[8,128]{1,0:T(8,128)S(1)}, f32[8,256]{1,0:T(8,128)S(1)}, bf16[384,512]{1,0:T(8,128)(2,1)S(1)}, f32[4,2048]{1,0:T(4,128)}, /*index=5*/f32[4,256]{1,0:T(4,128)}) custom-call(f32[112,512]{1,0:T(8,128)S(1)} %get-tuple-element.73.operator, f32[16,512]{1,0:T(8,128)S(1)} %get-tuple-element.82.prolong, ...), custom_call_target="tpu_custom_call" | custom-call | flops 1000000000 | tf_op jit(solution)/shard_map/pallas_call | solution.py:206
  31.3 0.0 collective-permute-done.10
  31.3 0.0 collective-permute-done.11
  31.3 0.1 collective-permute-start.12
  31.4 1.2 %collective-permute-done.12.rest_1_ = f32[16,128]{1,0:T(8,128)S(1)} collective-permute-done((f32[16,128]{1,0:T(8,128)S(1)}, f32[16,128]{1,0:T(8,128)S(1)}, u32[]{:S(2)}, u32[]{:S(2)}) %collective-permute-start.12) | collective-permute-done | bytes 8224 | tf_op jit(solution)/shard_map/ppermute | solution.py:748
  32.5 0.8 %shard_map.165 = (f32[8,128]{1,0:T(8,128)S(1)}, f32[8,128]{1,0:T(8,128)S(1)}, f32[8,128]{1,0:T(8,128)S(1)}, f32[8,128]{1,0:T(8,128)S(1)}) custom-call(f32[112,512]{1,0:T(8,128)S(1)} %get-tuple-element.73.operator, f32[8,512]{1,0:T(8,128)S(1)} %get-tuple-element.74.source, f32[8,512]{1,0:T(8,128)S(1)} %get-tuple-element.86.second_ref, ...), custom_call_target="tpu_custom_call" | custom-call | tf_op jit(solution)/shard_map/pallas_call | solution.py:206
  33.3 1.9 %collective-permute-start.13 = (f32[8,128]{1,0:T(8,128)S(1)}, f32[8,128]{1,0:T(8,128)S(1)}, u32[]{:S(2)}, u32[]{:S(2)}) collective-permute-start(f32[8,128]{1,0:T(8,128)S(1)} %get-tuple-element.103), channel_id=1, source_target_pairs={{0,4},{1,5},{2,7},{3,6},{4,0},{5,1},{6,3},{7,2},{8,12},{9,13},{10,... | collective-permute-start | bytes 12296 | tf_op jit(solution)/shard_map/ppermute | solution.py:680
  35.3 0.5 %collective-permute-start.16 = (f32[8,128]{1,0:T(8,128)S(1)}, f32[8,128]{1,0:T(8,128)S(1)}, u32[]{:S(2)}, u32[]{:S(2)}) collective-permute-start(f32[8,128]{1,0:T(8,128)S(1)} %get-tuple-element.104), channel_id=1, source_target_pairs={{0,1},{1,0},{2,14},{3,15},{4,5},{5,4},{6,10},{7,11},{8,9},{9,8},{1... | collective-permute-start | bytes 12296 | tf_op jit(solution)/shard_map/ppermute | solution.py:680
  35.8 1.6 %collective-permute-start.15 = (f32[8,128]{1,0:T(8,128)S(1)}, f32[8,128]{1,0:T(8,128)S(1)}, u32[]{:S(2)}, u32[]{:S(2)}) collective-permute-start(f32[8,128]{1,0:T(8,128)S(1)} %get-tuple-element.104), channel_id=1, source_target_pairs={{0,8},{1,9},{2,6},{3,7},{4,12},{5,13},{6,2},{7,3},{8,0},{9,1},{10,... | collective-permute-start | bytes 12296 | tf_op jit(solution)/shard_map/ppermute | solution.py:680
  37.4 0.2 collective-permute-start.14
  37.6 0.0 collective-permute-done.13.rest_0_
  37.6 1.3 %collective-permute-done.16.rest_3_ = f32[8,128]{1,0:T(8,128)S(1)} collective-permute-done((f32[8,128]{1,0:T(8,128)S(1)}, f32[8,128]{1,0:T(8,128)S(1)}, u32[]{:S(2)}, u32[]{:S(2)}) %collective-permute-start.16) | collective-permute-done | bytes 4128 | tf_op jit(solution)/shard_map/ppermute | solution.py:680
  38.9 0.5 %collective-permute-done.15.rest_2_ = f32[8,128]{1,0:T(8,128)S(1)} collective-permute-done((f32[8,128]{1,0:T(8,128)S(1)}, f32[8,128]{1,0:T(8,128)S(1)}, u32[]{:S(2)}, u32[]{:S(2)}) %collective-permute-start.15) | collective-permute-done | bytes 4128 | tf_op jit(solution)/shard_map/ppermute | solution.py:680
  39.4 0.0 collective-permute-done.14.rest_1_
  39.4 0.4 shard_map.166.own
  39.8 0.1 collective-permute-start.17
  39.9 1.1 %collective-permute-done.17.other = f32[8,128]{1,0:T(8,128)S(1)} collective-permute-done((f32[8,128]{1,0:T(8,128)S(1)}, f32[8,128]{1,0:T(8,128)S(1)}, u32[]{:S(2)}, u32[]{:S(2)}) %collective-permute-start.17) | collective-permute-done | bytes 4128 | tf_op jit(solution)/shard_map/ppermute | solution.py:748
  41.0 0.7 %shard_map.167 = f32[4,32]{1,0:T(4,128)} custom-call(f32[8,128]{1,0:T(8,128)S(1)} %get-tuple-element.99.source, f32[8,128]{1,0:T(8,128)S(1)} %get-tuple-element.95.weights_two.weights, f32[8,128]{1,0:T(8,128)S(1)} %get-tuple-element.100.first_two, f32[8,128]{1,0:T(8,128)S(1)} %shard_map.166.own, f32[8,128]{1,0:T(8,128)S(1)} %collective-permute-done.17.other), custom_call_target="tpu_custom_call" | custom-call | tf_op jit(solution)/shard_map/pallas_call | solution.py:206
  (2 shorter events, 0.0 us)
Async XLA Ops:
  2.9 5.3 %collective-permute-start = (f32[16,640]{1,0:T(8,128)S(1)}, f32[16,640]{1,0:T(8,128)S(1)}, u32[]{:S(2)}, u32[]{:S(2)}) collective-permute-start(f32[16,640]{1,0:T(8,128)S(1)} %get-tuple-element.63), channel_id=1, source_target_pairs={{0,2},{1,3},{2,0},{3,1},{4,6},{5,7},{6,4},{7,5},{8,10},{9,11},{10,... | collective-permute-start | bytes 122888 | tf_op jit(solution)/shard_map/ppermute | solution.py:748
  3.5 4.8 %collective-permute-start.1 = (f32[16,768]{1,0:T(8,128)S(1)}, f32[16,768]{1,0:T(8,128)S(1)}, u32[]{:S(2)}, u32[]{:S(2)}) collective-permute-start(f32[16,768]{1,0:T(8,128)S(1)} %get-tuple-element.64), channel_id=1, source_target_pairs={{0,1},{1,0},{2,4},{3,5},{4,2},{5,3},{6,8},{7,9},{8,6},{9,7},{10,12... | collective-permute-start | bytes 147464 | tf_op jit(solution)/shard_map/ppermute | solution.py:748
  6.0 4.1 %collective-permute-start.2 = (f32[16,768]{1,0:T(8,128)S(1)}, f32[16,768]{1,0:T(8,128)S(1)}, u32[]{:S(2)}, u32[]{:S(2)}) collective-permute-start(f32[16,768]{1,0:T(8,128)S(1)} %get-tuple-element.65), channel_id=1, source_target_pairs={{0,1},{1,0},{2,3},{3,2},{4,5},{5,4},{6,7},{7,6},{8,9},{9,8},{10,11... | collective-permute-start | bytes 147464 | tf_op jit(solution)/shard_map/ppermute | solution.py:759
  11.6 5.3 %collective-permute-start.4 = (f32[16,128]{1,0:T(8,128)S(1)}, f32[16,128]{1,0:T(8,128)S(1)}, u32[]{:S(2)}, u32[]{:S(2)}) collective-permute-start(f32[16,128]{1,0:T(8,128)S(1)} %get-tuple-element.70), channel_id=1, source_target_pairs={{0,1},{1,0},{2,4},{3,5},{4,2},{5,3},{6,8},{7,9},{8,6},{9,7},{10,12... | collective-permute-start | bytes 24584 | tf_op jit(solution)/shard_map/ppermute | solution.py:748
  12.6 4.2 %collective-permute-start.5 = (f32[16,128]{1,0:T(8,128)S(1)}, f32[16,128]{1,0:T(8,128)S(1)}, u32[]{:S(2)}, u32[]{:S(2)}) collective-permute-start(f32[16,128]{1,0:T(8,128)S(1)} %get-tuple-element.71), channel_id=1, source_target_pairs={{0,1},{1,0},{2,3},{3,2},{4,5},{5,4},{6,7},{7,6},{8,9},{9,8},{10,11... | collective-permute-start | bytes 24584 | tf_op jit(solution)/shard_map/ppermute | solution.py:759
  13.7 3.2 %collective-permute-start.3 = (f32[16,256]{1,0:T(8,128)S(1)}, f32[16,256]{1,0:T(8,128)S(1)}, u32[]{:S(2)}, u32[]{:S(2)}) collective-permute-start(f32[16,256]{1,0:T(8,128)S(1)} %get-tuple-element.69), channel_id=1, source_target_pairs={{0,2},{1,3},{2,0},{3,1},{4,6},{5,7},{6,4},{7,5},{8,10},{9,11},{10,... | collective-permute-start | bytes 49160 | tf_op jit(solution)/shard_map/ppermute | solution.py:748
  18.4 1.4 %collective-permute-start.6 = (f32[120,256]{1,0:T(8,128)S(1)}, f32[120,256]{1,0:T(8,128)S(1)}, u32[]{:S(2)}, u32[]{:S(2)}) collective-permute-start(f32[120,256]{1,0:T(8,128)S(1)} %shard_map.161.own), channel_id=1, source_target_pairs={{0,2},{1,3},{2,0},{3,1},{4,6},{5,7},{6,4},{7,5},{8,10},{9,11},{10,... | collective-permute-start | bytes 368648 | tf_op jit(solution)/shard_map/ppermute | solution.py:748
  20.1 3.6 %collective-permute-start.7 = (f32[8,128]{1,0:T(8,128)S(1)}, f32[8,128]{1,0:T(8,128)S(1)}, u32[]{:S(2)}, u32[]{:S(2)}) collective-permute-start(f32[8,128]{1,0:T(8,128)S(1)} %get-tuple-element.78), channel_id=1, source_target_pairs={{0,1},{1,0},{2,6},{3,7},{4,5},{5,4},{6,2},{7,3},{8,9},{9,8},{10,14... | collective-permute-start | bytes 12296 | tf_op jit(solution)/shard_map/ppermute | solution.py:680
  21.0 3.6 %collective-permute-start.8 = (f32[8,128]{1,0:T(8,128)S(1)}, f32[8,128]{1,0:T(8,128)S(1)}, u32[]{:S(2)}, u32[]{:S(2)}) collective-permute-start(f32[8,128]{1,0:T(8,128)S(1)} %get-tuple-element.79), channel_id=1, source_target_pairs={{0,4},{1,5},{2,3},{3,2},{4,0},{5,1},{6,10},{7,11},{8,12},{9,13},{1... | collective-permute-start | bytes 12296 | tf_op jit(solution)/shard_map/ppermute | solution.py:680
  24.6 1.2 %collective-permute-start.9 = (f32[16,128]{1,0:T(8,128)S(1)}, f32[16,128]{1,0:T(8,128)S(1)}, u32[]{:S(2)}, u32[]{:S(2)}) collective-permute-start(f32[16,128]{1,0:T(8,128)S(1)} %pad_maximum_fusion.mine), channel_id=1, source_target_pairs={{0,2},{1,3},{2,0},{3,1},{4,6},{5,7},{6,4},{7,5},{8,10},{9,11},{10,... | collective-permute-start | bytes 24584 | tf_op jit(solution)/shard_map/ppermute | solution.py:748
  26.5 4.8 %collective-permute-start.10 = (f32[8,128]{1,0:T(8,128)S(1)}, f32[8,128]{1,0:T(8,128)S(1)}, u32[]{:S(2)}, u32[]{:S(2)}) collective-permute-start(f32[8,128]{1,0:T(8,128)S(1)} %get-tuple-element.80), channel_id=1, source_target_pairs={{0,1},{1,0},{2,6},{3,7},{4,5},{5,4},{6,2},{7,3},{8,9},{9,8},{10,14... | collective-permute-start | bytes 12296 | tf_op jit(solution)/shard_map/ppermute | solution.py:680
  27.6 3.6 %collective-permute-start.11 = (f32[8,128]{1,0:T(8,128)S(1)}, f32[8,128]{1,0:T(8,128)S(1)}, u32[]{:S(2)}, u32[]{:S(2)}) collective-permute-start(f32[8,128]{1,0:T(8,128)S(1)} %get-tuple-element.81), channel_id=1, source_target_pairs={{0,4},{1,5},{2,3},{3,2},{4,0},{5,1},{6,10},{7,11},{8,12},{9,13},{1... | collective-permute-start | bytes 12296 | tf_op jit(solution)/shard_map/ppermute | solution.py:680
  31.3 1.2 %collective-permute-start.12 = (f32[16,128]{1,0:T(8,128)S(1)}, f32[16,128]{1,0:T(8,128)S(1)}, u32[]{:S(2)}, u32[]{:S(2)}) collective-permute-start(f32[16,128]{1,0:T(8,128)S(1)} %pad_maximum_fusion.1.rest_0_), channel_id=1, source_target_pairs={{0,2},{1,3},{2,0},{3,1},{4,6},{5,7},{6,4},{7,5},{8,10},{9,11},{10,... | collective-permute-start | bytes 24584 | tf_op jit(solution)/shard_map/ppermute | solution.py:748
  33.3 4.3 %collective-permute-start.13 = (f32[8,128]{1,0:T(8,128)S(1)}, f32[8,128]{1,0:T(8,128)S(1)}, u32[]{:S(2)}, u32[]{:S(2)}) collective-permute-start(f32[8,128]{1,0:T(8,128)S(1)} %get-tuple-element.103), channel_id=1, source_target_pairs={{0,4},{1,5},{2,7},{3,6},{4,0},{5,1},{6,3},{7,2},{8,12},{9,13},{10,... | collective-permute-start | bytes 12296 | tf_op jit(solution)/shard_map/ppermute | solution.py:680
  35.3 3.6 %collective-permute-start.16 = (f32[8,128]{1,0:T(8,128)S(1)}, f32[8,128]{1,0:T(8,128)S(1)}, u32[]{:S(2)}, u32[]{:S(2)}) collective-permute-start(f32[8,128]{1,0:T(8,128)S(1)} %get-tuple-element.104), channel_id=1, source_target_pairs={{0,1},{1,0},{2,14},{3,15},{4,5},{5,4},{6,10},{7,11},{8,9},{9,8},{1... | collective-permute-start | bytes 12296 | tf_op jit(solution)/shard_map/ppermute | solution.py:680
  35.8 3.6 %collective-permute-start.15 = (f32[8,128]{1,0:T(8,128)S(1)}, f32[8,128]{1,0:T(8,128)S(1)}, u32[]{:S(2)}, u32[]{:S(2)}) collective-permute-start(f32[8,128]{1,0:T(8,128)S(1)} %get-tuple-element.104), channel_id=1, source_target_pairs={{0,8},{1,9},{2,6},{3,7},{4,12},{5,13},{6,2},{7,3},{8,0},{9,1},{10,... | collective-permute-start | bytes 12296 | tf_op jit(solution)/shard_map/ppermute | solution.py:680
  37.4 2.0 %collective-permute-start.14 = (f32[8,128]{1,0:T(8,128)S(1)}, f32[8,128]{1,0:T(8,128)S(1)}, u32[]{:S(2)}, u32[]{:S(2)}) collective-permute-start(f32[8,128]{1,0:T(8,128)S(1)} %get-tuple-element.104), channel_id=1, source_target_pairs={{0,2},{1,3},{2,0},{3,1},{4,6},{5,7},{6,4},{7,5},{8,16},{9,17},{10,... | collective-permute-start | bytes 12296 | tf_op jit(solution)/shard_map/ppermute | solution.py:680
  39.8 1.2 %collective-permute-start.17 = (f32[8,128]{1,0:T(8,128)S(1)}, f32[8,128]{1,0:T(8,128)S(1)}, u32[]{:S(2)}, u32[]{:S(2)}) collective-permute-start(f32[8,128]{1,0:T(8,128)S(1)} %shard_map.166.own), channel_id=1, source_target_pairs={{0,2},{1,3},{2,0},{3,1},{4,6},{5,7},{6,4},{7,5},{8,10},{9,11},{10,... | collective-permute-start | bytes 12296 | tf_op jit(solution)/shard_map/ppermute | solution.py:748
